TPU v7x, 32 devices: a whole 2x2x4 slice. The times are simulated.
32 devices in a mesh: rows: 16 (over z, y, core), cols: 2 (over x).
Axes of the slice: x: 2, y: 2, z: 4, core: 2. Of those that a mesh axis runs over, the one named last changes fastest.
Arguments:
- users: bfloat16 [32768, 256], P('rows'), may hold values from -0.3984375 to 0.3984375
- items: bfloat16 [2, 256, 256], P('cols'), may hold values from -6 to 6
- ratings: bfloat16 [16, 2, 64, 128, 128], P('rows', 'cols'), may hold values from -6 to 6
- tile_users: int32 [16, 2, 64], P('rows', 'cols'), may hold values from 0 to 15
- tile_items: int32 [16, 2, 64], P('rows', 'cols'), may hold values from 0 to 1
- tile_count: int32 [16, 2], P('rows', 'cols'), may hold values from 16 to 64, as said below
- send_list: int32 [16, 2, 2, 1], P('rows', 'cols'), may hold values from 0 to 1
- block_target: int32 [16, 2, 2], P('rows', 'cols'), may hold values from 0 to 1
- similarity: bfloat16 [16, 2, 2, 128, 128], P('rows', 'cols'), may hold values from -6 to 6
Outputs:
- new_items: float32 [2, 256, 256], P('cols', 'rows')
Inputs may be any that keep to these rules, and one draw needn't show every extreme that they name: `tile_count`: every draw has some device with all 64 slots live; the device differs from draw to draw.
All inputs are finite; a program needn't handle non-finite values.
Results may differ from a plain program's by a relative error of at most 0.00065.
Values may be sent and summed in bfloat16 or wider, within the bound.
No kernel may reach another device: no remote copies, remote signals or barrier semaphores. Data moves between devices by JAX's collectives and lax.ppermute only.
A program may use at most 64 MiB of HBM per device.

v0:
```python
import jax
import jax.numpy as jnp
from jax import lax
from jax.sharding import PartitionSpec as P


def shards(
    users, items, ratings, tile_users, tile_items, tile_count, send_list, block_target, similarity
):
    rank = items.shape[2]
    icount = items.shape[1]
    tile = ratings.shape[-1]
    panels = items[0].reshape(-1, tile, rank)
    ntiles = panels.shape[0]
    user_tiles = users.reshape(-1, tile, rank)
    tiles_here = ratings.shape[2]
    width = min(16, tiles_here)
    nblocks = tiles_here // width
    live_count = tile_count[0, 0]
    tile_ids = jnp.arange(ntiles, dtype=jnp.int32)
    outgoing = panels[send_list[0, 0]]
    incoming = lax.all_to_all(outgoing, "cols", split_axis=0, concat_axis=0, tiled=True)
    blocks = similarity.shape[2]
    incoming = incoming.reshape(blocks, tile, rank)
    contrib = jnp.einsum(
        "kab,kbr->kar", similarity[0, 0], incoming, preferred_element_type=jnp.float32
    )
    targets = (tile_ids[:, None] == block_target[0, 0][None, :]).astype(jnp.float32)
    start_grad = jnp.einsum("kt,tbr->kbr", targets, contrib, precision=lax.Precision.HIGHEST)

    def tile_block(grad, pieces):
        user_idx, item_idx, rating, places = pieces
        left = user_tiles[user_idx]
        right = panels[item_idx]
        pred = jnp.einsum("tar,tbr->tab", left, right, preferred_element_type=jnp.float32)
        live = (places < live_count).astype(jnp.float32)
        err = ((pred - rating.astype(jnp.float32)) * live[:, None, None]).astype(jnp.bfloat16)
        part = jnp.einsum("tab,tar->tbr", err, left, preferred_element_type=jnp.float32)
        onehot = (tile_ids[:, None] == item_idx[None, :]).astype(jnp.float32)
        grad = grad + jnp.einsum("kt,tbr->kbr", onehot, part, precision=lax.Precision.HIGHEST)
        return (grad, None)

    inputs = (
        tile_users[0, 0].reshape(nblocks, width),
        tile_items[0, 0].reshape(nblocks, width),
        ratings[0, 0].reshape(nblocks, width, tile, tile),
        jnp.arange(tiles_here, dtype=jnp.int32).reshape(nblocks, width),
    )
    grad, unused = lax.scan(tile_block, start_grad, inputs)
    flat = grad.reshape(icount, rank)
    item_dev = icount // lax.axis_size("rows")
    total_entries = lax.axis_size("cols") * icount * rank
    owned = lax.psum_scatter(flat, "rows", scatter_dimension=0, tiled=True)
    squares = lax.psum(jnp.sum(owned * owned), ("rows", "cols"))
    meansq = squares / total_entries
    mine = lax.dynamic_slice_in_dim(
        items[0], lax.axis_index("rows") * item_dev, item_dev, 0
    ).astype(jnp.float32)
    updated = mine - 0.5 * owned / jnp.sqrt(meansq + 1e-06)
    return updated[None]


def solution(mesh):
    in_specs = (
        P("rows", None),
        P("cols", None, None),
        P("rows", "cols", None, None, None),
        P("rows", "cols", None),
        P("rows", "cols", None),
        P("rows", "cols"),
        P("rows", "cols", None, None),
        P("rows", "cols", None),
        P("rows", "cols", None, None, None),
    )
    out_specs = P("cols", "rows", None)
    return jax.shard_map(shards, mesh=mesh, in_specs=in_specs, out_specs=out_specs, check_vma=False)
```

profile of v0, /device:TPU:0, one launch (start us, length us, event | category | flops | bytes accessed | tf_op | source)
XLA Modules:
  0.0 168.8 jit_solution(12329898234035601331)
XLA Ops:
  6.5 0.0 copy-start
  6.5 0.7 fusion.33
  7.2 2.1 %gather_fusion.2 = bf16[2,128,256]{2,1,0:T(8,128)(2,1)} fusion(bf16[2,128,256]{2,1,0:T(8,128)(2,1)} %bitcast.74, s32[1024]{0:T(1024)S(1)} %pad_clamp_fusion.2), kind=kCustom, calls=%fused_computation.2 | custom fusion | bytes 262152 | tf_op jit(solution)/shard_map/gather | solution.py:21
  9.3 4.2 %all-to-all-start = ((bf16[2,1,128,256]{3,2,1,0:T(8,128)(2,1)}), bf16[2,1,128,256]{3,2,1,0:T(8,128)(2,1)S(1)}, u32[]{:S(2)}, u32[]{:S(2)}) async-start(bf16[2,1,128,256]{3,2,1,0:T(8,128)(2,1)} %bitcast.6), calls=%async_computation | async-start | bytes 262144 | tf_op jit(solution)/shard_map/all_to_all | solution.py:22
  13.5 0.0 reduce-scatter.2.cloned.1.call-start
  13.5 0.5 broadcast.98
  14.0 1.2 reduce.6
  15.3 0.1 reshape_squeeze.13
  15.4 1.2 reduce.7
  16.6 0.1 reshape_squeeze.14
  16.7 1.4 all-to-all-done
  18.1 0.0 copy-done
  18.1 0.2 fusion.26
  18.3 0.1 copy.13
  18.5 2.0 %fusion.24 = f32[2,128,256]{2,0,1:T(2,128)} fusion(f32[2,256,128]{1,0,2:T(2,128)S(1)} %copy.13, s32[2]{0:T(128)} %bitcast.80), kind=kOutput, calls=%fused_computation.33 | convolution fusion | flops 1572868 | bytes 524296 | tf_op jit(solution)/shard_map/kt,tbr->kbr/dot_general | solution.py:29
  20.5 39.8 %while.11 = (s32[]{:T(128)}, f32[2,128,256]{2,0,1:T(2,128)}, s32[4,16]{1,0:T(4,128)S(1)}, s32[4,16]{1,0:T(4,128)S(1)}, bf16[16,128,256]{2,1,0:T(8,128)(2,1)}, /*...) while((s32[]{:T(128)}, f32[2,128,256]{2,0,1:T(2,128)}, ...), condition=%wide.region_1.2_spmd.clone, body=%wide.region_0.1_spmd.clone.sunk | while | flops 282134688 | bytes 13117393 | solution.py:49
  20.5 0.0 copy-start.1
  20.5 1.9 %gather_fusion = bf16[16,128,256]{2,1,0:T(8,128)(2,1)S(1)} fusion(bf16[16,128,256]{2,1,0:T(8,128)(2,1)} %get-tuple-element.181, s32[1024]{0:T(1024)S(1)} %pad_clamp_fusion.5), kind=kCustom, calls=%fused_computation.clone.clone.1 | custom fusion | bytes 2097216 | tf_op jit(solution)/shard_map/while/body/eval_jaxpr/gather | solution.py:33
  22.4 0.0 copy-done.1
  22.4 1.6 gather_fusion.1
  24.0 0.7 fusion.54
  24.7 2.1 %fusion.55 = f32[16,128,256]{2,1,0:T(8,128)S(1)} fusion(bf16[16,128,256]{2,1,0:T(8,128)(2,1)S(1)} %gather_fusion, bf16[16,128,256]{2,1,0:T(8,128)(2,1)} %gather_fusion.1, f32[16]{0:T(128)S(1)} %fusion.54, bf16[4,16,128,128]{3,2,1,0:T(8,128)(2,1)} %get-tuple-element.183, s32[]{:T(128)} %get-tuple-element.167), kind=kOutput, calls=%fused_computation.9.clone.1 | convolution fusion | flops 269484032 | bytes 5768192 | tf_op jit(solution)/shard_map/while/body/eval_jaxpr/tab,tar->tbr/dot_general | solution.py:38
  26.8 3.7 %fusion.57 = f32[2,128,256]{2,0,1:T(2,128)} fusion(f32[2,128,256]{2,0,1:T(2,128)} %get-tuple-element.168, f32[16,128,256]{2,1,0:T(8,128)S(1)} %fusion.55, s32[16]{0:T(128)S(1)} %fusion.56), kind=kOutput, calls=%fused_computation.10.clone.1 | convolution fusion | flops 12648480 | bytes 2621504 | tf_op jit(solution)/shard_map/while/body/eval_jaxpr/kt,tbr->kbr/dot_general | solution.py:40
  30.4 0.0 copy-start.1
  30.4 1.9 %gather_fusion = bf16[16,128,256]{2,1,0:T(8,128)(2,1)S(1)} fusion(bf16[16,128,256]{2,1,0:T(8,128)(2,1)} %get-tuple-element.181, s32[1024]{0:T(1024)S(1)} %pad_clamp_fusion.5), kind=kCustom, calls=%fused_computation.clone.clone.1 | custom fusion | bytes 2097216 | tf_op jit(solution)/shard_map/while/body/eval_jaxpr/gather | solution.py:33
  32.3 0.0 copy-done.1
  32.4 1.6 gather_fusion.1
  34.0 0.7 fusion.54
  34.6 2.1 %fusion.55 = f32[16,128,256]{2,1,0:T(8,128)S(1)} fusion(bf16[16,128,256]{2,1,0:T(8,128)(2,1)S(1)} %gather_fusion, bf16[16,128,256]{2,1,0:T(8,128)(2,1)} %gather_fusion.1, f32[16]{0:T(128)S(1)} %fusion.54, bf16[4,16,128,128]{3,2,1,0:T(8,128)(2,1)} %get-tuple-element.183, s32[]{:T(128)} %get-tuple-element.167), kind=kOutput, calls=%fused_computation.9.clone.1 | convolution fusion | flops 269484032 | bytes 5768192 | tf_op jit(solution)/shard_map/while/body/eval_jaxpr/tab,tar->tbr/dot_general | solution.py:38
  36.7 3.7 %fusion.57 = f32[2,128,256]{2,0,1:T(2,128)} fusion(f32[2,128,256]{2,0,1:T(2,128)} %get-tuple-element.168, f32[16,128,256]{2,1,0:T(8,128)S(1)} %fusion.55, s32[16]{0:T(128)S(1)} %fusion.56), kind=kOutput, calls=%fused_computation.10.clone.1 | convolution fusion | flops 12648480 | bytes 2621504 | tf_op jit(solution)/shard_map/while/body/eval_jaxpr/kt,tbr->kbr/dot_general | solution.py:40
  40.4 1.9 %gather_fusion = bf16[16,128,256]{2,1,0:T(8,128)(2,1)S(1)} fusion(bf16[16,128,256]{2,1,0:T(8,128)(2,1)} %get-tuple-element.181, s32[1024]{0:T(1024)S(1)} %pad_clamp_fusion.5), kind=kCustom, calls=%fused_computation.clone.clone.1 | custom fusion | bytes 2097216 | tf_op jit(solution)/shard_map/while/body/eval_jaxpr/gather | solution.py:33
  42.3 0.0 copy-done.1
  42.3 1.6 gather_fusion.1
  43.9 0.7 fusion.54
  44.6 2.1 %fusion.55 = f32[16,128,256]{2,1,0:T(8,128)S(1)} fusion(bf16[16,128,256]{2,1,0:T(8,128)(2,1)S(1)} %gather_fusion, bf16[16,128,256]{2,1,0:T(8,128)(2,1)} %gather_fusion.1, f32[16]{0:T(128)S(1)} %fusion.54, bf16[4,16,128,128]{3,2,1,0:T(8,128)(2,1)} %get-tuple-element.183, s32[]{:T(128)} %get-tuple-element.167), kind=kOutput, calls=%fused_computation.9.clone.1 | convolution fusion | flops 269484032 | bytes 5768192 | tf_op jit(solution)/shard_map/while/body/eval_jaxpr/tab,tar->tbr/dot_general | solution.py:38
  46.7 3.7 %fusion.57 = f32[2,128,256]{2,0,1:T(2,128)} fusion(f32[2,128,256]{2,0,1:T(2,128)} %get-tuple-element.168, f32[16,128,256]{2,1,0:T(8,128)S(1)} %fusion.55, s32[16]{0:T(128)S(1)} %fusion.56), kind=kOutput, calls=%fused_computation.10.clone.1 | convolution fusion | flops 12648480 | bytes 2621504 | tf_op jit(solution)/shard_map/while/body/eval_jaxpr/kt,tbr->kbr/dot_general | solution.py:40
  50.4 1.9 %gather_fusion = bf16[16,128,256]{2,1,0:T(8,128)(2,1)S(1)} fusion(bf16[16,128,256]{2,1,0:T(8,128)(2,1)} %get-tuple-element.181, s32[1024]{0:T(1024)S(1)} %pad_clamp_fusion.5), kind=kCustom, calls=%fused_computation.clone.clone.1 | custom fusion | bytes 2097216 | tf_op jit(solution)/shard_map/while/body/eval_jaxpr/gather | solution.py:33
  52.3 0.0 copy-done.1
  52.3 1.6 gather_fusion.1
  53.9 0.7 fusion.54
  54.5 2.1 %fusion.55 = f32[16,128,256]{2,1,0:T(8,128)S(1)} fusion(bf16[16,128,256]{2,1,0:T(8,128)(2,1)S(1)} %gather_fusion, bf16[16,128,256]{2,1,0:T(8,128)(2,1)} %gather_fusion.1, f32[16]{0:T(128)S(1)} %fusion.54, bf16[4,16,128,128]{3,2,1,0:T(8,128)(2,1)} %get-tuple-element.183, s32[]{:T(128)} %get-tuple-element.167), kind=kOutput, calls=%fused_computation.9.clone.1 | convolution fusion | flops 269484032 | bytes 5768192 | tf_op jit(solution)/shard_map/while/body/eval_jaxpr/tab,tar->tbr/dot_general | solution.py:38
  56.6 3.7 %fusion.57 = f32[2,128,256]{2,0,1:T(2,128)} fusion(f32[2,128,256]{2,0,1:T(2,128)} %get-tuple-element.168, f32[16,128,256]{2,1,0:T(8,128)S(1)} %fusion.55, s32[16]{0:T(128)S(1)} %fusion.56), kind=kOutput, calls=%fused_computation.10.clone.1 | convolution fusion | flops 12648480 | bytes 2621504 | tf_op jit(solution)/shard_map/while/body/eval_jaxpr/kt,tbr->kbr/dot_general | solution.py:40
  60.3 1.7 copy.11
  62.0 0.0 reduce-scatter.2.cloned.1.call-update
  62.0 56.4 %reduce-scatter.2.cloned.1.call-done = f32[16,256]{1,0:T(8,128)} async-done(((f32[256,256]{1,0:T(8,128)}), f32[16,256]{1,0:T(8,128)}) %reduce-scatter.2.cloned.1.call-update) | async-done | bytes 16400 | tf_op jit(solution)/shard_map/reduce_scatter | solution.py:53
  118.4 1.3 multiply_reduce_fusion
  119.8 40.2 %psum.7 = f32[]{:T(128)} all-reduce(f32[]{:T(128)} %multiply_reduce_fusion), channel_id=1, replica_groups=mesh['rows'=16,'cols'=2] {'rows','cols'}, use_global_device_ids=true, to_apply=%region_4.5 | all-reduce | flops 1 | bytes 8 | tf_op jit(solution)/shard_map/psum | solution.py:54
  160.7 1.3 fusion.29
  (20 shorter events, 0.1 us)
Async XLA Ops:
  6.5 11.6 %copy-start = (bf16[1,1,2,128,128]{4,3,2,1,0:T(8,128)(2,1)S(1)}, bf16[1,1,2,128,128]{4,3,2,1,0:T(8,128)(2,1)}, u32[]{:S(2)}) copy-start(bf16[1,1,2,128,128]{4,3,2,1,0:T(8,128)(2,1)} %param.19) | copy-start | bytes 196612
  9.3 8.8 %all-to-all-start = ((bf16[2,1,128,256]{3,2,1,0:T(8,128)(2,1)}), bf16[2,1,128,256]{3,2,1,0:T(8,128)(2,1)S(1)}, u32[]{:S(2)}, u32[]{:S(2)}) async-start(bf16[2,1,128,256]{3,2,1,0:T(8,128)(2,1)} %bitcast.6), calls=%async_computation | async-start | bytes 262144 | tf_op jit(solution)/shard_map/all_to_all | solution.py:22
  13.5 104.9 %reduce-scatter.2.cloned.1.call-start = ((), (), s32[]{:S(2)}) async-start(), calls=%async_computation.2 | async-start | bytes 278528 | tf_op jit(solution)/shard_map/reduce_scatter | solution.py:53
  20.5 1.9 %copy-start.1 = (bf16[2,128,256]{2,1,0:T(8,128)(2,1)S(1)}, bf16[2,128,256]{2,1,0:T(8,128)(2,1)}, u32[]{:S(2)}) copy-start(bf16[2,128,256]{2,1,0:T(8,128)(2,1)} %get-tuple-element.182) | copy-start | bytes 393220 | tf_op jit(solution)/shard_map/while
  30.4 1.9 %copy-start.1 = (bf16[2,128,256]{2,1,0:T(8,128)(2,1)S(1)}, bf16[2,128,256]{2,1,0:T(8,128)(2,1)}, u32[]{:S(2)}) copy-start(bf16[2,128,256]{2,1,0:T(8,128)(2,1)} %get-tuple-element.182) | copy-start | bytes 393220 | tf_op jit(solution)/shard_map/while
  40.4 1.9 %copy-start.1 = (bf16[2,128,256]{2,1,0:T(8,128)(2,1)S(1)}, bf16[2,128,256]{2,1,0:T(8,128)(2,1)}, u32[]{:S(2)}) copy-start(bf16[2,128,256]{2,1,0:T(8,128)(2,1)} %get-tuple-element.182) | copy-start | bytes 393220 | tf_op jit(solution)/shard_map/while
  50.3 1.9 %copy-start.1 = (bf16[2,128,256]{2,1,0:T(8,128)(2,1)S(1)}, bf16[2,128,256]{2,1,0:T(8,128)(2,1)}, u32[]{:S(2)}) copy-start(bf16[2,128,256]{2,1,0:T(8,128)(2,1)} %get-tuple-element.182) | copy-start | bytes 393220 | tf_op jit(solution)/shard_map/while
Sparse Core Ops, SparseCore 0:
  62.1 56.2 reduce-scatter.1
where the time goes:
time: 170 us; the launch traced here: 169 us
  waiting for transfers between devices  57.9 us (34%)
  blocking collectives  40.2 us (24%)
  matrix products  25.2 us (15%)
  local copies, waits for them, and re-layouts  18.5 us (11%)
  between operations  14.1 us (8%)
  other arithmetic  8.52 us (5%)
  starting transfers between devices  4.21 us (2%)
    reduce_scatter x1, waiting for transfers between devices, shards(): owned = lax.psum_scatter(flat, 'rows', scatter_dimension=0, tiled=True)  56.4 us
    psum x1, blocking collectives, shards(): squares = lax.psum(jnp.sum(owned * owned), ('rows', 'cols'))  40.2 us
    dot_general x4, matrix products, tile_block(): jnp.einsum('kt,tbr->kbr', onehot, part, precision=lax.Precision.HIGHEST)  14.6 us
    dot_general x4, matrix products, tile_block(): jnp.einsum('tab,tar->tbr', err, left, preferred_element_type=jnp.float32)  8.35 us
    gather x4, local copies, waits for them, and re-layouts, tile_block(): left = user_tiles[user_idx]  7.5 us
    gather x4, local copies, waits for them, and re-layouts, tile_block(): right = panels[item_idx]  6.41 us
    all_to_all x1, starting transfers between devices, shards(): lax.all_to_all(outgoing, 'cols', split_axis=0, concat_axis=0, tiled=True)  4.21 us
  transfers between devices with their start and end apart: 2, of which 2 were waited for; matrix products, arithmetic and copies ran while one was open for 2% of the time, Pallas kernels for 0%

commit v1 on v0

v1 whole, which is shorter than its diff:
```python
import functools

import jax
import jax.numpy as jnp
from jax import lax
from jax.experimental import pallas as pl
from jax.experimental.pallas import tpu as pltpu
from jax.sharding import PartitionSpec as P

F32 = jnp.float32
BF16 = jnp.bfloat16
CHUNKS = 8


def dot(a, b, dims):
    return lax.dot_general(a, b, (dims, ((), ())), preferred_element_type=F32)


def rating_kernel(
    user_idx, item_idx, count, users_hbm, items_hbm, ratings_hbm, grad_ref,
    users, items, ratings, users_t, pred, err, sem_u, sem_i, sem_r,
):
    n_tiles, tile = ratings.shape[0], ratings.shape[1]
    n_user = users.shape[0] // tile
    n_item = items.shape[0] // tile
    width = n_tiles // CHUNKS
    live = count[0]
    copy_u = pltpu.make_async_copy(users_hbm, users, sem_u)
    copy_i = pltpu.make_async_copy(items_hbm, items, sem_i)
    copy_i.start()
    copy_u.start()

    def chunk_copy(c):
        span = pl.ds(c * width, width)
        return pltpu.make_async_copy(ratings_hbm.at[span], ratings.at[span], sem_r.at[c])

    for c in range(CHUNKS):
        @pl.when(c * width < live)
        def _():
            chunk_copy(c).start()

    err[...] = jnp.zeros_like(err)
    copy_i.wait()
    copy_u.wait()
    for u in range(n_user):
        rows = pl.ds(u * tile, tile)
        block = users[rows, :]
        users_t[:, rows] = block.T
        whole = dot(block, items[...], ((1,), (1,)))
        for j in range(n_item):
            pred[u * n_item + j] = whole[:, j * tile:(j + 1) * tile]

    def step(t, carry):
        place = user_idx[t] * n_item + item_idx[t]
        diff = pred[place] - ratings[t].astype(F32)
        err[place] += diff.astype(BF16).astype(F32)
        return carry

    for c in range(CHUNKS):
        @pl.when(c * width < live)
        def _():
            chunk_copy(c).wait()
            lax.fori_loop(c * width, jnp.minimum(live, (c + 1) * width), step, 0)

    for j in range(n_item):
        total = jnp.zeros((users.shape[1], tile), F32)
        for u in range(n_user):
            left = users_t[:, u * tile:(u + 1) * tile]
            whole = err[u * n_item + j]
            high = whole.astype(BF16)
            low = (whole - high.astype(F32)).astype(BF16)
            total += dot(left, high, ((1,), (0,))) + dot(left, low, ((1,), (0,)))
        grad_ref[j * tile:(j + 1) * tile, :] = total.T


def rating_part(user_idx, item_idx, count, users, items, ratings):
    n_tiles, tile, unused = ratings.shape
    n_pairs = (users.shape[0] // tile) * (items.shape[0] // tile)
    smem = pl.BlockSpec(memory_space=pltpu.SMEM)
    hbm = pl.BlockSpec(memory_space=pl.ANY)
    return pl.pallas_call(
        rating_kernel,
        name="rating_part",
        out_shape=jax.ShapeDtypeStruct(items.shape, F32),
        in_specs=[smem] * 3 + [hbm] * 3,
        out_specs=pl.BlockSpec(memory_space=pltpu.VMEM),
        scratch_shapes=[
            pltpu.VMEM(users.shape, BF16),
            pltpu.VMEM(items.shape, BF16),
            pltpu.VMEM(ratings.shape, BF16),
            pltpu.VMEM(users.shape[::-1], BF16),
            pltpu.VMEM((n_pairs, tile, tile), F32),
            pltpu.VMEM((n_pairs, tile, tile), F32),
            pltpu.SemaphoreType.DMA,
            pltpu.SemaphoreType.DMA,
            pltpu.SemaphoreType.DMA((CHUNKS,)),
        ],
        compiler_params=pltpu.CompilerParams(vmem_limit_bytes=48 * 1024 * 1024),
        cost_estimate=pl.CostEstimate(flops=4 * 10**8, bytes_accessed=4 * 10**6, transcendentals=0),
    )(user_idx, item_idx, count, users, items, ratings)


def graph_kernel(target, grad, similarity, panels, *outs):
    blocks, tile, unused = similarity.shape
    total = outs[-1]
    total[...] = grad[...]
    for k in range(blocks):
        rows = pl.ds(pl.multiple_of(target[k] * tile, tile), tile)
        total[rows, :] += dot(similarity[k], panels[k], ((1,), (0,)))
    me = lax.axis_index("rows")
    if len(outs) == 2:
        outs[0][...] = total[...]
        return
    keep, give = outs[:2]
    half, own = keep.shape[:2]
    for q in range(half):
        for core, out in ((0, keep), (1, give)):
            place = pl.multiple_of((me ^ (2 * q + core)) * own, own)
            out[q] = total[pl.ds(place, own), :]


def graph_part(target, grad, similarity, panels, out_shape):
    smem = pl.BlockSpec(memory_space=pltpu.SMEM)
    vmem = pl.BlockSpec(memory_space=pltpu.VMEM)
    return pl.pallas_call(
        graph_kernel,
        name="graph_part",
        out_shape=out_shape,
        in_specs=[smem] + [vmem] * 3,
        out_specs=jax.tree.map(lambda unused: vmem, out_shape),
        scratch_shapes=[pltpu.VMEM(grad.shape, F32)],
        compiler_params=pltpu.CompilerParams(vmem_limit_bytes=32 * 1024 * 1024),
    )(target, grad, similarity, panels)


def split_places(half, bit):
    return [q for q in range(half) if q & bit and not q & (bit - 1)]


def pack(total, payload, bit):
    half = total.shape[0]
    for q in range(half):
        payload[q] = total[q].astype(BF16)
    for n, q in enumerate(split_places(half, bit)):
        whole = total[q]
        payload[half + n] = (whole - whole.astype(BF16).astype(F32)).astype(BF16)


def unpack(received, q, bit, half):
    other = q ^ bit
    value = received[other].astype(F32)
    places = split_places(half, bit)
    if other in places:
        value = value + received[half + places.index(other)].astype(F32)
    return value


def first_kernel(keep, received, total, payload):
    total[...] = keep[...] + received[...]
    pack(total, payload, 1)


def next_kernel(bit, before, received, total, payload):
    half = total.shape[0]
    for q in range(half):
        total[q] = before[q] + unpack(received, q, bit, half)
    pack(total, payload, 2 * bit)


def last_kernel(bit, before, received, own, squares):
    half, rows, rank = before.shape
    part = jnp.zeros((8, 128), F32)
    for q in range(half):
        value = before[q] + unpack(received, q, bit, half)
        if q == 0:
            own[...] = value
        square = value * value
        for a in range(0, rows, 8):
            for b in range(0, rank, 128):
                part = part + square[a:a + 8, b:b + 128]
    squares[...] = part


def local_call(kernel, name, args, out_shape):
    vmem = pl.BlockSpec(memory_space=pltpu.VMEM)
    return pl.pallas_call(
        kernel, name=name, out_shape=out_shape, in_specs=[vmem] * len(args),
        out_specs=jax.tree.map(lambda unused: vmem, out_shape),
    )(*args)


def update_kernel(entries, items, own, squares, more, new):
    me = lax.axis_index("rows")
    rows = own.shape[0]
    meansq = jnp.sum(squares[...] + more[...], keepdims=True) / entries
    mine = items[pl.ds(pl.multiple_of(me * rows, rows), rows), :].astype(F32)
    new[...] = mine - 0.5 * own[...] / jnp.sqrt(meansq + 1e-06)


def swap(value, axis, bit):
    size = lax.axis_size(axis)
    return lax.ppermute(value, axis, [(i, i ^ bit) for i in range(size)])


def shards(
    users, items, ratings, tile_users, tile_items, tile_count, send_list, block_target, similarity
):
    n_rows, n_cols = lax.axis_size("rows"), lax.axis_size("cols")
    icount, rank = items.shape[1:]
    tile = ratings.shape[-1]
    blocks = similarity.shape[2]
    panels = items[0].reshape(-1, tile, rank)
    incoming = lax.all_to_all(panels[send_list[0, 0]], "cols", 0, 0, tiled=True)
    incoming = incoming.reshape(blocks, tile, rank)
    grad = rating_part(
        tile_users[0, 0], tile_items[0, 0], tile_count[0], users, items[0], ratings[0, 0]
    )
    own_rows = icount // n_rows
    entries = n_cols * icount * rank
    target = block_target[0, 0]
    if n_rows & (n_rows - 1) or n_rows < 4 or n_cols != 2 or own_rows % 16:
        flat = graph_part(target, grad, similarity[0, 0], incoming, (jax.ShapeDtypeStruct((icount, rank), F32),))[0]
        owned = lax.psum_scatter(flat, "rows", scatter_dimension=0, tiled=True)
        squares = lax.psum(jnp.sum(owned * owned), ("rows", "cols"))
        mine = lax.dynamic_slice_in_dim(items[0], lax.axis_index("rows") * own_rows, own_rows, 0)
        return (mine.astype(F32) - 0.5 * owned / jnp.sqrt(squares / entries + 1e-06))[None]

    half = n_rows // 2
    block = jax.ShapeDtypeStruct((half, own_rows, rank), F32)

    def payload(bit):
        return jax.ShapeDtypeStruct((half + len(split_places(half, bit)), own_rows, rank), BF16)

    keep, give = graph_part(target, grad, similarity[0, 0], incoming, (block, block))
    total, sent = local_call(first_kernel, "add_core", (keep, swap(give, "rows", 1)), (block, payload(1)))
    bit = 1
    while 2 * bit < half:
        received = swap(sent, "rows", 2 * bit)
        total, sent = local_call(
            functools.partial(next_kernel, bit), "add_" + str(bit), (total, received), (block, payload(2 * bit))
        )
        bit *= 2
    own, squares = local_call(
        functools.partial(last_kernel, bit), "add_last", (total, swap(sent, "rows", 2 * bit)),
        (jax.ShapeDtypeStruct((own_rows, rank), F32), jax.ShapeDtypeStruct((8, 128), F32)),
    )
    squares = squares + swap(squares, "rows", 1)
    updated = local_call(
        functools.partial(update_kernel, entries), "update", (items[0], own, squares, swap(squares, "cols", 1)),
        jax.ShapeDtypeStruct((own_rows, rank), F32),
    )
    return updated[None]


def solution(mesh):
    in_specs = (
        P("rows", None),
        P("cols", None, None),
        P("rows", "cols", None, None, None),
        P("rows", "cols", None),
        P("rows", "cols", None),
        P("rows", "cols"),
        P("rows", "cols", None, None),
        P("rows", "cols", None),
        P("rows", "cols", None, None, None),
    )
    out_specs = P("cols", "rows", None)
    return jax.shard_map(shards, mesh=mesh, in_specs=in_specs, out_specs=out_specs, check_vma=False)
```

time: 170 us -> 53.3 us (0.31)
  waiting for transfers between devices: 57.9 us -> 12.9 us
  blocking collectives: 40.2 us -> 0 us
  matrix products: 25.2 us -> 0 us
  between operations: 14.1 us -> 0.73 us
  Pallas kernels: 0 us -> 13.1 us
  starting transfers between devices: 4.21 us -> 13.3 us
  local copies, waits for them, and re-layouts: 18.5 us -> 10.9 us
  other arithmetic: 8.52 us -> 1.39 us
    reduce_scatter x1 -> x0, waiting for transfers between devices: 56.4 us -> none  [shards(): owned = lax.psum_scatter(flat, 'rows', scatter_dimension=0, tiled=True)]
    psum x1 -> x0, blocking collectives: 40.2 us -> none  [shards(): squares = lax.psum(jnp.sum(owned * owned), ('rows', 'cols'))]
    dot_general x10 -> x0, matrix products: 25.2 us -> none  [the longest x4 14.6 us: tile_block(): jnp.einsum('kt,tbr->kbr', onehot, part, precision=lax.Precision.HIGHEST)]
    gather x9 -> x1, local copies, waits for them, and re-layouts: 16 us -> 2.11 us  [shards(): incoming = lax.all_to_all(panels[send_list[0, 0]], 'cols', 0, 0, tiled=True)]
    pallas_call x0 -> x7, Pallas kernels: none -> 13.1 us  [the longest x5 8.25 us: local_call(): pl.pallas_call(kernel, name=name, out_shape=out_shape, in_specs=[vmem] *...]
    ppermute x0 -> x6, waiting for transfers between devices: none -> 12.9 us  [swap(): return lax.ppermute(value, axis, [(i, i ^ bit) for i in range(size)])]
    ppermute x0 -> x6, starting transfers between devices: none -> 9.09 us  [swap(): return lax.ppermute(value, axis, [(i, i ^ bit) for i in range(size)])]
    unnamed x3 -> x28, local copies, waits for them, and re-layouts: 0.51 us -> 8.78 us
  transfers between devices with their start and end apart: 2 -> 7, of which waited for: 2 -> 6; matrix products, arithmetic and copies ran while one was open for 2% -> 0% of each run, Pallas kernels for 0% -> 8%
where the time goes in v1:
time: 53.3 us; the launch traced here: 52.4 us
  starting transfers between devices  13.3 us (25%)
  Pallas kernels  13.1 us (25%)
  waiting for transfers between devices  12.9 us (24%)
  local copies, waits for them, and re-layouts  10.9 us (20%)
  other arithmetic  1.39 us (3%)
  between operations  0.73 us (1%)
    ppermute x6, waiting for transfers between devices, swap(): return lax.ppermute(value, axis, [(i, i ^ bit) for i in range(size)])  12.9 us
    ppermute x6, starting transfers between devices, swap(): return lax.ppermute(value, axis, [(i, i ^ bit) for i in range(size)])  9.09 us
    unnamed x28, local copies, waits for them, and re-layouts  8.78 us
    pallas_call x5, Pallas kernels, local_call(): pl.pallas_call(kernel, name=name, out_shape=out_shape, in_specs=[vmem] *...  8.25 us
    all_to_all x1, starting transfers between devices, shards(): incoming = lax.all_to_all(panels[send_list[0, 0]], 'cols', 0, 0, tiled=True)  4.21 us
    pallas_call x1, Pallas kernels, rating_part(): pl.pallas_call(rating_kernel, name='rating_part', out_shape=jax.ShapeDtyp...  4.13 us
    gather x1, local copies, waits for them, and re-layouts, shards(): incoming = lax.all_to_all(panels[send_list[0, 0]], 'cols', 0, 0, tiled=True)  2.11 us
  transfers between devices with their start and end apart: 7, of which 6 were waited for; matrix products, arithmetic and copies ran while one was open for 0% of the time, Pallas kernels for 8%

profile of v1, /device:TPU:0, one launch (start us, length us, event | category | flops | bytes accessed | tf_op | source)
XLA Modules:
  0.0 52.4 jit_solution(4044635913671631828)
XLA Ops:
  0.0 0.0 copy-start.4
  0.0 0.0 copy-start.7
  0.0 0.7 %fusion = s32[2]{0:T(128)S(1)} fusion(s32[1,1,2,1]{2,3,1,0:T(1,128)} %param.15), kind=kLoop, calls=%fused_computation.3 | loop fusion | flops 6 | bytes 16 | tf_op jit(solution)/shard_map/select_n | solution.py:213
  0.7 2.1 %gather_fusion = bf16[2,128,256]{2,1,0:T(8,128)(2,1)} fusion(bf16[2,128,256]{2,1,0:T(8,128)(2,1)} %bitcast.17, s32[1024]{0:T(1024)S(1)} %pad_clamp_fusion), kind=kCustom, calls=%fused_computation | custom fusion | bytes 262152 | tf_op jit(solution)/shard_map/gather | solution.py:213
  2.8 4.2 %all-to-all-start = ((bf16[2,1,128,256]{3,2,1,0:T(8,128)(2,1)}), bf16[2,1,128,256]{3,2,1,0:T(8,128)(2,1)S(1)}, u32[]{:S(2)}, u32[]{:S(2)}) async-start(bf16[2,1,128,256]{3,2,1,0:T(8,128)(2,1)} %bitcast.10), calls=%async_computation | async-start | bytes 262144 | tf_op jit(solution)/shard_map/all_to_all | solution.py:213
  7.7 0.0 copy-start
  7.7 1.6 %copy-done = bf16[1,1,64,128,128]{4,3,2,1,0:T(8,128)(2,1)S(1)} copy-done((bf16[1,1,64,128,128]{4,3,2,1,0:T(8,128)(2,1)S(1)}, bf16[1,1,64,128,128]{4,3,2,1,0:T(8,128)(2,1)}, u32[]{:S(2)}) %copy-start) | copy-done | bytes 2097176
  9.3 0.0 copy-start.1
  9.3 0.9 %copy-done.1 = bf16[1,256,256]{2,1,0:T(8,128)(2,1)S(1)} copy-done((bf16[1,256,256]{2,1,0:T(8,128)(2,1)S(1)}, bf16[1,256,256]{2,1,0:T(8,128)(2,1)}, u32[]{:S(2)}) %copy-start.1) | copy-done | bytes 131096
  10.2 0.0 copy-start.2
  10.2 1.2 %copy-done.2 = bf16[2048,256]{1,0:T(8,128)(2,1)S(1)} copy-done((bf16[2048,256]{1,0:T(8,128)(2,1)S(1)}, bf16[2048,256]{1,0:T(8,128)(2,1)}, u32[]{:S(2)}) %copy-start.2) | copy-done | bytes 1048600
  11.4 0.0 copy-start.5
  11.4 0.7 %copy-done.5 = s32[1,1,64]{2,1,0:T(1,128)S(1)} copy-done((s32[1,1,64]{2,1,0:T(1,128)S(1)}, s32[1,1,64]{2,1,0:T(1,128)}, u32[]{:S(2)}) %copy-start.5) | copy-done | bytes 280
  12.1 0.0 copy-start.6
  12.1 0.7 %copy-done.6 = s32[1,1,64]{2,1,0:T(1,128)S(1)} copy-done((s32[1,1,64]{2,1,0:T(1,128)S(1)}, s32[1,1,64]{2,1,0:T(1,128)}, u32[]{:S(2)}) %copy-start.6) | copy-done | bytes 280
  12.7 4.1 %rating_part.1.grad = f32[256,256]{1,0:T(8,128)S(1)} custom-call(s32[64]{0:T(128)S(1)} %bitcast.22, s32[64]{0:T(128)S(1)} %bitcast.23, s32[1]{0:T(128)} %bitcast.15.count, bf16[2048,256]{1,0:T(8,128)(2,1)S(1)} %copy-done.2, bf16[256,256]{1,0:T(8,128)(2,1)S(1)} %bitcast.19, bf16[64,128,128]{2,1,0:T(8,128)(2,1)S(1)} %bitcast.16), custom_call_target="tpu_custom_call" | custom-call | flops 400000000 | bytes 4000000 | tf_op jit(solution)/shard_map/rating_part/pallas_call | solution.py:81
  16.8 0.0 all-to-all-done
  16.9 0.0 copy-done.4
  16.9 0.0 copy-done.7
  16.9 0.7 %graph_part.1 = (f32[8,16,256]{2,1,0:T(8,128)S(1)}, f32[8,16,256]{2,1,0:T(8,128)S(1)}) custom-call(s32[2]{0:T(128)S(1)} %bitcast.24, f32[256,256]{1,0:T(8,128)S(1)} %rating_part.1.grad, bf16[2,128,128]{2,1,0:T(8,128)(2,1)S(1)} %bitcast.21, bf16[2,128,256]{2,1,0:T(8,128)(2,1)S(1)} %bitcast.20), custom_call_target="tpu_custom_call" | custom-call | tf_op jit(solution)/shard_map/graph_part/pallas_call | solution.py:125
  17.6 0.0 copy-start.3
  17.6 0.6 %copy-done.3 = f32[8,16,256]{2,1,0:T(8,128)} copy-done((f32[8,16,256]{2,1,0:T(8,128)}, f32[8,16,256]{2,1,0:T(8,128)S(1)}, u32[]{:S(2)}) %copy-start.3) | copy-done | bytes 131096
  18.3 0.0 collective-permute-start
  18.3 1.3 %collective-permute-done.received = f32[8,16,256]{2,1,0:T(8,128)S(1)} collective-permute-done((f32[8,16,256]{2,1,0:T(8,128)S(1)}, f32[8,16,256]{2,1,0:T(8,128)S(1)}, u32[]{:S(2)}, u32[]{:S(2)}) %collective-permute-start) | collective-permute-done | bytes 131104 | tf_op jit(solution)/shard_map/ppermute | solution.py:202
  19.6 0.0 copy-start.8
  19.6 0.6 %copy-done.8 = f32[8,16,256]{2,1,0:T(8,128)} copy-done((f32[8,16,256]{2,1,0:T(8,128)}, f32[8,16,256]{2,1,0:T(8,128)S(1)}, u32[]{:S(2)}) %copy-start.8) | copy-done | bytes 131096
  20.3 1.7 %add_core.1 = (f32[8,16,256]{2,1,0:T(8,128)}, bf16[12,16,256]{2,1,0:T(8,128)(2,1)}) custom-call(f32[8,16,256]{2,1,0:T(8,128)} %copy-done.3, f32[8,16,256]{2,1,0:T(8,128)} %copy-done.8), custom_call_target="tpu_custom_call" | custom-call | tf_op jit(solution)/shard_map/add_core/pallas_call | solution.py:186
  22.0 1.8 %collective-permute-start.1 = (bf16[12,16,256]{2,1,0:T(8,128)(2,1)}, bf16[12,16,256]{2,1,0:T(8,128)(2,1)S(1)}, u32[]{:S(2)}, u32[]{:S(2)}) collective-permute-start(bf16[12,16,256]{2,1,0:T(8,128)(2,1)} %get-tuple-element.18), channel_id=1, source_target_pairs={{0,4},{2,6},{4,0},{6,2},{8,12},{10,14},{12,8},{14,10},{16,20},{18,... | collective-permute-start | bytes 294920 | tf_op jit(solution)/shard_map/ppermute | solution.py:202
  23.7 3.3 %collective-permute-done.1.received = bf16[12,16,256]{2,1,0:T(8,128)(2,1)S(1)} collective-permute-done((bf16[12,16,256]{2,1,0:T(8,128)(2,1)}, bf16[12,16,256]{2,1,0:T(8,128)(2,1)S(1)}, u32[]{:S(2)}, u32[]{:S(2)}) %collective-permute-start.1) | collective-permute-done | bytes 98336 | tf_op jit(solution)/shard_map/ppermute | solution.py:202
  27.1 0.0 copy-start.9
  27.1 0.6 %copy-done.9 = bf16[12,16,256]{2,1,0:T(8,128)(2,1)} copy-done((bf16[12,16,256]{2,1,0:T(8,128)(2,1)}, bf16[12,16,256]{2,1,0:T(8,128)(2,1)S(1)}, u32[]{:S(2)}) %copy-start.9) | copy-done | bytes 98328
  27.7 1.7 %add_1.1 = (f32[8,16,256]{2,1,0:T(8,128)}, bf16[10,16,256]{2,1,0:T(8,128)(2,1)}) custom-call(f32[8,16,256]{2,1,0:T(8,128)} %get-tuple-element.17.before, bf16[12,16,256]{2,1,0:T(8,128)(2,1)} %copy-done.9), custom_call_target="tpu_custom_call" | custom-call | tf_op jit(solution)/shard_map/add_1/pallas_call | solution.py:186
  29.4 2.1 %collective-permute-start.2 = (bf16[10,16,256]{2,1,0:T(8,128)(2,1)}, bf16[10,16,256]{2,1,0:T(8,128)(2,1)S(1)}, u32[]{:S(2)}, u32[]{:S(2)}) collective-permute-start(bf16[10,16,256]{2,1,0:T(8,128)(2,1)} %get-tuple-element.20), channel_id=1, source_target_pairs={{0,8},{2,10},{4,12},{6,14},{8,0},{10,2},{12,4},{14,6},{16,24},{18,... | collective-permute-start | bytes 245768 | tf_op jit(solution)/shard_map/ppermute | solution.py:202
  31.4 2.6 %collective-permute-done.2.received = bf16[10,16,256]{2,1,0:T(8,128)(2,1)S(1)} collective-permute-done((bf16[10,16,256]{2,1,0:T(8,128)(2,1)}, bf16[10,16,256]{2,1,0:T(8,128)(2,1)S(1)}, u32[]{:S(2)}, u32[]{:S(2)}) %collective-permute-start.2) | collective-permute-done | bytes 81952 | tf_op jit(solution)/shard_map/ppermute | solution.py:202
  34.1 0.6 %copy-done.10 = bf16[10,16,256]{2,1,0:T(8,128)(2,1)} copy-done((bf16[10,16,256]{2,1,0:T(8,128)(2,1)}, bf16[10,16,256]{2,1,0:T(8,128)(2,1)S(1)}, u32[]{:S(2)}) %copy-start.10) | copy-done | bytes 81944
  34.7 1.6 %add_2.1 = (f32[8,16,256]{2,1,0:T(8,128)}, bf16[9,16,256]{2,1,0:T(8,128)(2,1)}) custom-call(f32[8,16,256]{2,1,0:T(8,128)} %get-tuple-element.19.before, bf16[10,16,256]{2,1,0:T(8,128)(2,1)} %copy-done.10), custom_call_target="tpu_custom_call" | custom-call | tf_op jit(solution)/shard_map/add_2/pallas_call | solution.py:186
  36.3 3.4 %collective-permute-start.3 = (bf16[9,16,256]{2,1,0:T(8,128)(2,1)}, bf16[9,16,256]{2,1,0:T(8,128)(2,1)S(1)}, u32[]{:S(2)}, u32[]{:S(2)}) collective-permute-start(bf16[9,16,256]{2,1,0:T(8,128)(2,1)} %get-tuple-element.22), channel_id=1, source_target_pairs={{0,16},{2,18},{4,20},{6,22},{8,24},{10,26},{12,28},{14,30},{16,0},... | collective-permute-start | bytes 221192 | tf_op jit(solution)/shard_map/ppermute | solution.py:202
  39.7 2.5 %collective-permute-done.3.received = bf16[9,16,256]{2,1,0:T(8,128)(2,1)S(1)} collective-permute-done((bf16[9,16,256]{2,1,0:T(8,128)(2,1)}, bf16[9,16,256]{2,1,0:T(8,128)(2,1)S(1)}, u32[]{:S(2)}, u32[]{:S(2)}) %collective-permute-start.3) | collective-permute-done | bytes 73760 | tf_op jit(solution)/shard_map/ppermute | solution.py:202
  42.2 0.6 %copy-done.11 = bf16[9,16,256]{2,1,0:T(8,128)(2,1)} copy-done((bf16[9,16,256]{2,1,0:T(8,128)(2,1)}, bf16[9,16,256]{2,1,0:T(8,128)(2,1)S(1)}, u32[]{:S(2)}) %copy-start.11) | copy-done | bytes 73752
  42.9 1.6 %add_last.1 = (f32[16,256]{1,0:T(8,128)}, f32[8,128]{1,0:T(8,128)}) custom-call(f32[8,16,256]{2,1,0:T(8,128)} %get-tuple-element.21.before, bf16[9,16,256]{2,1,0:T(8,128)(2,1)} %copy-done.11), custom_call_target="tpu_custom_call" | custom-call | tf_op jit(solution)/shard_map/add_last/pallas_call | solution.py:186
  44.4 0.0 collective-permute-start.4
  44.4 1.4 %collective-permute-done.4 = f32[8,128]{1,0:T(8,128)S(1)} collective-permute-done((f32[8,128]{1,0:T(8,128)}, f32[8,128]{1,0:T(8,128)S(1)}, u32[]{:S(2)}, u32[]{:S(2)}) %collective-permute-start.4) | collective-permute-done | bytes 4128 | tf_op jit(solution)/shard_map/ppermute | solution.py:202
  45.8 0.7 %add.16.squares = f32[8,128]{1,0:T(8,128)S(1)} add(f32[8,128]{1,0:T(8,128)} %get-tuple-element.24, f32[8,128]{1,0:T(8,128)S(1)} %collective-permute-done.4) | non-fusion elementwise | flops 1024 | bytes 12288 | tf_op jit(solution)/shard_map/add | solution.py:247
  46.5 1.9 %collective-permute-start.5 = (f32[8,128]{1,0:T(8,128)S(1)}, f32[8,128]{1,0:T(8,128)S(1)}, u32[]{:S(2)}, u32[]{:S(2)}) collective-permute-start(f32[8,128]{1,0:T(8,128)S(1)} %add.16.squares), channel_id=1, source_target_pairs={{0,1},{1,0},{2,3},{3,2},{4,5},{5,4},{6,7},{7,6},{8,9},{9,8},{10,11... | collective-permute-start | bytes 12296 | tf_op jit(solution)/shard_map/ppermute | solution.py:202
  48.4 1.7 %collective-permute-done.5.more = f32[8,128]{1,0:T(8,128)S(1)} collective-permute-done((f32[8,128]{1,0:T(8,128)S(1)}, f32[8,128]{1,0:T(8,128)S(1)}, u32[]{:S(2)}, u32[]{:S(2)}) %collective-permute-start.5) | collective-permute-done | bytes 4128 | tf_op jit(solution)/shard_map/ppermute | solution.py:202
  50.1 0.0 copy-done.12
  50.1 0.6 %copy-done.13 = f32[8,128]{1,0:T(8,128)} copy-done((f32[8,128]{1,0:T(8,128)}, f32[8,128]{1,0:T(8,128)S(1)}, u32[]{:S(2)}) %copy-start.13) | copy-done | bytes 4120
  50.7 1.7 %update.1 = f32[16,256]{1,0:T(8,128)} custom-call(bf16[256,256]{1,0:T(8,128)(2,1)} %bitcast.18, f32[16,256]{1,0:T(8,128)} %get-tuple-element.23.own, f32[8,128]{1,0:T(8,128)} %copy-done.12, f32[8,128]{1,0:T(8,128)} %copy-done.13), custom_call_target="tpu_custom_call" | custom-call | tf_op jit(solution)/shard_map/update/pallas_call | solution.py:186
  (5 shorter events, 0.0 us)
Async XLA Ops:
  0.0 16.9 %copy-start.4 = (bf16[1,1,2,128,128]{4,3,2,1,0:T(8,128)(2,1)S(1)}, bf16[1,1,2,128,128]{4,3,2,1,0:T(8,128)(2,1)}, u32[]{:S(2)}) copy-start(bf16[1,1,2,128,128]{4,3,2,1,0:T(8,128)(2,1)} %param.17) | copy-start | bytes 196612
  0.0 16.9 %copy-start.7 = (s32[1,1,2]{2,1,0:T(1,128)S(1)}, s32[1,1,2]{2,1,0:T(1,128)}, u32[]{:S(2)}) copy-start(s32[1,1,2]{2,1,0:T(1,128)} %param.16) | copy-start | bytes 28
  2.8 14.0 %all-to-all-start = ((bf16[2,1,128,256]{3,2,1,0:T(8,128)(2,1)}), bf16[2,1,128,256]{3,2,1,0:T(8,128)(2,1)S(1)}, u32[]{:S(2)}, u32[]{:S(2)}) async-start(bf16[2,1,128,256]{3,2,1,0:T(8,128)(2,1)} %bitcast.10), calls=%async_computation | async-start | bytes 262144 | tf_op jit(solution)/shard_map/all_to_all | solution.py:213
  7.7 1.6 %copy-start = (bf16[1,1,64,128,128]{4,3,2,1,0:T(8,128)(2,1)S(1)}, bf16[1,1,64,128,128]{4,3,2,1,0:T(8,128)(2,1)}, u32[]{:S(2)}) copy-start(bf16[1,1,64,128,128]{4,3,2,1,0:T(8,128)(2,1)} %param.11) | copy-start | bytes 6291460
  9.3 0.9 %copy-start.1 = (bf16[1,256,256]{2,1,0:T(8,128)(2,1)S(1)}, bf16[1,256,256]{2,1,0:T(8,128)(2,1)}, u32[]{:S(2)}) copy-start(bf16[1,256,256]{2,1,0:T(8,128)(2,1)} %param.10) | copy-start | bytes 393220
  10.2 1.2 %copy-start.2 = (bf16[2048,256]{1,0:T(8,128)(2,1)S(1)}, bf16[2048,256]{1,0:T(8,128)(2,1)}, u32[]{:S(2)}) copy-start(bf16[2048,256]{1,0:T(8,128)(2,1)} %users_hbm.1) | copy-start | bytes 3145732
  11.4 0.7 %copy-start.5 = (s32[1,1,64]{2,1,0:T(1,128)S(1)}, s32[1,1,64]{2,1,0:T(1,128)}, u32[]{:S(2)}) copy-start(s32[1,1,64]{2,1,0:T(1,128)} %param.12) | copy-start | bytes 772
  12.1 0.7 %copy-start.6 = (s32[1,1,64]{2,1,0:T(1,128)S(1)}, s32[1,1,64]{2,1,0:T(1,128)}, u32[]{:S(2)}) copy-start(s32[1,1,64]{2,1,0:T(1,128)} %param.13) | copy-start | bytes 772
  17.6 0.6 %copy-start.3 = (f32[8,16,256]{2,1,0:T(8,128)}, f32[8,16,256]{2,1,0:T(8,128)S(1)}, u32[]{:S(2)}) copy-start(f32[8,16,256]{2,1,0:T(8,128)S(1)} %get-tuple-element.15.keep) | copy-start | bytes 393220
  18.3 1.3 %collective-permute-start = (f32[8,16,256]{2,1,0:T(8,128)S(1)}, f32[8,16,256]{2,1,0:T(8,128)S(1)}, u32[]{:S(2)}, u32[]{:S(2)}) collective-permute-start(f32[8,16,256]{2,1,0:T(8,128)S(1)} %get-tuple-element.16), channel_id=1, source_target_pairs={{0,2},{2,0},{4,6},{6,4},{8,10},{10,8},{12,14},{14,12},{16,18},{18,... | collective-permute-start | bytes 393224 | tf_op jit(solution)/shard_map/ppermute | solution.py:202
  19.6 0.6 %copy-start.8 = (f32[8,16,256]{2,1,0:T(8,128)}, f32[8,16,256]{2,1,0:T(8,128)S(1)}, u32[]{:S(2)}) copy-start(f32[8,16,256]{2,1,0:T(8,128)S(1)} %collective-permute-done.received) | copy-start | bytes 393220
  22.0 5.1 %collective-permute-start.1 = (bf16[12,16,256]{2,1,0:T(8,128)(2,1)}, bf16[12,16,256]{2,1,0:T(8,128)(2,1)S(1)}, u32[]{:S(2)}, u32[]{:S(2)}) collective-permute-start(bf16[12,16,256]{2,1,0:T(8,128)(2,1)} %get-tuple-element.18), channel_id=1, source_target_pairs={{0,4},{2,6},{4,0},{6,2},{8,12},{10,14},{12,8},{14,10},{16,20},{18,... | collective-permute-start | bytes 294920 | tf_op jit(solution)/shard_map/ppermute | solution.py:202
  27.1 0.6 %copy-start.9 = (bf16[12,16,256]{2,1,0:T(8,128)(2,1)}, bf16[12,16,256]{2,1,0:T(8,128)(2,1)S(1)}, u32[]{:S(2)}) copy-start(bf16[12,16,256]{2,1,0:T(8,128)(2,1)S(1)} %collective-permute-done.1.received) | copy-start | bytes 294916
  29.4 4.7 %collective-permute-start.2 = (bf16[10,16,256]{2,1,0:T(8,128)(2,1)}, bf16[10,16,256]{2,1,0:T(8,128)(2,1)S(1)}, u32[]{:S(2)}, u32[]{:S(2)}) collective-permute-start(bf16[10,16,256]{2,1,0:T(8,128)(2,1)} %get-tuple-element.20), channel_id=1, source_target_pairs={{0,8},{2,10},{4,12},{6,14},{8,0},{10,2},{12,4},{14,6},{16,24},{18,... | collective-permute-start | bytes 245768 | tf_op jit(solution)/shard_map/ppermute | solution.py:202
  34.1 0.6 %copy-start.10 = (bf16[10,16,256]{2,1,0:T(8,128)(2,1)}, bf16[10,16,256]{2,1,0:T(8,128)(2,1)S(1)}, u32[]{:S(2)}) copy-start(bf16[10,16,256]{2,1,0:T(8,128)(2,1)S(1)} %collective-permute-done.2.received) | copy-start | bytes 245764
  36.3 5.9 %collective-permute-start.3 = (bf16[9,16,256]{2,1,0:T(8,128)(2,1)}, bf16[9,16,256]{2,1,0:T(8,128)(2,1)S(1)}, u32[]{:S(2)}, u32[]{:S(2)}) collective-permute-start(bf16[9,16,256]{2,1,0:T(8,128)(2,1)} %get-tuple-element.22), channel_id=1, source_target_pairs={{0,16},{2,18},{4,20},{6,22},{8,24},{10,26},{12,28},{14,30},{16,0},... | collective-permute-start | bytes 221192 | tf_op jit(solution)/shard_map/ppermute | solution.py:202
  42.2 0.6 %copy-start.11 = (bf16[9,16,256]{2,1,0:T(8,128)(2,1)}, bf16[9,16,256]{2,1,0:T(8,128)(2,1)S(1)}, u32[]{:S(2)}) copy-start(bf16[9,16,256]{2,1,0:T(8,128)(2,1)S(1)} %collective-permute-done.3.received) | copy-start | bytes 221188
  44.4 1.4 %collective-permute-start.4 = (f32[8,128]{1,0:T(8,128)}, f32[8,128]{1,0:T(8,128)S(1)}, u32[]{:S(2)}, u32[]{:S(2)}) collective-permute-start(f32[8,128]{1,0:T(8,128)} %get-tuple-element.24), channel_id=1, source_target_pairs={{0,2},{2,0},{4,6},{6,4},{8,10},{10,8},{12,14},{14,12},{16,18},{18,... | collective-permute-start | bytes 12296 | tf_op jit(solution)/shard_map/ppermute | solution.py:202
  46.5 3.6 %copy-start.12 = (f32[8,128]{1,0:T(8,128)}, f32[8,128]{1,0:T(8,128)S(1)}, u32[]{:S(2)}) copy-start(f32[8,128]{1,0:T(8,128)S(1)} %add.16.squares) | copy-start | bytes 12292
  46.5 3.6 %collective-permute-start.5 = (f32[8,128]{1,0:T(8,128)S(1)}, f32[8,128]{1,0:T(8,128)S(1)}, u32[]{:S(2)}, u32[]{:S(2)}) collective-permute-start(f32[8,128]{1,0:T(8,128)S(1)} %add.16.squares), channel_id=1, source_target_pairs={{0,1},{1,0},{2,3},{3,2},{4,5},{5,4},{6,7},{7,6},{8,9},{9,8},{10,11... | collective-permute-start | bytes 12296 | tf_op jit(solution)/shard_map/ppermute | solution.py:202
  50.1 0.6 %copy-start.13 = (f32[8,128]{1,0:T(8,128)}, f32[8,128]{1,0:T(8,128)S(1)}, u32[]{:S(2)}) copy-start(f32[8,128]{1,0:T(8,128)S(1)} %collective-permute-done.5.more) | copy-start | bytes 12292

commit v2 on v1

--- a/solution.py
+++ b/solution.py
@@ -10,6 +10,11 @@
 F32 = jnp.float32
 BF16 = jnp.bfloat16
 CHUNKS = 8
+SMALL = 4 * 1024 * 1024
+
+
+def in_hbm(*arrays):
+    return [pltpu.with_memory_space_constraint(a, pltpu.HBM) for a in arrays]
 
 
 def dot(a, b, dims):
@@ -17,18 +22,26 @@
 
 
 def rating_kernel(
-    user_idx, item_idx, count, users_hbm, items_hbm, ratings_hbm, grad_ref,
-    users, items, ratings, users_t, pred, err, sem_u, sem_i, sem_r,
+    user_idx_hbm, item_idx_hbm, count_hbm, users_hbm, items_hbm, ratings_hbm, grad_ref, mine_ref,
+    user_idx, item_idx, count, users, items, ratings, users_t, pred, err, sem_s, sem_u, sem_i, sem_r,
 ):
     n_tiles, tile = ratings.shape[0], ratings.shape[1]
     n_user = users.shape[0] // tile
     n_item = items.shape[0] // tile
     width = n_tiles // CHUNKS
-    live = count[0]
+    scalars = [
+        pltpu.make_async_copy(source, target, sem_s.at[n])
+        for n, (source, target) in enumerate(((count_hbm, count), (user_idx_hbm, user_idx), (item_idx_hbm, item_idx)))
+    ]
+    for copy in scalars:
+        copy.start()
     copy_u = pltpu.make_async_copy(users_hbm, users, sem_u)
     copy_i = pltpu.make_async_copy(items_hbm, items, sem_i)
     copy_i.start()
     copy_u.start()
+    for copy in scalars:
+        copy.wait()
+    live = count[0]
 
     def chunk_copy(c):
         span = pl.ds(c * width, width)
@@ -41,6 +54,8 @@
 
     err[...] = jnp.zeros_like(err)
     copy_i.wait()
+    rows = mine_ref.shape[0]
+    mine_ref[...] = items[pl.ds(pl.multiple_of(lax.axis_index("rows") * rows, rows), rows), :]
     copy_u.wait()
     for u in range(n_user):
         rows = pl.ds(u * tile, tile)
@@ -73,64 +88,124 @@
         grad_ref[j * tile:(j + 1) * tile, :] = total.T
 
 
-def rating_part(user_idx, item_idx, count, users, items, ratings):
+def rating_part(user_idx, item_idx, count, users, items, ratings, own_rows):
     n_tiles, tile, unused = ratings.shape
     n_pairs = (users.shape[0] // tile) * (items.shape[0] // tile)
-    smem = pl.BlockSpec(memory_space=pltpu.SMEM)
-    hbm = pl.BlockSpec(memory_space=pl.ANY)
+    hbm = pl.BlockSpec(memory_space=pltpu.HBM)
+    vmem = pl.BlockSpec(memory_space=pltpu.VMEM)
     return pl.pallas_call(
         rating_kernel,
         name="rating_part",
-        out_shape=jax.ShapeDtypeStruct(items.shape, F32),
-        in_specs=[smem] * 3 + [hbm] * 3,
-        out_specs=pl.BlockSpec(memory_space=pltpu.VMEM),
+        out_shape=(
+            jax.ShapeDtypeStruct(items.shape, F32),
+            jax.ShapeDtypeStruct((own_rows, items.shape[1]), BF16),
+        ),
+        in_specs=[hbm] * 6,
+        out_specs=(vmem, vmem),
         scratch_shapes=[
+            pltpu.SMEM(user_idx.shape, jnp.int32),
+            pltpu.SMEM(item_idx.shape, jnp.int32),
+            pltpu.SMEM(count.shape, jnp.int32),
             pltpu.VMEM(users.shape, BF16),
             pltpu.VMEM(items.shape, BF16),
             pltpu.VMEM(ratings.shape, BF16),
             pltpu.VMEM(users.shape[::-1], BF16),
             pltpu.VMEM((n_pairs, tile, tile), F32),
             pltpu.VMEM((n_pairs, tile, tile), F32),
+            pltpu.SemaphoreType.DMA((3,)),
             pltpu.SemaphoreType.DMA,
             pltpu.SemaphoreType.DMA,
             pltpu.SemaphoreType.DMA((CHUNKS,)),
         ],
         compiler_params=pltpu.CompilerParams(vmem_limit_bytes=48 * 1024 * 1024),
         cost_estimate=pl.CostEstimate(flops=4 * 10**8, bytes_accessed=4 * 10**6, transcendentals=0),
-    )(user_idx, item_idx, count, users, items, ratings)
-
-
-def graph_kernel(target, grad, similarity, panels, *outs):
+    )(*in_hbm(user_idx, item_idx), count, *in_hbm(users, items, ratings))
+
+
+def pick_kernel(send_list_hbm, items_hbm, kept, sent, send_list, items, sem_s, sem):
+    copy_list = pltpu.make_async_copy(send_list_hbm, send_list, sem_s)
+    copy = pltpu.make_async_copy(items_hbm, items, sem)
+    copy_list.start()
+    copy.start()
+    copy_list.wait()
+    copy.wait()
+    tile = kept.shape[0]
+    me = lax.axis_index("cols")
+    for out, col in ((kept, me), (sent, 1 - me)):
+        out[...] = items[pl.ds(pl.multiple_of(send_list[col] * tile, tile), tile), :]
+
+
+def pick_panels(send_list, items, tile):
+    panel = jax.ShapeDtypeStruct((tile, items.shape[1]), BF16)
+    vmem = pl.BlockSpec(memory_space=pltpu.VMEM)
+    return pl.pallas_call(
+        pick_kernel,
+        name="pick_panels",
+        out_shape=(panel, panel),
+        in_specs=[pl.BlockSpec(memory_space=pltpu.HBM)] * 2,
+        out_specs=(vmem, vmem),
+        scratch_shapes=[
+            pltpu.SMEM(send_list.shape, jnp.int32),
+            pltpu.VMEM(items.shape, BF16),
+            pltpu.SemaphoreType.DMA,
+            pltpu.SemaphoreType.DMA,
+        ],
+        compiler_params=pltpu.CompilerParams(vmem_limit_bytes=SMALL),
+    )(*in_hbm(send_list, items))
+
+
+def parity(value):
+    return bin(value).count("1") % 2
+
+
+def hops(n_rows, odd):
+    bits = [1 << b for b in range(1, n_rows.bit_length() - 1)]
+    return bits[1:] + bits[:1] if odd else bits
+
+
+def offset(n_rows, odd, q):
+    value = sum(bit for b, bit in enumerate(hops(n_rows, odd)) if q >> b & 1)
+    return value | parity(value)
+
+
+def graph_kernel(n_panels, target, grad, similarity, *refs):
+    panels, outs, total = refs[:n_panels], refs[n_panels:-1], refs[-1]
     blocks, tile, unused = similarity.shape
-    total = outs[-1]
     total[...] = grad[...]
+    col = lax.axis_index("cols")
     for k in range(blocks):
-        rows = pl.ds(pl.multiple_of(target[k] * tile, tile), tile)
-        total[rows, :] += dot(similarity[k], panels[k], ((1,), (0,)))
+        block = k if n_panels == 1 else k ^ col
+        panel = panels[0][k] if n_panels == 1 else panels[k][...]
+        rows = pl.ds(pl.multiple_of(target[block] * tile, tile), tile)
+        total[rows, :] += dot(similarity[block], panel, ((1,), (0,)))
     me = lax.axis_index("rows")
-    if len(outs) == 2:
+    if len(outs) == 1:
         outs[0][...] = total[...]
         return
-    keep, give = outs[:2]
+    keep, give = outs
     half, own = keep.shape[:2]
+    odd = sum((me >> b) & 1 for b in range(half.bit_length())) % 2
     for q in range(half):
-        for core, out in ((0, keep), (1, give)):
-            place = pl.multiple_of((me ^ (2 * q + core)) * own, own)
-            out[q] = total[pl.ds(place, own), :]
+        even_place, odd_place = (offset(2 * half, parity_, q) for parity_ in (0, 1))
+        for out, block in (
+            (keep, me ^ jnp.where(odd == 1, odd_place, even_place)),
+            (give, me ^ 1 ^ jnp.where(odd == 1, even_place, odd_place)),
+        ):
+            out[q] = total[pl.ds(pl.multiple_of(block * own, own), own), :]
 
 
 def graph_part(target, grad, similarity, panels, out_shape):
     smem = pl.BlockSpec(memory_space=pltpu.SMEM)
     vmem = pl.BlockSpec(memory_space=pltpu.VMEM)
     return pl.pallas_call(
-        graph_kernel,
+        functools.partial(graph_kernel, len(panels)),
         name="graph_part",
         out_shape=out_shape,
-        in_specs=[smem] + [vmem] * 3,
+        in_specs=[smem] + [vmem] * (2 + len(panels)),
         out_specs=jax.tree.map(lambda unused: vmem, out_shape),
         scratch_shapes=[pltpu.VMEM(grad.shape, F32)],
-        compiler_params=pltpu.CompilerParams(vmem_limit_bytes=32 * 1024 * 1024),
-    )(target, grad, similarity, panels)
+        compiler_params=pltpu.CompilerParams(vmem_limit_bytes=SMALL if grad.size <= 2**16 else 32 * 1024 * 1024),
+    )(target, grad, similarity, *panels)
 
 
 def split_places(half, bit):
@@ -186,20 +261,23 @@
     return pl.pallas_call(
         kernel, name=name, out_shape=out_shape, in_specs=[vmem] * len(args),
         out_specs=jax.tree.map(lambda unused: vmem, out_shape),
+        compiler_params=pltpu.CompilerParams(vmem_limit_bytes=SMALL),
     )(*args)
 
 
-def update_kernel(entries, items, own, squares, more, new):
-    me = lax.axis_index("rows")
-    rows = own.shape[0]
+def update_kernel(entries, mine, own, squares, more, new):
     meansq = jnp.sum(squares[...] + more[...], keepdims=True) / entries
-    mine = items[pl.ds(pl.multiple_of(me * rows, rows), rows), :].astype(F32)
-    new[...] = mine - 0.5 * own[...] / jnp.sqrt(meansq + 1e-06)
+    new[...] = mine[...].astype(F32) - 0.5 * own[...] / jnp.sqrt(meansq + 1e-06)
 
 
 def swap(value, axis, bit):
     size = lax.axis_size(axis)
     return lax.ppermute(value, axis, [(i, i ^ bit) for i in range(size)])
+
+
+def hop(value, b):
+    size = lax.axis_size("rows")
+    return lax.ppermute(value, "rows", [(i, i ^ 1 ^ hops(size, parity(i))[b]) for i in range(size)])
 
 
 def shards(
@@ -210,19 +288,23 @@
     tile = ratings.shape[-1]
     blocks = similarity.shape[2]
     panels = items[0].reshape(-1, tile, rank)
-    incoming = lax.all_to_all(panels[send_list[0, 0]], "cols", 0, 0, tiled=True)
-    incoming = incoming.reshape(blocks, tile, rank)
-    grad = rating_part(
-        tile_users[0, 0], tile_items[0, 0], tile_count[0], users, items[0], ratings[0, 0]
+    slots = send_list.shape[3]
+    if n_cols == 2 and slots == 1:
+        kept, sent = pick_panels(send_list.reshape(-1), items[0], tile)
+        incoming = (kept, swap(sent, "cols", 1))
+    else:
+        incoming = lax.all_to_all(panels[send_list[0, 0]], "cols", 0, 0, tiled=True)
+        incoming = (incoming.reshape(blocks, tile, rank),)
+    own_rows = icount // n_rows
+    grad, mine = rating_part(
+        tile_users.reshape(-1), tile_items.reshape(-1), tile_count.reshape(-1), users, items[0], ratings[0, 0], own_rows
     )
-    own_rows = icount // n_rows
     entries = n_cols * icount * rank
     target = block_target[0, 0]
     if n_rows & (n_rows - 1) or n_rows < 4 or n_cols != 2 or own_rows % 16:
         flat = graph_part(target, grad, similarity[0, 0], incoming, (jax.ShapeDtypeStruct((icount, rank), F32),))[0]
         owned = lax.psum_scatter(flat, "rows", scatter_dimension=0, tiled=True)
         squares = lax.psum(jnp.sum(owned * owned), ("rows", "cols"))
-        mine = lax.dynamic_slice_in_dim(items[0], lax.axis_index("rows") * own_rows, own_rows, 0)
         return (mine.astype(F32) - 0.5 * owned / jnp.sqrt(squares / entries + 1e-06))[None]
 
     half = n_rows // 2
@@ -233,20 +315,18 @@
 
     keep, give = graph_part(target, grad, similarity[0, 0], incoming, (block, block))
     total, sent = local_call(first_kernel, "add_core", (keep, swap(give, "rows", 1)), (block, payload(1)))
-    bit = 1
-    while 2 * bit < half:
-        received = swap(sent, "rows", 2 * bit)
+    n_hops = len(hops(n_rows, 0))
+    for b in range(n_hops - 1):
         total, sent = local_call(
-            functools.partial(next_kernel, bit), "add_" + str(bit), (total, received), (block, payload(2 * bit))
+            functools.partial(next_kernel, 1 << b), "add_" + str(b), (total, hop(sent, b)), (block, payload(2 << b))
         )
-        bit *= 2
     own, squares = local_call(
-        functools.partial(last_kernel, bit), "add_last", (total, swap(sent, "rows", 2 * bit)),
+        functools.partial(last_kernel, half // 2), "add_last", (total, hop(sent, n_hops - 1)),
         (jax.ShapeDtypeStruct((own_rows, rank), F32), jax.ShapeDtypeStruct((8, 128), F32)),
     )
     squares = squares + swap(squares, "rows", 1)
     updated = local_call(
-        functools.partial(update_kernel, entries), "update", (items[0], own, squares, swap(squares, "cols", 1)),
+        functools.partial(update_kernel, entries), "update", (mine, own, squares, swap(squares, ("rows", "cols"), 3)),
         jax.ShapeDtypeStruct((own_rows, rank), F32),
     )
     return updated[None]

time: 53.3 us -> 29.9 us (0.56); the launches traced: 52.4 us -> 29.7 us
  local copies, waits for them, and re-layouts: 10.9 us -> 0.01 us
  Pallas kernels: 13.1 us -> 6.84 us
  starting transfers between devices: 13.3 us -> 10.2 us
  other arithmetic: 1.39 us -> 0.01 us
  waiting for transfers between devices: 12.9 us -> 11.9 us
    unnamed x28 -> x4, local copies, waits for them, and re-layouts: 8.78 us -> 0.01 us
    ppermute x6 -> x4, waiting for transfers between devices: 12.9 us -> 4.77 us  [swap(): return lax.ppermute(value, axis, [(i, i ^ bit) for i in range(size)])]
    pallas_call x5, Pallas kernels: 8.25 us -> 0.85 us  [local_call(): pl.pallas_call(kernel, name=name, out_shape=out_shape, in_specs=[vmem] *...]
    ppermute x0 -> x3, waiting for transfers between devices: none -> 7.13 us  [hop(): lax.ppermute(value, 'rows', [(i, i ^ 1 ^ hops(size, parity(i))[b]) for i...]
    ppermute x0 -> x3, starting transfers between devices: none -> 6.35 us  [hop(): lax.ppermute(value, 'rows', [(i, i ^ 1 ^ hops(size, parity(i))[b]) for i...]
    ppermute x6 -> x4, starting transfers between devices: 9.09 us -> 3.89 us  [swap(): return lax.ppermute(value, axis, [(i, i ^ bit) for i in range(size)])]
    all_to_all x1 -> x0, starting transfers between devices: 4.21 us -> none  [shards(): incoming = lax.all_to_all(panels[send_list[0, 0]], 'cols', 0, 0, tiled=True)]
    gather x1 -> x0, local copies, waits for them, and re-layouts: 2.11 us -> none  [shards(): incoming = lax.all_to_all(panels[send_list[0, 0]], 'cols', 0, 0, tiled=True)]
  transfers between devices with their start and end apart: 7 -> 7, of which waited for: 6 -> 6; matrix products, arithmetic and copies ran while one was open for 0% -> 0% of each run, Pallas kernels for 8% -> 14%
where the time goes in v2:
time: 29.9 us; the launch traced here: 29.7 us
  waiting for transfers between devices  11.9 us (40%)
  starting transfers between devices  10.2 us (34%)
  Pallas kernels  6.84 us (23%)
  between operations  0.73 us (2%)
    ppermute x3, waiting for transfers between devices, hop(): lax.ppermute(value, 'rows', [(i, i ^ 1 ^ hops(size, parity(i))[b]) for i...  7.13 us
    ppermute x3, starting transfers between devices, hop(): lax.ppermute(value, 'rows', [(i, i ^ 1 ^ hops(size, parity(i))[b]) for i...  6.35 us
    ppermute x4, waiting for transfers between devices, swap(): return lax.ppermute(value, axis, [(i, i ^ bit) for i in range(size)])  4.77 us
    pallas_call x1, Pallas kernels, rating_part(): pl.pallas_call(rating_kernel, name='rating_part', out_shape=(jax.ShapeDty...  4.28 us
    ppermute x4, starting transfers between devices, swap(): return lax.ppermute(value, axis, [(i, i ^ bit) for i in range(size)])  3.89 us
    pallas_call x1, Pallas kernels, pick_panels(): pl.pallas_call(pick_kernel, name='pick_panels', out_shape=(panel, panel),...  0.96 us
    pallas_call x5, Pallas kernels, local_call(): pl.pallas_call(kernel, name=name, out_shape=out_shape, in_specs=[vmem] *...  0.85 us
    pallas_call x1, Pallas kernels, graph_part(): pl.pallas_call(functools.partial(graph_kernel, len(panels)), name='graph_...  0.75 us
  transfers between devices with their start and end apart: 7, of which 6 were waited for; matrix products, arithmetic and copies ran while one was open for 0% of the time, Pallas kernels for 14%

profile of v2, /device:TPU:0, one launch (start us, length us, event | category | flops | bytes accessed | tf_op | source)
XLA Modules:
  0.0 29.7 jit_solution(3382579981599959340)
XLA Ops:
  0.0 0.0 copy-start
  0.0 0.0 copy-start.1
  0.0 1.0 %pick_panels.1 = (bf16[128,256]{1,0:T(8,128)(2,1)S(1)}, bf16[128,256]{1,0:T(8,128)(2,1)S(1)}) custom-call(s32[2]{0:T(128)} %bitcast.15, bf16[256,256]{1,0:T(8,128)(2,1)} %bitcast.13), custom_call_target="tpu_custom_call" | custom-call | tf_op jit(solution)/shard_map/pick_panels/pallas_call | solution.py:141
  1.0 3.0 %collective-permute-start = (bf16[128,256]{1,0:T(8,128)(2,1)S(1)}, bf16[128,256]{1,0:T(8,128)(2,1)S(1)}, u32[]{:S(2)}, u32[]{:S(2)}) collective-permute-start(bf16[128,256]{1,0:T(8,128)(2,1)S(1)} %get-tuple-element.22), channel_id=1, source_target_pairs={{0,1},{1,0},{2,3},{3,2},{4,5},{5,4},{6,7},{7,6},{8,9},{9,8},{10,11... | collective-permute-start | bytes 196616 | tf_op jit(solution)/shard_map/ppermute | solution.py:275
  4.6 4.3 %rating_part.1 = (f32[256,256]{1,0:T(8,128)S(1)}, bf16[16,256]{1,0:T(8,128)(2,1)S(1)}) custom-call(s32[64]{0:T(128)} %bitcast.16, s32[64]{0:T(128)} %bitcast.17, s32[1]{0:T(128)} %bitcast.9.count_hbm, bf16[2048,256]{1,0:T(8,128)(2,1)} %users_hbm.1, bf16[256,256]{1,0:T(8,128)(2,1)} %bitcast.14, bf16[64,128,128]{2,1,0:T(8,128)(2,1)} %bitcast.12), custom_call_target="tpu_custom_call" | custom-call | flops 400000000 | bytes 4000000 | tf_op jit(solution)/shard_map/rating_part/pallas_call | solution.py:96
  8.9 0.0 collective-permute-done.refs_1_
  8.9 0.0 copy-done
  8.9 0.0 copy-done.1
  8.9 0.7 %graph_part.1 = (f32[8,16,256]{2,1,0:T(8,128)S(1)}, f32[8,16,256]{2,1,0:T(8,128)S(1)}) custom-call(s32[2]{0:T(128)S(1)} %bitcast.11, f32[256,256]{1,0:T(8,128)S(1)} %get-tuple-element.20.grad, bf16[2,128,128]{2,1,0:T(8,128)(2,1)S(1)} %bitcast.10, bf16[128,256]{1,0:T(8,128)(2,1)S(1)} %get-tuple-element.21.refs_0_, ...), custom_call_target="tpu_custom_call" | custom-call | tf_op jit(solution)/shard_map/graph_part/pallas_call | solution.py:200
  9.7 0.1 collective-permute-start.1
  9.8 1.3 %collective-permute-done.1.received = f32[8,16,256]{2,1,0:T(8,128)S(1)} collective-permute-done((f32[8,16,256]{2,1,0:T(8,128)S(1)}, f32[8,16,256]{2,1,0:T(8,128)S(1)}, u32[]{:S(2)}, u32[]{:S(2)}) %collective-permute-start.1) | collective-permute-done | bytes 131104 | tf_op jit(solution)/shard_map/ppermute | solution.py:275
  11.1 1.6 %collective-permute-start.2 = (bf16[12,16,256]{2,1,0:T(8,128)(2,1)S(1)}, bf16[12,16,256]{2,1,0:T(8,128)(2,1)S(1)}, u32[]{:S(2)}, u32[]{:S(2)}) collective-permute-start(bf16[12,16,256]{2,1,0:T(8,128)(2,1)S(1)} %get-tuple-element.26), channel_id=1, source_target_pairs={{0,6},{2,8},{4,14},{6,0},{8,2},{10,12},{12,10},{14,4},{16,26},{18,... | collective-permute-start | bytes 294920 | tf_op jit(solution)/shard_map/ppermute | solution.py:280
  12.7 2.5 %collective-permute-done.2.received = bf16[12,16,256]{2,1,0:T(8,128)(2,1)S(1)} collective-permute-done((bf16[12,16,256]{2,1,0:T(8,128)(2,1)S(1)}, bf16[12,16,256]{2,1,0:T(8,128)(2,1)S(1)}, u32[]{:S(2)}, u32[]{:S(2)}) %collective-permute-start.2) | collective-permute-done | bytes 98336 | tf_op jit(solution)/shard_map/ppermute | solution.py:280
  15.3 1.7 %collective-permute-start.3 = (bf16[10,16,256]{2,1,0:T(8,128)(2,1)S(1)}, bf16[10,16,256]{2,1,0:T(8,128)(2,1)S(1)}, u32[]{:S(2)}, u32[]{:S(2)}) collective-permute-start(bf16[10,16,256]{2,1,0:T(8,128)(2,1)S(1)} %get-tuple-element.28), channel_id=1, source_target_pairs={{0,10},{2,16},{4,22},{6,12},{8,26},{10,0},{12,6},{14,28},{16,2},{1... | collective-permute-start | bytes 245768 | tf_op jit(solution)/shard_map/ppermute | solution.py:280
  16.9 2.5 %collective-permute-done.3.received = bf16[10,16,256]{2,1,0:T(8,128)(2,1)S(1)} collective-permute-done((bf16[10,16,256]{2,1,0:T(8,128)(2,1)S(1)}, bf16[10,16,256]{2,1,0:T(8,128)(2,1)S(1)}, u32[]{:S(2)}, u32[]{:S(2)}) %collective-permute-start.3) | collective-permute-done | bytes 81952 | tf_op jit(solution)/shard_map/ppermute | solution.py:280
  19.5 3.1 %collective-permute-start.4 = (bf16[9,16,256]{2,1,0:T(8,128)(2,1)S(1)}, bf16[9,16,256]{2,1,0:T(8,128)(2,1)S(1)}, u32[]{:S(2)}, u32[]{:S(2)}) collective-permute-start(bf16[9,16,256]{2,1,0:T(8,128)(2,1)S(1)} %get-tuple-element.30), channel_id=1, source_target_pairs={{0,18},{2,4},{4,2},{6,20},{8,14},{10,24},{12,30},{14,8},{16,22},{1... | collective-permute-start | bytes 221192 | tf_op jit(solution)/shard_map/ppermute | solution.py:280
  22.6 2.0 %collective-permute-done.4.received = bf16[9,16,256]{2,1,0:T(8,128)(2,1)S(1)} collective-permute-done((bf16[9,16,256]{2,1,0:T(8,128)(2,1)S(1)}, bf16[9,16,256]{2,1,0:T(8,128)(2,1)S(1)}, u32[]{:S(2)}, u32[]{:S(2)}) %collective-permute-start.4) | collective-permute-done | bytes 73760 | tf_op jit(solution)/shard_map/ppermute | solution.py:280
  24.7 0.1 collective-permute-start.5
  24.8 1.2 %collective-permute-done.5 = f32[8,128]{1,0:T(8,128)S(1)} collective-permute-done((f32[8,128]{1,0:T(8,128)S(1)}, f32[8,128]{1,0:T(8,128)S(1)}, u32[]{:S(2)}, u32[]{:S(2)}) %collective-permute-start.5) | collective-permute-done | bytes 4128 | tf_op jit(solution)/shard_map/ppermute | solution.py:275
  25.9 0.7 %collective-permute-start.6 = (f32[8,128]{1,0:T(8,128)S(1)}, f32[8,128]{1,0:T(8,128)S(1)}, u32[]{:S(2)}, u32[]{:S(2)}) collective-permute-start(f32[8,128]{1,0:T(8,128)S(1)} %add.3.squares), channel_id=1, source_target_pairs={{0,3},{1,2},{2,1},{3,0},{4,7},{5,6},{6,5},{7,4},{8,11},{9,10},{10,... | collective-permute-start | bytes 12296 | tf_op jit(solution)/shard_map/ppermute | solution.py:275
  26.7 2.3 %collective-permute-done.6.more = f32[8,128]{1,0:T(8,128)S(1)} collective-permute-done((f32[8,128]{1,0:T(8,128)S(1)}, f32[8,128]{1,0:T(8,128)S(1)}, u32[]{:S(2)}, u32[]{:S(2)}) %collective-permute-start.6) | collective-permute-done | bytes 4128 | tf_op jit(solution)/shard_map/ppermute | solution.py:275
  29.0 0.7 %update.1 = f32[16,256]{1,0:T(8,128)} custom-call(bf16[16,256]{1,0:T(8,128)(2,1)S(1)} %get-tuple-element.19.mine, f32[16,256]{1,0:T(8,128)S(1)} %get-tuple-element.31.own, f32[8,128]{1,0:T(8,128)S(1)} %add.3.squares, f32[8,128]{1,0:T(8,128)S(1)} %collective-permute-done.6.more), custom_call_target="tpu_custom_call" | custom-call | tf_op jit(solution)/shard_map/update/pallas_call | solution.py:261
  (5 shorter events, 0.1 us)
Async XLA Ops:
  0.0 8.9 %copy-start = (bf16[1,1,2,128,128]{4,3,2,1,0:T(8,128)(2,1)S(1)}, bf16[1,1,2,128,128]{4,3,2,1,0:T(8,128)(2,1)}, u32[]{:S(2)}) copy-start(bf16[1,1,2,128,128]{4,3,2,1,0:T(8,128)(2,1)} %param.17) | copy-start | bytes 196612
  0.0 8.9 %copy-start.1 = (s32[1,1,2]{2,1,0:T(1,128)S(1)}, s32[1,1,2]{2,1,0:T(1,128)}, u32[]{:S(2)}) copy-start(s32[1,1,2]{2,1,0:T(1,128)} %param.16) | copy-start | bytes 28
  1.0 7.9 %collective-permute-start = (bf16[128,256]{1,0:T(8,128)(2,1)S(1)}, bf16[128,256]{1,0:T(8,128)(2,1)S(1)}, u32[]{:S(2)}, u32[]{:S(2)}) collective-permute-start(bf16[128,256]{1,0:T(8,128)(2,1)S(1)} %get-tuple-element.22), channel_id=1, source_target_pairs={{0,1},{1,0},{2,3},{3,2},{4,5},{5,4},{6,7},{7,6},{8,9},{9,8},{10,11... | collective-permute-start | bytes 196616 | tf_op jit(solution)/shard_map/ppermute | solution.py:275
  9.7 1.4 %collective-permute-start.1 = (f32[8,16,256]{2,1,0:T(8,128)S(1)}, f32[8,16,256]{2,1,0:T(8,128)S(1)}, u32[]{:S(2)}, u32[]{:S(2)}) collective-permute-start(f32[8,16,256]{2,1,0:T(8,128)S(1)} %get-tuple-element.24), channel_id=1, source_target_pairs={{0,2},{2,0},{4,6},{6,4},{8,10},{10,8},{12,14},{14,12},{16,18},{18,... | collective-permute-start | bytes 393224 | tf_op jit(solution)/shard_map/ppermute | solution.py:275
  11.1 4.1 %collective-permute-start.2 = (bf16[12,16,256]{2,1,0:T(8,128)(2,1)S(1)}, bf16[12,16,256]{2,1,0:T(8,128)(2,1)S(1)}, u32[]{:S(2)}, u32[]{:S(2)}) collective-permute-start(bf16[12,16,256]{2,1,0:T(8,128)(2,1)S(1)} %get-tuple-element.26), channel_id=1, source_target_pairs={{0,6},{2,8},{4,14},{6,0},{8,2},{10,12},{12,10},{14,4},{16,26},{18,... | collective-permute-start | bytes 294920 | tf_op jit(solution)/shard_map/ppermute | solution.py:280
  15.3 4.2 %collective-permute-start.3 = (bf16[10,16,256]{2,1,0:T(8,128)(2,1)S(1)}, bf16[10,16,256]{2,1,0:T(8,128)(2,1)S(1)}, u32[]{:S(2)}, u32[]{:S(2)}) collective-permute-start(bf16[10,16,256]{2,1,0:T(8,128)(2,1)S(1)} %get-tuple-element.28), channel_id=1, source_target_pairs={{0,10},{2,16},{4,22},{6,12},{8,26},{10,0},{12,6},{14,28},{16,2},{1... | collective-permute-start | bytes 245768 | tf_op jit(solution)/shard_map/ppermute | solution.py:280
  19.5 5.2 %collective-permute-start.4 = (bf16[9,16,256]{2,1,0:T(8,128)(2,1)S(1)}, bf16[9,16,256]{2,1,0:T(8,128)(2,1)S(1)}, u32[]{:S(2)}, u32[]{:S(2)}) collective-permute-start(bf16[9,16,256]{2,1,0:T(8,128)(2,1)S(1)} %get-tuple-element.30), channel_id=1, source_target_pairs={{0,18},{2,4},{4,2},{6,20},{8,14},{10,24},{12,30},{14,8},{16,22},{1... | collective-permute-start | bytes 221192 | tf_op jit(solution)/shard_map/ppermute | solution.py:280
  24.7 1.2 %collective-permute-start.5 = (f32[8,128]{1,0:T(8,128)S(1)}, f32[8,128]{1,0:T(8,128)S(1)}, u32[]{:S(2)}, u32[]{:S(2)}) collective-permute-start(f32[8,128]{1,0:T(8,128)S(1)} %get-tuple-element.32), channel_id=1, source_target_pairs={{0,2},{2,0},{4,6},{6,4},{8,10},{10,8},{12,14},{14,12},{16,18},{18,... | collective-permute-start | bytes 12296 | tf_op jit(solution)/shard_map/ppermute | solution.py:275
  25.9 3.0 %collective-permute-start.6 = (f32[8,128]{1,0:T(8,128)S(1)}, f32[8,128]{1,0:T(8,128)S(1)}, u32[]{:S(2)}, u32[]{:S(2)}) collective-permute-start(f32[8,128]{1,0:T(8,128)S(1)} %add.3.squares), channel_id=1, source_target_pairs={{0,3},{1,2},{2,1},{3,0},{4,7},{5,6},{6,5},{7,4},{8,11},{9,10},{10,... | collective-permute-start | bytes 12296 | tf_op jit(solution)/shard_map/ppermute | solution.py:275

commit v3 on v2

--- a/solution.py
+++ b/solution.py
@@ -9,7 +9,7 @@
 
 F32 = jnp.float32
 BF16 = jnp.bfloat16
-CHUNKS = 8
+UNROLL = 4
 SMALL = 4 * 1024 * 1024
 
 
@@ -22,104 +22,92 @@
 
 
 def rating_kernel(
-    user_idx_hbm, item_idx_hbm, count_hbm, users_hbm, items_hbm, ratings_hbm, grad_ref, mine_ref,
-    user_idx, item_idx, count, users, items, ratings, users_t, pred, err, sem_s, sem_u, sem_i, sem_r,
+    user_idx_hbm, item_idx_hbm, target_hbm, count, users, items, ratings, grad_ref, mine_ref, hit_ref,
+    user_idx, item_idx, target, items_t, pred, err, sem_s,
 ):
     n_tiles, tile = ratings.shape[0], ratings.shape[1]
-    n_user = users.shape[0] // tile
     n_item = items.shape[0] // tile
-    width = n_tiles // CHUNKS
     scalars = [
         pltpu.make_async_copy(source, target, sem_s.at[n])
-        for n, (source, target) in enumerate(((count_hbm, count), (user_idx_hbm, user_idx), (item_idx_hbm, item_idx)))
+        for n, (source, target) in enumerate(((target_hbm, target), (user_idx_hbm, user_idx), (item_idx_hbm, item_idx)))
     ]
     for copy in scalars:
         copy.start()
-    copy_u = pltpu.make_async_copy(users_hbm, users, sem_u)
-    copy_i = pltpu.make_async_copy(items_hbm, items, sem_i)
-    copy_i.start()
-    copy_u.start()
+    own = mine_ref.shape[0]
+    mine_ref[...] = items[pl.ds(pl.multiple_of(lax.axis_index("rows") * own, own), own), :]
+    for j in range(n_item):
+        items_t[j] = items[j * tile:(j + 1) * tile, :].T
+    for first in range(0, n_item, 2):
+        both = range(first, min(first + 2, n_item))
+        whole = dot(users[...], jnp.concatenate([items_t[j] for j in both], axis=1), ((1,), (0,)))
+        for n, j in enumerate(both):
+            pred[j] = whole[:, n * tile:(n + 1) * tile]
+
+    @pl.loop(0, users.shape[0] // tile)
+    def _(c):
+        for j in range(n_item):
+            err[j, pl.ds(pl.multiple_of(c * tile, tile), tile), :] = jnp.zeros((tile, tile), F32)
+
     for copy in scalars:
         copy.wait()
-    live = count[0]
-
-    def chunk_copy(c):
-        span = pl.ds(c * width, width)
-        return pltpu.make_async_copy(ratings_hbm.at[span], ratings.at[span], sem_r.at[c])
-
-    for c in range(CHUNKS):
-        @pl.when(c * width < live)
-        def _():
-            chunk_copy(c).start()
-
-    err[...] = jnp.zeros_like(err)
-    copy_i.wait()
-    rows = mine_ref.shape[0]
-    mine_ref[...] = items[pl.ds(pl.multiple_of(lax.axis_index("rows") * rows, rows), rows), :]
-    copy_u.wait()
-    for u in range(n_user):
-        rows = pl.ds(u * tile, tile)
-        block = users[rows, :]
-        users_t[:, rows] = block.T
-        whole = dot(block, items[...], ((1,), (1,)))
+    live = count[0, 0]
+    for k in range(hit_ref.shape[0]):
         for j in range(n_item):
-            pred[u * n_item + j] = whole[:, j * tile:(j + 1) * tile]
-
-    def step(t, carry):
-        place = user_idx[t] * n_item + item_idx[t]
-        diff = pred[place] - ratings[t].astype(F32)
-        err[place] += diff.astype(BF16).astype(F32)
-        return carry
-
-    for c in range(CHUNKS):
-        @pl.when(c * width < live)
-        def _():
-            chunk_copy(c).wait()
-            lax.fori_loop(c * width, jnp.minimum(live, (c + 1) * width), step, 0)
+            hit_ref[k, j] = jnp.full((8, 128), (target[k] == j).astype(F32))
+
+    def add_tile(t):
+        j = item_idx[t]
+        rows = pl.ds(pl.multiple_of(user_idx[t] * tile, tile), tile)
+        diff = pred[j, rows, :] - ratings[t].astype(F32)
+        err[j, rows, :] += diff.astype(BF16).astype(F32)
+
+    groups = lax.div(live, UNROLL)
+
+    @pl.loop(0, groups)
+    def _(g):
+        for k in range(UNROLL):
+            add_tile(g * UNROLL + k)
+
+    @pl.loop(groups * UNROLL, live)
+    def _(t):
+        add_tile(t)
 
     for j in range(n_item):
-        total = jnp.zeros((users.shape[1], tile), F32)
-        for u in range(n_user):
-            left = users_t[:, u * tile:(u + 1) * tile]
-            whole = err[u * n_item + j]
-            high = whole.astype(BF16)
-            low = (whole - high.astype(F32)).astype(BF16)
-            total += dot(left, high, ((1,), (0,))) + dot(left, low, ((1,), (0,)))
-        grad_ref[j * tile:(j + 1) * tile, :] = total.T
-
-
-def rating_part(user_idx, item_idx, count, users, items, ratings, own_rows):
-    n_tiles, tile, unused = ratings.shape
-    n_pairs = (users.shape[0] // tile) * (items.shape[0] // tile)
+        whole = err[j]
+        high = whole.astype(BF16)
+        low = (whole - high.astype(F32)).astype(BF16)
+        grad_ref[j * tile:(j + 1) * tile, :] = dot(high, users[...], ((0,), (0,))) + dot(low, users[...], ((0,), (0,)))
+
+
+def rating_part(user_idx, item_idx, count, target, users, items, ratings, own_rows):
+    tile = ratings.shape[1]
+    n_item = items.shape[0] // tile
+    smem = pl.BlockSpec(memory_space=pltpu.SMEM)
     hbm = pl.BlockSpec(memory_space=pltpu.HBM)
     vmem = pl.BlockSpec(memory_space=pltpu.VMEM)
+    sums = pltpu.VMEM((n_item, users.shape[0], tile), F32)
+    limit = 16 if n_item <= 2 else 56
     return pl.pallas_call(
         rating_kernel,
         name="rating_part",
         out_shape=(
             jax.ShapeDtypeStruct(items.shape, F32),
             jax.ShapeDtypeStruct((own_rows, items.shape[1]), BF16),
+            jax.ShapeDtypeStruct((target.shape[0], n_item, 8, 128), F32),
         ),
-        in_specs=[hbm] * 6,
-        out_specs=(vmem, vmem),
+        in_specs=[hbm] * 3 + [smem] + [vmem] * 3,
+        out_specs=(vmem, vmem, vmem),
         scratch_shapes=[
             pltpu.SMEM(user_idx.shape, jnp.int32),
             pltpu.SMEM(item_idx.shape, jnp.int32),
-            pltpu.SMEM(count.shape, jnp.int32),
-            pltpu.VMEM(users.shape, BF16),
-            pltpu.VMEM(items.shape, BF16),
-            pltpu.VMEM(ratings.shape, BF16),
-            pltpu.VMEM(users.shape[::-1], BF16),
-            pltpu.VMEM((n_pairs, tile, tile), F32),
-            pltpu.VMEM((n_pairs, tile, tile), F32),
+            pltpu.SMEM(target.shape, jnp.int32),
+            pltpu.VMEM((n_item, items.shape[1], tile), BF16),
+            sums,
+            sums,
             pltpu.SemaphoreType.DMA((3,)),
-            pltpu.SemaphoreType.DMA,
-            pltpu.SemaphoreType.DMA,
-            pltpu.SemaphoreType.DMA((CHUNKS,)),
         ],
-        compiler_params=pltpu.CompilerParams(vmem_limit_bytes=48 * 1024 * 1024),
-        cost_estimate=pl.CostEstimate(flops=4 * 10**8, bytes_accessed=4 * 10**6, transcendentals=0),
-    )(*in_hbm(user_idx, item_idx), count, *in_hbm(users, items, ratings))
+        compiler_params=pltpu.CompilerParams(vmem_limit_bytes=limit * 1024 * 1024),
+    )(*in_hbm(user_idx, item_idx, target), count, users, items, ratings)
 
 
 def pick_kernel(send_list_hbm, items_hbm, kept, sent, send_list, items, sem_s, sem):
@@ -151,6 +139,7 @@
             pltpu.SemaphoreType.DMA,
         ],
         compiler_params=pltpu.CompilerParams(vmem_limit_bytes=SMALL),
+        cost_estimate=pl.CostEstimate(flops=10**10, bytes_accessed=3 * 10**7, transcendentals=0),
     )(*in_hbm(send_list, items))
 
 
@@ -168,7 +157,7 @@
     return value | parity(value)
 
 
-def graph_kernel(n_panels, target, grad, similarity, *refs):
+def graph_kernel(n_panels, hit, grad, similarity, *refs):
     panels, outs, total = refs[:n_panels], refs[n_panels:-1], refs[-1]
     blocks, tile, unused = similarity.shape
     total[...] = grad[...]
@@ -176,8 +165,10 @@
     for k in range(blocks):
         block = k if n_panels == 1 else k ^ col
         panel = panels[0][k] if n_panels == 1 else panels[k][...]
-        rows = pl.ds(pl.multiple_of(target[block] * tile, tile), tile)
-        total[rows, :] += dot(similarity[block], panel, ((1,), (0,)))
+        part = dot(similarity[block], panel, ((1,), (0,)))
+        for j in range(total.shape[0] // tile):
+            chosen = jnp.broadcast_to(hit[block, j][:1, :1], part.shape) > 0
+            total[j * tile:(j + 1) * tile, :] += jnp.where(chosen, part, 0)
     me = lax.axis_index("rows")
     if len(outs) == 1:
         outs[0][...] = total[...]
@@ -194,18 +185,17 @@
             out[q] = total[pl.ds(pl.multiple_of(block * own, own), own), :]
 
 
-def graph_part(target, grad, similarity, panels, out_shape):
-    smem = pl.BlockSpec(memory_space=pltpu.SMEM)
+def graph_part(hit, grad, similarity, panels, out_shape):
     vmem = pl.BlockSpec(memory_space=pltpu.VMEM)
     return pl.pallas_call(
         functools.partial(graph_kernel, len(panels)),
         name="graph_part",
         out_shape=out_shape,
-        in_specs=[smem] + [vmem] * (2 + len(panels)),
+        in_specs=[vmem] * (3 + len(panels)),
         out_specs=jax.tree.map(lambda unused: vmem, out_shape),
         scratch_shapes=[pltpu.VMEM(grad.shape, F32)],
         compiler_params=pltpu.CompilerParams(vmem_limit_bytes=SMALL if grad.size <= 2**16 else 32 * 1024 * 1024),
-    )(target, grad, similarity, *panels)
+    )(hit, grad, similarity, *panels)
 
 
 def split_places(half, bit):
@@ -296,13 +286,14 @@
         incoming = lax.all_to_all(panels[send_list[0, 0]], "cols", 0, 0, tiled=True)
         incoming = (incoming.reshape(blocks, tile, rank),)
     own_rows = icount // n_rows
-    grad, mine = rating_part(
-        tile_users.reshape(-1), tile_items.reshape(-1), tile_count.reshape(-1), users, items[0], ratings[0, 0], own_rows
+    target = block_target.reshape(-1)
+    grad, mine, hit = rating_part(
+        tile_users.reshape(-1), tile_items.reshape(-1), tile_count, target, users, items[0],
+        ratings[0, 0], own_rows,
     )
     entries = n_cols * icount * rank
-    target = block_target[0, 0]
     if n_rows & (n_rows - 1) or n_rows < 4 or n_cols != 2 or own_rows % 16:
-        flat = graph_part(target, grad, similarity[0, 0], incoming, (jax.ShapeDtypeStruct((icount, rank), F32),))[0]
+        flat = graph_part(hit, grad, similarity[0, 0], incoming, (jax.ShapeDtypeStruct((icount, rank), F32),))[0]
         owned = lax.psum_scatter(flat, "rows", scatter_dimension=0, tiled=True)
         squares = lax.psum(jnp.sum(owned * owned), ("rows", "cols"))
         return (mine.astype(F32) - 0.5 * owned / jnp.sqrt(squares / entries + 1e-06))[None]
@@ -313,7 +304,7 @@
     def payload(bit):
         return jax.ShapeDtypeStruct((half + len(split_places(half, bit)), own_rows, rank), BF16)
 
-    keep, give = graph_part(target, grad, similarity[0, 0], incoming, (block, block))
+    keep, give = graph_part(hit, grad, similarity[0, 0], incoming, (block, block))
     total, sent = local_call(first_kernel, "add_core", (keep, swap(give, "rows", 1)), (block, payload(1)))
     n_hops = len(hops(n_rows, 0))
     for b in range(n_hops - 1):

time: 29.9 us -> 27.2 us (0.910)
  Pallas kernels: 6.84 us -> 3.99 us
  starting transfers between devices: 10.2 us -> 11.5 us
  waiting for transfers between devices: 11.9 us -> 10.6 us
    pallas_call x1, Pallas kernels: 4.28 us -> 1.86 us  [rating_part(): pl.pallas_call(rating_kernel, name='rating_part', out_shape=(jax.ShapeDty...]
    ppermute x4, starting transfers between devices: 3.89 us -> 4.83 us  [swap(): return lax.ppermute(value, axis, [(i, i ^ bit) for i in range(size)])]
    ppermute x4, waiting for transfers between devices: 4.77 us -> 3.84 us  [swap(): return lax.ppermute(value, axis, [(i, i ^ bit) for i in range(size)])]
    pallas_call x1, Pallas kernels: 0.75 us -> 0.19 us  [graph_part(): pl.pallas_call(functools.partial(graph_kernel, len(panels)), name='graph_...]
    ppermute x3, waiting for transfers between devices: 7.13 us -> 6.77 us  [hop(): lax.ppermute(value, 'rows', [(i, i ^ 1 ^ hops(size, parity(i))[b]) for i...]
    ppermute x3, starting transfers between devices: 6.35 us -> 6.65 us  [hop(): lax.ppermute(value, 'rows', [(i, i ^ 1 ^ hops(size, parity(i))[b]) for i...]
  transfers between devices with their start and end apart: 7 -> 7, of which waited for: 6 -> 6; matrix products, arithmetic and copies ran while one was open for 0% -> 0% of each run, Pallas kernels for 14% -> 7%
where the time goes in v3:
time: 27.2 us; the launch traced here: 26.8 us
  starting transfers between devices  11.5 us (42%)
  waiting for transfers between devices  10.6 us (39%)
  Pallas kernels  3.99 us (15%)
  between operations  0.75 us (3%)
    ppermute x3, waiting for transfers between devices, hop(): lax.ppermute(value, 'rows', [(i, i ^ 1 ^ hops(size, parity(i))[b]) for i...  6.77 us
    ppermute x3, starting transfers between devices, hop(): lax.ppermute(value, 'rows', [(i, i ^ 1 ^ hops(size, parity(i))[b]) for i...  6.65 us
    ppermute x4, starting transfers between devices, swap(): return lax.ppermute(value, axis, [(i, i ^ bit) for i in range(size)])  4.83 us
    ppermute x4, waiting for transfers between devices, swap(): return lax.ppermute(value, axis, [(i, i ^ bit) for i in range(size)])  3.84 us
    pallas_call x1, Pallas kernels, rating_part(): pl.pallas_call(rating_kernel, name='rating_part', out_shape=(jax.ShapeDty...  1.86 us
    pallas_call x1, Pallas kernels, pick_panels(): pl.pallas_call(pick_kernel, name='pick_panels', out_shape=(panel, panel),...  1.08 us
    pallas_call x5, Pallas kernels, local_call(): pl.pallas_call(kernel, name=name, out_shape=out_shape, in_specs=[vmem] *...  0.85 us
  transfers between devices with their start and end apart: 7, of which 6 were waited for; matrix products, arithmetic and copies ran while one was open for 0% of the time, Pallas kernels for 7%

profile of v3, /device:TPU:0, one launch (start us, length us, event | category | flops | bytes accessed | tf_op | source)
XLA Modules:
  0.0 26.8 jit_solution(5965269520058761762)
XLA Ops:
  0.0 0.0 copy-start
  0.0 0.0 copy-start.1
  0.0 0.0 copy-start.2
  0.0 1.1 %pick_panels.1 = (bf16[128,256]{1,0:T(8,128)(2,1)S(1)}, bf16[128,256]{1,0:T(8,128)(2,1)S(1)}) custom-call(s32[2]{0:T(128)} %bitcast.15, bf16[256,256]{1,0:T(8,128)(2,1)} %bitcast.9), custom_call_target="tpu_custom_call" | custom-call | flops 10000000000 | bytes 30000000 | tf_op jit(solution)/shard_map/pick_panels/pallas_call | solution.py:129
  1.1 0.0 copy-start.3
  1.1 3.0 %collective-permute-start = (bf16[128,256]{1,0:T(8,128)(2,1)S(1)}, bf16[128,256]{1,0:T(8,128)(2,1)S(1)}, u32[]{:S(2)}, u32[]{:S(2)}) collective-permute-start(bf16[128,256]{1,0:T(8,128)(2,1)S(1)} %get-tuple-element.24), channel_id=1, source_target_pairs={{0,1},{1,0},{2,3},{3,2},{4,5},{5,4},{6,7},{7,6},{8,9},{9,8},{10,11... | collective-permute-start | bytes 196616 | tf_op jit(solution)/shard_map/ppermute | solution.py:265
  4.8 0.0 copy-done
  4.8 0.0 copy-done.1
  4.8 0.0 copy-done.2
  4.8 1.9 %rating_part.1 = (f32[256,256]{1,0:T(8,128)S(1)}, bf16[16,256]{1,0:T(8,128)(2,1)S(1)}, f32[2,2,8,128]{3,2,1,0:T(8,128)S(1)}) custom-call(s32[64]{0:T(128)} %bitcast.12, s32[64]{0:T(128)} %bitcast.13, s32[2]{0:T(128)} %bitcast.14, s32[1,1]{1,0:T(1,128)S(6)} %copy.10.count, bf16[2048,256]{1,0:T(8,128)(2,1)S(1)} %copy-done.1, bf16[256,256]{1,0:T(8,128)(2,1)S(1)} %bitcast.10, ...), custom_call_target="tpu_custom_call" | custom-call | tf_op jit(solution)/shard_map/rating_part/pallas_call | solution.py:90
  6.7 0.0 collective-permute-done.refs_1_
  6.7 0.0 copy-done.3
  6.7 0.2 graph_part.1
  6.9 0.1 collective-permute-start.1
  7.0 1.3 %collective-permute-done.1.received = f32[8,16,256]{2,1,0:T(8,128)S(1)} collective-permute-done((f32[8,16,256]{2,1,0:T(8,128)S(1)}, f32[8,16,256]{2,1,0:T(8,128)S(1)}, u32[]{:S(2)}, u32[]{:S(2)}) %collective-permute-start.1) | collective-permute-done | bytes 131104 | tf_op jit(solution)/shard_map/ppermute | solution.py:265
  8.3 1.7 %collective-permute-start.2 = (bf16[12,16,256]{2,1,0:T(8,128)(2,1)S(1)}, bf16[12,16,256]{2,1,0:T(8,128)(2,1)S(1)}, u32[]{:S(2)}, u32[]{:S(2)}) collective-permute-start(bf16[12,16,256]{2,1,0:T(8,128)(2,1)S(1)} %get-tuple-element.28), channel_id=1, source_target_pairs={{0,6},{2,8},{4,14},{6,0},{8,2},{10,12},{12,10},{14,4},{16,26},{18,... | collective-permute-start | bytes 294920 | tf_op jit(solution)/shard_map/ppermute | solution.py:270
  10.0 2.4 %collective-permute-done.2.received = bf16[12,16,256]{2,1,0:T(8,128)(2,1)S(1)} collective-permute-done((bf16[12,16,256]{2,1,0:T(8,128)(2,1)S(1)}, bf16[12,16,256]{2,1,0:T(8,128)(2,1)S(1)}, u32[]{:S(2)}, u32[]{:S(2)}) %collective-permute-start.2) | collective-permute-done | bytes 98336 | tf_op jit(solution)/shard_map/ppermute | solution.py:270
  12.5 1.6 %collective-permute-start.3 = (bf16[10,16,256]{2,1,0:T(8,128)(2,1)S(1)}, bf16[10,16,256]{2,1,0:T(8,128)(2,1)S(1)}, u32[]{:S(2)}, u32[]{:S(2)}) collective-permute-start(bf16[10,16,256]{2,1,0:T(8,128)(2,1)S(1)} %get-tuple-element.30), channel_id=1, source_target_pairs={{0,10},{2,16},{4,22},{6,12},{8,26},{10,0},{12,6},{14,28},{16,2},{1... | collective-permute-start | bytes 245768 | tf_op jit(solution)/shard_map/ppermute | solution.py:270
  14.1 2.3 %collective-permute-done.3.received = bf16[10,16,256]{2,1,0:T(8,128)(2,1)S(1)} collective-permute-done((bf16[10,16,256]{2,1,0:T(8,128)(2,1)S(1)}, bf16[10,16,256]{2,1,0:T(8,128)(2,1)S(1)}, u32[]{:S(2)}, u32[]{:S(2)}) %collective-permute-start.3) | collective-permute-done | bytes 81952 | tf_op jit(solution)/shard_map/ppermute | solution.py:270
  16.4 3.3 %collective-permute-start.4 = (bf16[9,16,256]{2,1,0:T(8,128)(2,1)S(1)}, bf16[9,16,256]{2,1,0:T(8,128)(2,1)S(1)}, u32[]{:S(2)}, u32[]{:S(2)}) collective-permute-start(bf16[9,16,256]{2,1,0:T(8,128)(2,1)S(1)} %get-tuple-element.32), channel_id=1, source_target_pairs={{0,18},{2,4},{4,2},{6,20},{8,14},{10,24},{12,30},{14,8},{16,22},{1... | collective-permute-start | bytes 221192 | tf_op jit(solution)/shard_map/ppermute | solution.py:270
  19.8 2.0 %collective-permute-done.4.received = bf16[9,16,256]{2,1,0:T(8,128)(2,1)S(1)} collective-permute-done((bf16[9,16,256]{2,1,0:T(8,128)(2,1)S(1)}, bf16[9,16,256]{2,1,0:T(8,128)(2,1)S(1)}, u32[]{:S(2)}, u32[]{:S(2)}) %collective-permute-start.4) | collective-permute-done | bytes 73760 | tf_op jit(solution)/shard_map/ppermute | solution.py:270
  21.8 0.4 %collective-permute-start.5 = (f32[8,128]{1,0:T(8,128)S(1)}, f32[8,128]{1,0:T(8,128)S(1)}, u32[]{:S(2)}, u32[]{:S(2)}) collective-permute-start(f32[8,128]{1,0:T(8,128)S(1)} %get-tuple-element.34), channel_id=1, source_target_pairs={{0,2},{2,0},{4,6},{6,4},{8,10},{10,8},{12,14},{14,12},{16,18},{18,... | collective-permute-start | bytes 12296 | tf_op jit(solution)/shard_map/ppermute | solution.py:265
  22.2 0.8 %collective-permute-done.5 = f32[8,128]{1,0:T(8,128)S(1)} collective-permute-done((f32[8,128]{1,0:T(8,128)S(1)}, f32[8,128]{1,0:T(8,128)S(1)}, u32[]{:S(2)}, u32[]{:S(2)}) %collective-permute-start.5) | collective-permute-done | bytes 4128 | tf_op jit(solution)/shard_map/ppermute | solution.py:265
  23.1 1.4 %collective-permute-start.6 = (f32[8,128]{1,0:T(8,128)S(1)}, f32[8,128]{1,0:T(8,128)S(1)}, u32[]{:S(2)}, u32[]{:S(2)}) collective-permute-start(f32[8,128]{1,0:T(8,128)S(1)} %add.3.squares), channel_id=1, source_target_pairs={{0,3},{1,2},{2,1},{3,0},{4,7},{5,6},{6,5},{7,4},{8,11},{9,10},{10,... | collective-permute-start | bytes 12296 | tf_op jit(solution)/shard_map/ppermute | solution.py:265
  24.4 1.7 %collective-permute-done.6.more = f32[8,128]{1,0:T(8,128)S(1)} collective-permute-done((f32[8,128]{1,0:T(8,128)S(1)}, f32[8,128]{1,0:T(8,128)S(1)}, u32[]{:S(2)}, u32[]{:S(2)}) %collective-permute-start.6) | collective-permute-done | bytes 4128 | tf_op jit(solution)/shard_map/ppermute | solution.py:265
  26.1 0.7 %update.1 = f32[16,256]{1,0:T(8,128)} custom-call(bf16[16,256]{1,0:T(8,128)(2,1)S(1)} %get-tuple-element.20.mine, f32[16,256]{1,0:T(8,128)S(1)} %get-tuple-element.33.own, f32[8,128]{1,0:T(8,128)S(1)} %add.3.squares, f32[8,128]{1,0:T(8,128)S(1)} %collective-permute-done.6.more), custom_call_target="tpu_custom_call" | custom-call | tf_op jit(solution)/shard_map/update/pallas_call | solution.py:251
  (5 shorter events, 0.1 us)
Async XLA Ops:
  0.0 4.8 %copy-start = (bf16[1,1,64,128,128]{4,3,2,1,0:T(8,128)(2,1)S(1)}, bf16[1,1,64,128,128]{4,3,2,1,0:T(8,128)(2,1)}, u32[]{:S(2)}) copy-start(bf16[1,1,64,128,128]{4,3,2,1,0:T(8,128)(2,1)} %param.11) | copy-start | bytes 6291460
  0.0 4.8 %copy-start.1 = (bf16[2048,256]{1,0:T(8,128)(2,1)S(1)}, bf16[2048,256]{1,0:T(8,128)(2,1)}, u32[]{:S(2)}) copy-start(bf16[2048,256]{1,0:T(8,128)(2,1)} %users.1) | copy-start | bytes 3145732
  0.0 4.8 %copy-start.2 = (bf16[1,256,256]{2,1,0:T(8,128)(2,1)S(1)}, bf16[1,256,256]{2,1,0:T(8,128)(2,1)}, u32[]{:S(2)}) copy-start(bf16[1,256,256]{2,1,0:T(8,128)(2,1)} %param.10) | copy-start | bytes 393220
  1.1 5.6 %copy-start.3 = (bf16[1,1,2,128,128]{4,3,2,1,0:T(8,128)(2,1)S(1)}, bf16[1,1,2,128,128]{4,3,2,1,0:T(8,128)(2,1)}, u32[]{:S(2)}) copy-start(bf16[1,1,2,128,128]{4,3,2,1,0:T(8,128)(2,1)} %param.17) | copy-start | bytes 196612
  1.1 5.6 %collective-permute-start = (bf16[128,256]{1,0:T(8,128)(2,1)S(1)}, bf16[128,256]{1,0:T(8,128)(2,1)S(1)}, u32[]{:S(2)}, u32[]{:S(2)}) collective-permute-start(bf16[128,256]{1,0:T(8,128)(2,1)S(1)} %get-tuple-element.24), channel_id=1, source_target_pairs={{0,1},{1,0},{2,3},{3,2},{4,5},{5,4},{6,7},{7,6},{8,9},{9,8},{10,11... | collective-permute-start | bytes 196616 | tf_op jit(solution)/shard_map/ppermute | solution.py:265
  6.9 1.4 %collective-permute-start.1 = (f32[8,16,256]{2,1,0:T(8,128)S(1)}, f32[8,16,256]{2,1,0:T(8,128)S(1)}, u32[]{:S(2)}, u32[]{:S(2)}) collective-permute-start(f32[8,16,256]{2,1,0:T(8,128)S(1)} %get-tuple-element.26), channel_id=1, source_target_pairs={{0,2},{2,0},{4,6},{6,4},{8,10},{10,8},{12,14},{14,12},{16,18},{18,... | collective-permute-start | bytes 393224 | tf_op jit(solution)/shard_map/ppermute | solution.py:265
  8.3 4.1 %collective-permute-start.2 = (bf16[12,16,256]{2,1,0:T(8,128)(2,1)S(1)}, bf16[12,16,256]{2,1,0:T(8,128)(2,1)S(1)}, u32[]{:S(2)}, u32[]{:S(2)}) collective-permute-start(bf16[12,16,256]{2,1,0:T(8,128)(2,1)S(1)} %get-tuple-element.28), channel_id=1, source_target_pairs={{0,6},{2,8},{4,14},{6,0},{8,2},{10,12},{12,10},{14,4},{16,26},{18,... | collective-permute-start | bytes 294920 | tf_op jit(solution)/shard_map/ppermute | solution.py:270
  12.5 3.9 %collective-permute-start.3 = (bf16[10,16,256]{2,1,0:T(8,128)(2,1)S(1)}, bf16[10,16,256]{2,1,0:T(8,128)(2,1)S(1)}, u32[]{:S(2)}, u32[]{:S(2)}) collective-permute-start(bf16[10,16,256]{2,1,0:T(8,128)(2,1)S(1)} %get-tuple-element.30), channel_id=1, source_target_pairs={{0,10},{2,16},{4,22},{6,12},{8,26},{10,0},{12,6},{14,28},{16,2},{1... | collective-permute-start | bytes 245768 | tf_op jit(solution)/shard_map/ppermute | solution.py:270
  16.4 5.4 %collective-permute-start.4 = (bf16[9,16,256]{2,1,0:T(8,128)(2,1)S(1)}, bf16[9,16,256]{2,1,0:T(8,128)(2,1)S(1)}, u32[]{:S(2)}, u32[]{:S(2)}) collective-permute-start(bf16[9,16,256]{2,1,0:T(8,128)(2,1)S(1)} %get-tuple-element.32), channel_id=1, source_target_pairs={{0,18},{2,4},{4,2},{6,20},{8,14},{10,24},{12,30},{14,8},{16,22},{1... | collective-permute-start | bytes 221192 | tf_op jit(solution)/shard_map/ppermute | solution.py:270
  21.8 1.2 %collective-permute-start.5 = (f32[8,128]{1,0:T(8,128)S(1)}, f32[8,128]{1,0:T(8,128)S(1)}, u32[]{:S(2)}, u32[]{:S(2)}) collective-permute-start(f32[8,128]{1,0:T(8,128)S(1)} %get-tuple-element.34), channel_id=1, source_target_pairs={{0,2},{2,0},{4,6},{6,4},{8,10},{10,8},{12,14},{14,12},{16,18},{18,... | collective-permute-start | bytes 12296 | tf_op jit(solution)/shard_map/ppermute | solution.py:265
  23.1 3.0 %collective-permute-start.6 = (f32[8,128]{1,0:T(8,128)S(1)}, f32[8,128]{1,0:T(8,128)S(1)}, u32[]{:S(2)}, u32[]{:S(2)}) collective-permute-start(f32[8,128]{1,0:T(8,128)S(1)} %add.3.squares), channel_id=1, source_target_pairs={{0,3},{1,2},{2,1},{3,0},{4,7},{5,6},{6,5},{7,4},{8,11},{9,10},{10,... | collective-permute-start | bytes 12296 | tf_op jit(solution)/shard_map/ppermute | solution.py:265

commit v4 on v3

--- a/solution.py
+++ b/solution.py
@@ -9,7 +9,7 @@
 
 F32 = jnp.float32
 BF16 = jnp.bfloat16
-UNROLL = 4
+UNROLL = 8
 SMALL = 4 * 1024 * 1024
 
 
@@ -110,14 +110,19 @@
     )(*in_hbm(user_idx, item_idx, target), count, users, items, ratings)
 
 
-def pick_kernel(send_list_hbm, items_hbm, kept, sent, send_list, items, sem_s, sem):
+def pick_kernel(send_list_hbm, items_hbm, kept, sent, send_list, items, sem_s, sems):
+    tile = kept.shape[0]
     copy_list = pltpu.make_async_copy(send_list_hbm, send_list, sem_s)
-    copy = pltpu.make_async_copy(items_hbm, items, sem)
+    copies = []
+    for n in range(sems.shape[0]):
+        rows = pl.ds(n * tile // 2, tile // 2)
+        copies.append(pltpu.make_async_copy(items_hbm.at[rows], items.at[rows], sems.at[n]))
+    for copy in copies:
+        copy.start()
     copy_list.start()
-    copy.start()
     copy_list.wait()
-    copy.wait()
-    tile = kept.shape[0]
+    for copy in copies:
+        copy.wait()
     me = lax.axis_index("cols")
     for out, col in ((kept, me), (sent, 1 - me)):
         out[...] = items[pl.ds(pl.multiple_of(send_list[col] * tile, tile), tile), :]
@@ -136,7 +141,7 @@
             pltpu.SMEM(send_list.shape, jnp.int32),
             pltpu.VMEM(items.shape, BF16),
             pltpu.SemaphoreType.DMA,
-            pltpu.SemaphoreType.DMA,
+            pltpu.SemaphoreType.DMA((2 * items.shape[0] // tile,)),
         ],
         compiler_params=pltpu.CompilerParams(vmem_limit_bytes=SMALL),
         cost_estimate=pl.CostEstimate(flops=10**10, bytes_accessed=3 * 10**7, transcendentals=0),

time: 27.2 us -> 27.1 us (level)
  starting transfers between devices: 11.5 us -> 10.6 us
  waiting for transfers between devices: 10.6 us -> 11.4 us
    ppermute x3, starting transfers between devices: 6.65 us -> 5.76 us  [hop(): lax.ppermute(value, 'rows', [(i, i ^ 1 ^ hops(size, parity(i))[b]) for i...]
    ppermute x3, waiting for transfers between devices: 6.77 us -> 7.43 us  [hop(): lax.ppermute(value, 'rows', [(i, i ^ 1 ^ hops(size, parity(i))[b]) for i...]
  transfers between devices with their start and end apart: 7 -> 7, of which waited for: 6 -> 6; matrix products, arithmetic and copies ran while one was open for 0% -> 0% of each run, Pallas kernels for 7% -> 8%
where the time goes in v4:
time: 27.1 us; the launch traced here: 26.9 us
  waiting for transfers between devices  11.4 us (42%)
  starting transfers between devices  10.6 us (39%)
  Pallas kernels  4.17 us (15%)
  between operations  0.75 us (3%)
    ppermute x3, waiting for transfers between devices, hop(): lax.ppermute(value, 'rows', [(i, i ^ 1 ^ hops(size, parity(i))[b]) for i...  7.43 us
    ppermute x3, starting transfers between devices, hop(): lax.ppermute(value, 'rows', [(i, i ^ 1 ^ hops(size, parity(i))[b]) for i...  5.76 us
    ppermute x4, starting transfers between devices, swap(): return lax.ppermute(value, axis, [(i, i ^ bit) for i in range(size)])  4.82 us
    ppermute x4, waiting for transfers between devices, swap(): return lax.ppermute(value, axis, [(i, i ^ bit) for i in range(size)])  4 us
    pallas_call x1, Pallas kernels, rating_part(): pl.pallas_call(rating_kernel, name='rating_part', out_shape=(jax.ShapeDty...  2.12 us
    pallas_call x1, Pallas kernels, pick_panels(): pl.pallas_call(pick_kernel, name='pick_panels', out_shape=(panel, panel),...  1.01 us
    pallas_call x5, Pallas kernels, local_call(): pl.pallas_call(kernel, name=name, out_shape=out_shape, in_specs=[vmem] *...  0.85 us
  transfers between devices with their start and end apart: 7, of which 6 were waited for; matrix products, arithmetic and copies ran while one was open for 0% of the time, Pallas kernels for 8%

profile of v4, /device:TPU:0, one launch (start us, length us, event | category | flops | bytes accessed | tf_op | source)
XLA Modules:
  0.0 26.9 jit_solution(9411416487503550133)
XLA Ops:
  0.0 0.0 copy-start
  0.0 0.0 copy-start.1
  0.0 0.0 copy-start.2
  0.0 1.0 %pick_panels.1 = (bf16[128,256]{1,0:T(8,128)(2,1)S(1)}, bf16[128,256]{1,0:T(8,128)(2,1)S(1)}) custom-call(s32[2]{0:T(128)} %bitcast.15, bf16[256,256]{1,0:T(8,128)(2,1)} %bitcast.9), custom_call_target="tpu_custom_call" | custom-call | flops 10000000000 | bytes 30000000 | tf_op jit(solution)/shard_map/pick_panels/pallas_call | solution.py:134
  1.0 0.0 copy-start.3
  1.0 3.0 %collective-permute-start = (bf16[128,256]{1,0:T(8,128)(2,1)S(1)}, bf16[128,256]{1,0:T(8,128)(2,1)S(1)}, u32[]{:S(2)}, u32[]{:S(2)}) collective-permute-start(bf16[128,256]{1,0:T(8,128)(2,1)S(1)} %get-tuple-element.24), channel_id=1, source_target_pairs={{0,1},{1,0},{2,3},{3,2},{4,5},{5,4},{6,7},{7,6},{8,9},{9,8},{10,11... | collective-permute-start | bytes 196616 | tf_op jit(solution)/shard_map/ppermute | solution.py:270
  4.7 0.0 copy-done
  4.7 0.0 copy-done.1
  4.7 0.0 copy-done.2
  4.7 2.1 %rating_part.1 = (f32[256,256]{1,0:T(8,128)S(1)}, bf16[16,256]{1,0:T(8,128)(2,1)S(1)}, f32[2,2,8,128]{3,2,1,0:T(8,128)S(1)}) custom-call(s32[64]{0:T(128)} %bitcast.12, s32[64]{0:T(128)} %bitcast.13, s32[2]{0:T(128)} %bitcast.14, s32[1,1]{1,0:T(1,128)S(6)} %copy.10.count, bf16[2048,256]{1,0:T(8,128)(2,1)S(1)} %copy-done.1, bf16[256,256]{1,0:T(8,128)(2,1)S(1)} %bitcast.10, ...), custom_call_target="tpu_custom_call" | custom-call | tf_op jit(solution)/shard_map/rating_part/pallas_call | solution.py:90
  6.9 0.0 collective-permute-done.refs_1_
  6.9 0.0 copy-done.3
  6.9 0.2 graph_part.1
  7.1 0.1 collective-permute-start.1
  7.2 1.3 %collective-permute-done.1.received = f32[8,16,256]{2,1,0:T(8,128)S(1)} collective-permute-done((f32[8,16,256]{2,1,0:T(8,128)S(1)}, f32[8,16,256]{2,1,0:T(8,128)S(1)}, u32[]{:S(2)}, u32[]{:S(2)}) %collective-permute-start.1) | collective-permute-done | bytes 131104 | tf_op jit(solution)/shard_map/ppermute | solution.py:270
  8.5 1.3 %collective-permute-start.2 = (bf16[12,16,256]{2,1,0:T(8,128)(2,1)S(1)}, bf16[12,16,256]{2,1,0:T(8,128)(2,1)S(1)}, u32[]{:S(2)}, u32[]{:S(2)}) collective-permute-start(bf16[12,16,256]{2,1,0:T(8,128)(2,1)S(1)} %get-tuple-element.28), channel_id=1, source_target_pairs={{0,6},{2,8},{4,14},{6,0},{8,2},{10,12},{12,10},{14,4},{16,26},{18,... | collective-permute-start | bytes 294920 | tf_op jit(solution)/shard_map/ppermute | solution.py:275
  9.8 2.8 %collective-permute-done.2.received = bf16[12,16,256]{2,1,0:T(8,128)(2,1)S(1)} collective-permute-done((bf16[12,16,256]{2,1,0:T(8,128)(2,1)S(1)}, bf16[12,16,256]{2,1,0:T(8,128)(2,1)S(1)}, u32[]{:S(2)}, u32[]{:S(2)}) %collective-permute-start.2) | collective-permute-done | bytes 98336 | tf_op jit(solution)/shard_map/ppermute | solution.py:275
  12.6 1.4 %collective-permute-start.3 = (bf16[10,16,256]{2,1,0:T(8,128)(2,1)S(1)}, bf16[10,16,256]{2,1,0:T(8,128)(2,1)S(1)}, u32[]{:S(2)}, u32[]{:S(2)}) collective-permute-start(bf16[10,16,256]{2,1,0:T(8,128)(2,1)S(1)} %get-tuple-element.30), channel_id=1, source_target_pairs={{0,10},{2,16},{4,22},{6,12},{8,26},{10,0},{12,6},{14,28},{16,2},{1... | collective-permute-start | bytes 245768 | tf_op jit(solution)/shard_map/ppermute | solution.py:275
  14.0 2.6 %collective-permute-done.3.received = bf16[10,16,256]{2,1,0:T(8,128)(2,1)S(1)} collective-permute-done((bf16[10,16,256]{2,1,0:T(8,128)(2,1)S(1)}, bf16[10,16,256]{2,1,0:T(8,128)(2,1)S(1)}, u32[]{:S(2)}, u32[]{:S(2)}) %collective-permute-start.3) | collective-permute-done | bytes 81952 | tf_op jit(solution)/shard_map/ppermute | solution.py:275
  16.6 3.1 %collective-permute-start.4 = (bf16[9,16,256]{2,1,0:T(8,128)(2,1)S(1)}, bf16[9,16,256]{2,1,0:T(8,128)(2,1)S(1)}, u32[]{:S(2)}, u32[]{:S(2)}) collective-permute-start(bf16[9,16,256]{2,1,0:T(8,128)(2,1)S(1)} %get-tuple-element.32), channel_id=1, source_target_pairs={{0,18},{2,4},{4,2},{6,20},{8,14},{10,24},{12,30},{14,8},{16,22},{1... | collective-permute-start | bytes 221192 | tf_op jit(solution)/shard_map/ppermute | solution.py:275
  19.7 2.0 %collective-permute-done.4.received = bf16[9,16,256]{2,1,0:T(8,128)(2,1)S(1)} collective-permute-done((bf16[9,16,256]{2,1,0:T(8,128)(2,1)S(1)}, bf16[9,16,256]{2,1,0:T(8,128)(2,1)S(1)}, u32[]{:S(2)}, u32[]{:S(2)}) %collective-permute-start.4) | collective-permute-done | bytes 73760 | tf_op jit(solution)/shard_map/ppermute | solution.py:275
  21.8 0.5 %collective-permute-start.5 = (f32[8,128]{1,0:T(8,128)S(1)}, f32[8,128]{1,0:T(8,128)S(1)}, u32[]{:S(2)}, u32[]{:S(2)}) collective-permute-start(f32[8,128]{1,0:T(8,128)S(1)} %get-tuple-element.34), channel_id=1, source_target_pairs={{0,2},{2,0},{4,6},{6,4},{8,10},{10,8},{12,14},{14,12},{16,18},{18,... | collective-permute-start | bytes 12296 | tf_op jit(solution)/shard_map/ppermute | solution.py:270
  22.3 0.8 %collective-permute-done.5 = f32[8,128]{1,0:T(8,128)S(1)} collective-permute-done((f32[8,128]{1,0:T(8,128)S(1)}, f32[8,128]{1,0:T(8,128)S(1)}, u32[]{:S(2)}, u32[]{:S(2)}) %collective-permute-start.5) | collective-permute-done | bytes 4128 | tf_op jit(solution)/shard_map/ppermute | solution.py:270
  23.2 1.2 %collective-permute-start.6 = (f32[8,128]{1,0:T(8,128)S(1)}, f32[8,128]{1,0:T(8,128)S(1)}, u32[]{:S(2)}, u32[]{:S(2)}) collective-permute-start(f32[8,128]{1,0:T(8,128)S(1)} %add.3.squares), channel_id=1, source_target_pairs={{0,3},{1,2},{2,1},{3,0},{4,7},{5,6},{6,5},{7,4},{8,11},{9,10},{10,... | collective-permute-start | bytes 12296 | tf_op jit(solution)/shard_map/ppermute | solution.py:270
  24.4 1.8 %collective-permute-done.6.more = f32[8,128]{1,0:T(8,128)S(1)} collective-permute-done((f32[8,128]{1,0:T(8,128)S(1)}, f32[8,128]{1,0:T(8,128)S(1)}, u32[]{:S(2)}, u32[]{:S(2)}) %collective-permute-start.6) | collective-permute-done | bytes 4128 | tf_op jit(solution)/shard_map/ppermute | solution.py:270
  26.2 0.7 %update.1 = f32[16,256]{1,0:T(8,128)} custom-call(bf16[16,256]{1,0:T(8,128)(2,1)S(1)} %get-tuple-element.20.mine, f32[16,256]{1,0:T(8,128)S(1)} %get-tuple-element.33.own, f32[8,128]{1,0:T(8,128)S(1)} %add.3.squares, f32[8,128]{1,0:T(8,128)S(1)} %collective-permute-done.6.more), custom_call_target="tpu_custom_call" | custom-call | tf_op jit(solution)/shard_map/update/pallas_call | solution.py:256
  (5 shorter events, 0.1 us)
Async XLA Ops:
  0.0 4.7 %copy-start = (bf16[1,1,64,128,128]{4,3,2,1,0:T(8,128)(2,1)S(1)}, bf16[1,1,64,128,128]{4,3,2,1,0:T(8,128)(2,1)}, u32[]{:S(2)}) copy-start(bf16[1,1,64,128,128]{4,3,2,1,0:T(8,128)(2,1)} %param.11) | copy-start | bytes 6291460
  0.0 4.7 %copy-start.1 = (bf16[2048,256]{1,0:T(8,128)(2,1)S(1)}, bf16[2048,256]{1,0:T(8,128)(2,1)}, u32[]{:S(2)}) copy-start(bf16[2048,256]{1,0:T(8,128)(2,1)} %users.1) | copy-start | bytes 3145732
  0.0 4.7 %copy-start.2 = (bf16[1,256,256]{2,1,0:T(8,128)(2,1)S(1)}, bf16[1,256,256]{2,1,0:T(8,128)(2,1)}, u32[]{:S(2)}) copy-start(bf16[1,256,256]{2,1,0:T(8,128)(2,1)} %param.10) | copy-start | bytes 393220
  1.0 5.8 %copy-start.3 = (bf16[1,1,2,128,128]{4,3,2,1,0:T(8,128)(2,1)S(1)}, bf16[1,1,2,128,128]{4,3,2,1,0:T(8,128)(2,1)}, u32[]{:S(2)}) copy-start(bf16[1,1,2,128,128]{4,3,2,1,0:T(8,128)(2,1)} %param.17) | copy-start | bytes 196612
  1.0 5.8 %collective-permute-start = (bf16[128,256]{1,0:T(8,128)(2,1)S(1)}, bf16[128,256]{1,0:T(8,128)(2,1)S(1)}, u32[]{:S(2)}, u32[]{:S(2)}) collective-permute-start(bf16[128,256]{1,0:T(8,128)(2,1)S(1)} %get-tuple-element.24), channel_id=1, source_target_pairs={{0,1},{1,0},{2,3},{3,2},{4,5},{5,4},{6,7},{7,6},{8,9},{9,8},{10,11... | collective-permute-start | bytes 196616 | tf_op jit(solution)/shard_map/ppermute | solution.py:270
  7.1 1.4 %collective-permute-start.1 = (f32[8,16,256]{2,1,0:T(8,128)S(1)}, f32[8,16,256]{2,1,0:T(8,128)S(1)}, u32[]{:S(2)}, u32[]{:S(2)}) collective-permute-start(f32[8,16,256]{2,1,0:T(8,128)S(1)} %get-tuple-element.26), channel_id=1, source_target_pairs={{0,2},{2,0},{4,6},{6,4},{8,10},{10,8},{12,14},{14,12},{16,18},{18,... | collective-permute-start | bytes 393224 | tf_op jit(solution)/shard_map/ppermute | solution.py:270
  8.5 4.1 %collective-permute-start.2 = (bf16[12,16,256]{2,1,0:T(8,128)(2,1)S(1)}, bf16[12,16,256]{2,1,0:T(8,128)(2,1)S(1)}, u32[]{:S(2)}, u32[]{:S(2)}) collective-permute-start(bf16[12,16,256]{2,1,0:T(8,128)(2,1)S(1)} %get-tuple-element.28), channel_id=1, source_target_pairs={{0,6},{2,8},{4,14},{6,0},{8,2},{10,12},{12,10},{14,4},{16,26},{18,... | collective-permute-start | bytes 294920 | tf_op jit(solution)/shard_map/ppermute | solution.py:275
  12.6 3.9 %collective-permute-start.3 = (bf16[10,16,256]{2,1,0:T(8,128)(2,1)S(1)}, bf16[10,16,256]{2,1,0:T(8,128)(2,1)S(1)}, u32[]{:S(2)}, u32[]{:S(2)}) collective-permute-start(bf16[10,16,256]{2,1,0:T(8,128)(2,1)S(1)} %get-tuple-element.30), channel_id=1, source_target_pairs={{0,10},{2,16},{4,22},{6,12},{8,26},{10,0},{12,6},{14,28},{16,2},{1... | collective-permute-start | bytes 245768 | tf_op jit(solution)/shard_map/ppermute | solution.py:275
  16.6 5.1 %collective-permute-start.4 = (bf16[9,16,256]{2,1,0:T(8,128)(2,1)S(1)}, bf16[9,16,256]{2,1,0:T(8,128)(2,1)S(1)}, u32[]{:S(2)}, u32[]{:S(2)}) collective-permute-start(bf16[9,16,256]{2,1,0:T(8,128)(2,1)S(1)} %get-tuple-element.32), channel_id=1, source_target_pairs={{0,18},{2,4},{4,2},{6,20},{8,14},{10,24},{12,30},{14,8},{16,22},{1... | collective-permute-start | bytes 221192 | tf_op jit(solution)/shard_map/ppermute | solution.py:275
  21.8 1.4 %collective-permute-start.5 = (f32[8,128]{1,0:T(8,128)S(1)}, f32[8,128]{1,0:T(8,128)S(1)}, u32[]{:S(2)}, u32[]{:S(2)}) collective-permute-start(f32[8,128]{1,0:T(8,128)S(1)} %get-tuple-element.34), channel_id=1, source_target_pairs={{0,2},{2,0},{4,6},{6,4},{8,10},{10,8},{12,14},{14,12},{16,18},{18,... | collective-permute-start | bytes 12296 | tf_op jit(solution)/shard_map/ppermute | solution.py:270
  23.2 3.0 %collective-permute-start.6 = (f32[8,128]{1,0:T(8,128)S(1)}, f32[8,128]{1,0:T(8,128)S(1)}, u32[]{:S(2)}, u32[]{:S(2)}) collective-permute-start(f32[8,128]{1,0:T(8,128)S(1)} %add.3.squares), channel_id=1, source_target_pairs={{0,3},{1,2},{2,1},{3,0},{4,7},{5,6},{6,5},{7,4},{8,11},{9,10},{10,... | collective-permute-start | bytes 12296 | tf_op jit(solution)/shard_map/ppermute | solution.py:270

commit v5 on v4

--- a/solution.py
+++ b/solution.py
@@ -165,15 +165,17 @@
 def graph_kernel(n_panels, hit, grad, similarity, *refs):
     panels, outs, total = refs[:n_panels], refs[n_panels:-1], refs[-1]
     blocks, tile, unused = similarity.shape
-    total[...] = grad[...]
     col = lax.axis_index("cols")
+    parts = []
     for k in range(blocks):
         block = k if n_panels == 1 else k ^ col
         panel = panels[0][k] if n_panels == 1 else panels[k][...]
-        part = dot(similarity[block], panel, ((1,), (0,)))
-        for j in range(total.shape[0] // tile):
-            chosen = jnp.broadcast_to(hit[block, j][:1, :1], part.shape) > 0
-            total[j * tile:(j + 1) * tile, :] += jnp.where(chosen, part, 0)
+        parts.append((block, dot(similarity[block], panel, ((1,), (0,)))))
+    for j in range(total.shape[0] // tile):
+        value = grad[j * tile:(j + 1) * tile, :]
+        for block, part in parts:
+            value += jnp.where(jnp.broadcast_to(hit[block, j][:1, :1], part.shape) > 0, part, 0)
+        total[j * tile:(j + 1) * tile, :] = value
     me = lax.axis_index("rows")
     if len(outs) == 1:
         outs[0][...] = total[...]
@@ -248,7 +250,7 @@
         for a in range(0, rows, 8):
             for b in range(0, rank, 128):
                 part = part + square[a:a + 8, b:b + 128]
-    squares[...] = part
+    squares[...] = jnp.sum(part, axis=0, keepdims=True)
 
 
 def local_call(kernel, name, args, out_shape):
@@ -261,8 +263,8 @@
 
 
 def update_kernel(entries, mine, own, squares, more, new):
-    meansq = jnp.sum(squares[...] + more[...], keepdims=True) / entries
-    new[...] = mine[...].astype(F32) - 0.5 * own[...] / jnp.sqrt(meansq + 1e-06)
+    meansq = jnp.sum(jnp.broadcast_to(squares[...] + more[...], (8, 128)), axis=1, keepdims=True)[:1] * (1 / entries)
+    new[...] = mine[...].astype(F32) - own[...] * (0.5 * lax.rsqrt(meansq + 1e-06))
 
 
 def swap(value, axis, bit):
@@ -318,7 +320,7 @@
         )
     own, squares = local_call(
         functools.partial(last_kernel, half // 2), "add_last", (total, hop(sent, n_hops - 1)),
-        (jax.ShapeDtypeStruct((own_rows, rank), F32), jax.ShapeDtypeStruct((8, 128), F32)),
+        (jax.ShapeDtypeStruct((own_rows, rank), F32), jax.ShapeDtypeStruct((1, 128), F32)),
     )
     squares = squares + swap(squares, "rows", 1)
     updated = local_call(

time: 27.1 us -> 26.9 us (level)
  starting transfers between devices: 10.6 us -> 11.4 us
  waiting for transfers between devices: 11.4 us -> 10.7 us
  Pallas kernels: 4.17 us -> 3.85 us
    ppermute x3, starting transfers between devices: 5.76 us -> 6.67 us  [hop(): lax.ppermute(value, 'rows', [(i, i ^ 1 ^ hops(size, parity(i))[b]) for i...]
    ppermute x3, waiting for transfers between devices: 7.43 us -> 6.83 us  [hop(): lax.ppermute(value, 'rows', [(i, i ^ 1 ^ hops(size, parity(i))[b]) for i...]
    pallas_call x1, Pallas kernels: 2.12 us -> 1.83 us  [rating_part(): pl.pallas_call(rating_kernel, name='rating_part', out_shape=(jax.ShapeDty...]
  transfers between devices with their start and end apart: 7 -> 7, of which waited for: 6 -> 6; matrix products, arithmetic and copies ran while one was open for 0% -> 0% of each run, Pallas kernels for 8% -> 7%
where the time goes in v5:
time: 26.9 us; the launch traced here: 26.7 us
  starting transfers between devices  11.4 us (42%)
  waiting for transfers between devices  10.7 us (40%)
  Pallas kernels  3.85 us (14%)
  between operations  0.75 us (3%)
    ppermute x3, waiting for transfers between devices, hop(): lax.ppermute(value, 'rows', [(i, i ^ 1 ^ hops(size, parity(i))[b]) for i...  6.83 us
    ppermute x3, starting transfers between devices, hop(): lax.ppermute(value, 'rows', [(i, i ^ 1 ^ hops(size, parity(i))[b]) for i...  6.67 us
    ppermute x4, starting transfers between devices, swap(): return lax.ppermute(value, axis, [(i, i ^ bit) for i in range(size)])  4.7 us
    ppermute x4, waiting for transfers between devices, swap(): return lax.ppermute(value, axis, [(i, i ^ bit) for i in range(size)])  3.86 us
    pallas_call x1, Pallas kernels, rating_part(): pl.pallas_call(rating_kernel, name='rating_part', out_shape=(jax.ShapeDty...  1.83 us
    pallas_call x1, Pallas kernels, pick_panels(): pl.pallas_call(pick_kernel, name='pick_panels', out_shape=(panel, panel),...  1.01 us
    pallas_call x5, Pallas kernels, local_call(): pl.pallas_call(kernel, name=name, out_shape=out_shape, in_specs=[vmem] *...  0.81 us
  transfers between devices with their start and end apart: 7, of which 6 were waited for; matrix products, arithmetic and copies ran while one was open for 0% of the time, Pallas kernels for 7%

profile of v5, /device:TPU:0, one launch (start us, length us, event | category | flops | bytes accessed | tf_op | source)
XLA Modules:
  0.0 26.7 jit_solution(18042600099758230792)
XLA Ops:
  0.0 0.0 copy-start
  0.0 0.0 copy-start.1
  0.0 0.0 copy-start.2
  0.0 1.0 %pick_panels.1 = (bf16[128,256]{1,0:T(8,128)(2,1)S(1)}, bf16[128,256]{1,0:T(8,128)(2,1)S(1)}) custom-call(s32[2]{0:T(128)} %bitcast.15, bf16[256,256]{1,0:T(8,128)(2,1)} %bitcast.9), custom_call_target="tpu_custom_call" | custom-call | flops 10000000000 | bytes 30000000 | tf_op jit(solution)/shard_map/pick_panels/pallas_call | solution.py:134
  1.0 0.0 copy-start.3
  1.0 3.0 %collective-permute-start = (bf16[128,256]{1,0:T(8,128)(2,1)S(1)}, bf16[128,256]{1,0:T(8,128)(2,1)S(1)}, u32[]{:S(2)}, u32[]{:S(2)}) collective-permute-start(bf16[128,256]{1,0:T(8,128)(2,1)S(1)} %get-tuple-element.24), channel_id=1, source_target_pairs={{0,1},{1,0},{2,3},{3,2},{4,5},{5,4},{6,7},{7,6},{8,9},{9,8},{10,11... | collective-permute-start | bytes 196616 | tf_op jit(solution)/shard_map/ppermute | solution.py:272
  4.7 0.0 copy-done
  4.7 0.0 copy-done.1
  4.7 0.0 copy-done.2
  4.7 1.8 %rating_part.1 = (f32[256,256]{1,0:T(8,128)S(1)}, bf16[16,256]{1,0:T(8,128)(2,1)S(1)}, f32[2,2,8,128]{3,2,1,0:T(8,128)S(1)}) custom-call(s32[64]{0:T(128)} %bitcast.12, s32[64]{0:T(128)} %bitcast.13, s32[2]{0:T(128)} %bitcast.14, s32[1,1]{1,0:T(1,128)S(6)} %copy.10.count, bf16[2048,256]{1,0:T(8,128)(2,1)S(1)} %copy-done.1, bf16[256,256]{1,0:T(8,128)(2,1)S(1)} %bitcast.10, ...), custom_call_target="tpu_custom_call" | custom-call | tf_op jit(solution)/shard_map/rating_part/pallas_call | solution.py:90
  6.6 0.0 collective-permute-done.refs_1_
  6.6 0.0 copy-done.3
  6.6 0.2 graph_part.1
  6.8 0.1 collective-permute-start.1
  6.9 1.3 %collective-permute-done.1.received = f32[8,16,256]{2,1,0:T(8,128)S(1)} collective-permute-done((f32[8,16,256]{2,1,0:T(8,128)S(1)}, f32[8,16,256]{2,1,0:T(8,128)S(1)}, u32[]{:S(2)}, u32[]{:S(2)}) %collective-permute-start.1) | collective-permute-done | bytes 131104 | tf_op jit(solution)/shard_map/ppermute | solution.py:272
  8.2 1.6 %collective-permute-start.2 = (bf16[12,16,256]{2,1,0:T(8,128)(2,1)S(1)}, bf16[12,16,256]{2,1,0:T(8,128)(2,1)S(1)}, u32[]{:S(2)}, u32[]{:S(2)}) collective-permute-start(bf16[12,16,256]{2,1,0:T(8,128)(2,1)S(1)} %get-tuple-element.28), channel_id=1, source_target_pairs={{0,6},{2,8},{4,14},{6,0},{8,2},{10,12},{12,10},{14,4},{16,26},{18,... | collective-permute-start | bytes 294920 | tf_op jit(solution)/shard_map/ppermute | solution.py:277
  9.8 2.5 %collective-permute-done.2.received = bf16[12,16,256]{2,1,0:T(8,128)(2,1)S(1)} collective-permute-done((bf16[12,16,256]{2,1,0:T(8,128)(2,1)S(1)}, bf16[12,16,256]{2,1,0:T(8,128)(2,1)S(1)}, u32[]{:S(2)}, u32[]{:S(2)}) %collective-permute-start.2) | collective-permute-done | bytes 98336 | tf_op jit(solution)/shard_map/ppermute | solution.py:277
  12.4 1.7 %collective-permute-start.3 = (bf16[10,16,256]{2,1,0:T(8,128)(2,1)S(1)}, bf16[10,16,256]{2,1,0:T(8,128)(2,1)S(1)}, u32[]{:S(2)}, u32[]{:S(2)}) collective-permute-start(bf16[10,16,256]{2,1,0:T(8,128)(2,1)S(1)} %get-tuple-element.30), channel_id=1, source_target_pairs={{0,10},{2,16},{4,22},{6,12},{8,26},{10,0},{12,6},{14,28},{16,2},{1... | collective-permute-start | bytes 245768 | tf_op jit(solution)/shard_map/ppermute | solution.py:277
  14.0 2.3 %collective-permute-done.3.received = bf16[10,16,256]{2,1,0:T(8,128)(2,1)S(1)} collective-permute-done((bf16[10,16,256]{2,1,0:T(8,128)(2,1)S(1)}, bf16[10,16,256]{2,1,0:T(8,128)(2,1)S(1)}, u32[]{:S(2)}, u32[]{:S(2)}) %collective-permute-start.3) | collective-permute-done | bytes 81952 | tf_op jit(solution)/shard_map/ppermute | solution.py:277
  16.3 3.4 %collective-permute-start.4 = (bf16[9,16,256]{2,1,0:T(8,128)(2,1)S(1)}, bf16[9,16,256]{2,1,0:T(8,128)(2,1)S(1)}, u32[]{:S(2)}, u32[]{:S(2)}) collective-permute-start(bf16[9,16,256]{2,1,0:T(8,128)(2,1)S(1)} %get-tuple-element.32), channel_id=1, source_target_pairs={{0,18},{2,4},{4,2},{6,20},{8,14},{10,24},{12,30},{14,8},{16,22},{1... | collective-permute-start | bytes 221192 | tf_op jit(solution)/shard_map/ppermute | solution.py:277
  19.7 2.0 %collective-permute-done.4.received = bf16[9,16,256]{2,1,0:T(8,128)(2,1)S(1)} collective-permute-done((bf16[9,16,256]{2,1,0:T(8,128)(2,1)S(1)}, bf16[9,16,256]{2,1,0:T(8,128)(2,1)S(1)}, u32[]{:S(2)}, u32[]{:S(2)}) %collective-permute-start.4) | collective-permute-done | bytes 73760 | tf_op jit(solution)/shard_map/ppermute | solution.py:277
  21.8 0.3 %collective-permute-start.5 = (f32[1,128]{1,0:T(1,128)S(1)}, f32[1,128]{1,0:T(1,128)S(1)}, u32[]{:S(2)}, u32[]{:S(2)}) collective-permute-start(f32[1,128]{1,0:T(1,128)S(1)} %get-tuple-element.34), channel_id=1, source_target_pairs={{0,2},{2,0},{4,6},{6,4},{8,10},{10,8},{12,14},{14,12},{16,18},{18,... | collective-permute-start | bytes 1544 | tf_op jit(solution)/shard_map/ppermute | solution.py:272
  22.2 0.9 %collective-permute-done.5 = f32[1,128]{1,0:T(1,128)S(1)} collective-permute-done((f32[1,128]{1,0:T(1,128)S(1)}, f32[1,128]{1,0:T(1,128)S(1)}, u32[]{:S(2)}, u32[]{:S(2)}) %collective-permute-start.5) | collective-permute-done | bytes 544 | tf_op jit(solution)/shard_map/ppermute | solution.py:272
  23.0 1.3 %collective-permute-start.6 = (f32[1,128]{1,0:T(1,128)S(1)}, f32[1,128]{1,0:T(1,128)S(1)}, u32[]{:S(2)}, u32[]{:S(2)}) collective-permute-start(f32[1,128]{1,0:T(1,128)S(1)} %add.3.squares), channel_id=1, source_target_pairs={{0,3},{1,2},{2,1},{3,0},{4,7},{5,6},{6,5},{7,4},{8,11},{9,10},{10,... | collective-permute-start | bytes 1544 | tf_op jit(solution)/shard_map/ppermute | solution.py:272
  24.3 1.7 %collective-permute-done.6.more = f32[1,128]{1,0:T(1,128)S(1)} collective-permute-done((f32[1,128]{1,0:T(1,128)S(1)}, f32[1,128]{1,0:T(1,128)S(1)}, u32[]{:S(2)}, u32[]{:S(2)}) %collective-permute-start.6) | collective-permute-done | bytes 544 | tf_op jit(solution)/shard_map/ppermute | solution.py:272
  26.0 0.7 %update.1 = f32[16,256]{1,0:T(8,128)} custom-call(bf16[16,256]{1,0:T(8,128)(2,1)S(1)} %get-tuple-element.20.mine, f32[16,256]{1,0:T(8,128)S(1)} %get-tuple-element.33.own, f32[1,128]{1,0:T(1,128)S(1)} %add.3.squares, f32[1,128]{1,0:T(1,128)S(1)} %collective-permute-done.6.more), custom_call_target="tpu_custom_call" | custom-call | tf_op jit(solution)/shard_map/update/pallas_call | solution.py:258
  (5 shorter events, 0.1 us)
Async XLA Ops:
  0.0 4.7 %copy-start = (bf16[1,1,64,128,128]{4,3,2,1,0:T(8,128)(2,1)S(1)}, bf16[1,1,64,128,128]{4,3,2,1,0:T(8,128)(2,1)}, u32[]{:S(2)}) copy-start(bf16[1,1,64,128,128]{4,3,2,1,0:T(8,128)(2,1)} %param.11) | copy-start | bytes 6291460
  0.0 4.7 %copy-start.1 = (bf16[2048,256]{1,0:T(8,128)(2,1)S(1)}, bf16[2048,256]{1,0:T(8,128)(2,1)}, u32[]{:S(2)}) copy-start(bf16[2048,256]{1,0:T(8,128)(2,1)} %users.1) | copy-start | bytes 3145732
  0.0 4.7 %copy-start.2 = (bf16[1,256,256]{2,1,0:T(8,128)(2,1)S(1)}, bf16[1,256,256]{2,1,0:T(8,128)(2,1)}, u32[]{:S(2)}) copy-start(bf16[1,256,256]{2,1,0:T(8,128)(2,1)} %param.10) | copy-start | bytes 393220
  1.0 5.6 %copy-start.3 = (bf16[1,1,2,128,128]{4,3,2,1,0:T(8,128)(2,1)S(1)}, bf16[1,1,2,128,128]{4,3,2,1,0:T(8,128)(2,1)}, u32[]{:S(2)}) copy-start(bf16[1,1,2,128,128]{4,3,2,1,0:T(8,128)(2,1)} %param.17) | copy-start | bytes 196612
  1.0 5.5 %collective-permute-start = (bf16[128,256]{1,0:T(8,128)(2,1)S(1)}, bf16[128,256]{1,0:T(8,128)(2,1)S(1)}, u32[]{:S(2)}, u32[]{:S(2)}) collective-permute-start(bf16[128,256]{1,0:T(8,128)(2,1)S(1)} %get-tuple-element.24), channel_id=1, source_target_pairs={{0,1},{1,0},{2,3},{3,2},{4,5},{5,4},{6,7},{7,6},{8,9},{9,8},{10,11... | collective-permute-start | bytes 196616 | tf_op jit(solution)/shard_map/ppermute | solution.py:272
  6.8 1.4 %collective-permute-start.1 = (f32[8,16,256]{2,1,0:T(8,128)S(1)}, f32[8,16,256]{2,1,0:T(8,128)S(1)}, u32[]{:S(2)}, u32[]{:S(2)}) collective-permute-start(f32[8,16,256]{2,1,0:T(8,128)S(1)} %get-tuple-element.26), channel_id=1, source_target_pairs={{0,2},{2,0},{4,6},{6,4},{8,10},{10,8},{12,14},{14,12},{16,18},{18,... | collective-permute-start | bytes 393224 | tf_op jit(solution)/shard_map/ppermute | solution.py:272
  8.2 4.1 %collective-permute-start.2 = (bf16[12,16,256]{2,1,0:T(8,128)(2,1)S(1)}, bf16[12,16,256]{2,1,0:T(8,128)(2,1)S(1)}, u32[]{:S(2)}, u32[]{:S(2)}) collective-permute-start(bf16[12,16,256]{2,1,0:T(8,128)(2,1)S(1)} %get-tuple-element.28), channel_id=1, source_target_pairs={{0,6},{2,8},{4,14},{6,0},{8,2},{10,12},{12,10},{14,4},{16,26},{18,... | collective-permute-start | bytes 294920 | tf_op jit(solution)/shard_map/ppermute | solution.py:277
  12.4 3.9 %collective-permute-start.3 = (bf16[10,16,256]{2,1,0:T(8,128)(2,1)S(1)}, bf16[10,16,256]{2,1,0:T(8,128)(2,1)S(1)}, u32[]{:S(2)}, u32[]{:S(2)}) collective-permute-start(bf16[10,16,256]{2,1,0:T(8,128)(2,1)S(1)} %get-tuple-element.30), channel_id=1, source_target_pairs={{0,10},{2,16},{4,22},{6,12},{8,26},{10,0},{12,6},{14,28},{16,2},{1... | collective-permute-start | bytes 245768 | tf_op jit(solution)/shard_map/ppermute | solution.py:277
  16.3 5.5 %collective-permute-start.4 = (bf16[9,16,256]{2,1,0:T(8,128)(2,1)S(1)}, bf16[9,16,256]{2,1,0:T(8,128)(2,1)S(1)}, u32[]{:S(2)}, u32[]{:S(2)}) collective-permute-start(bf16[9,16,256]{2,1,0:T(8,128)(2,1)S(1)} %get-tuple-element.32), channel_id=1, source_target_pairs={{0,18},{2,4},{4,2},{6,20},{8,14},{10,24},{12,30},{14,8},{16,22},{1... | collective-permute-start | bytes 221192 | tf_op jit(solution)/shard_map/ppermute | solution.py:277
  21.8 1.2 %collective-permute-start.5 = (f32[1,128]{1,0:T(1,128)S(1)}, f32[1,128]{1,0:T(1,128)S(1)}, u32[]{:S(2)}, u32[]{:S(2)}) collective-permute-start(f32[1,128]{1,0:T(1,128)S(1)} %get-tuple-element.34), channel_id=1, source_target_pairs={{0,2},{2,0},{4,6},{6,4},{8,10},{10,8},{12,14},{14,12},{16,18},{18,... | collective-permute-start | bytes 1544 | tf_op jit(solution)/shard_map/ppermute | solution.py:272
  23.0 3.0 %collective-permute-start.6 = (f32[1,128]{1,0:T(1,128)S(1)}, f32[1,128]{1,0:T(1,128)S(1)}, u32[]{:S(2)}, u32[]{:S(2)}) collective-permute-start(f32[1,128]{1,0:T(1,128)S(1)} %add.3.squares), channel_id=1, source_target_pairs={{0,3},{1,2},{2,1},{3,0},{4,7},{5,6},{6,5},{7,4},{8,11},{9,10},{10,... | collective-permute-start | bytes 1544 | tf_op jit(solution)/shard_map/ppermute | solution.py:272

commit v6 on v5

--- a/solution.py
+++ b/solution.py
@@ -21,10 +21,9 @@
     return lax.dot_general(a, b, (dims, ((), ())), preferred_element_type=F32)
 
 
-def rating_kernel(
-    user_idx_hbm, item_idx_hbm, target_hbm, count, users, items, ratings, grad_ref, mine_ref, hit_ref,
-    user_idx, item_idx, target, items_t, pred, err, sem_s,
-):
+def rating_kernel(half, user_idx_hbm, item_idx_hbm, target_hbm, count, users, items, ratings, similarity, near, *refs):
+    grad_out, mine_ref, keep_far, give_far, give_out = refs[:5]
+    grad_ref, far_ref, user_idx, item_idx, target, items_t, pred, err, sem_s = refs[5:]
     n_tiles, tile = ratings.shape[0], ratings.shape[1]
     n_item = items.shape[0] // tile
     scalars = [
@@ -51,9 +50,10 @@
     for copy in scalars:
         copy.wait()
     live = count[0, 0]
-    for k in range(hit_ref.shape[0]):
-        for j in range(n_item):
-            hit_ref[k, j] = jnp.full((8, 128), (target[k] == j).astype(F32))
+    col = lax.axis_index("cols")
+    block = similarity[1 - col]
+    for j in range(n_item):
+        far_ref[j * tile:(j + 1) * tile, :] = jnp.where(target[1 - col] == j, block, jnp.zeros_like(block))
 
     def add_tile(t):
         j = item_idx[t]
@@ -76,10 +76,28 @@
         whole = err[j]
         high = whole.astype(BF16)
         low = (whole - high.astype(F32)).astype(BF16)
-        grad_ref[j * tile:(j + 1) * tile, :] = dot(high, users[...], ((0,), (0,))) + dot(low, users[...], ((0,), (0,)))
-
-
-def rating_part(user_idx, item_idx, count, target, users, items, ratings, own_rows):
+        whole = dot(jnp.concatenate([high, low], axis=1), users[...], ((0,), (0,)))
+        grad_ref[j * tile:(j + 1) * tile, :] = whole[:tile] + whole[tile:]
+    if not half:
+        grad_out[...] = grad_ref[...]
+        return
+    rows = pl.ds(pl.multiple_of(target[col] * tile, tile), tile)
+    grad_ref[rows, :] += dot(similarity[col], near[...], ((1,), (0,)))
+    me = lax.axis_index("rows")
+    odd = sum((me >> b) & 1 for b in range(half.bit_length())) % 2
+    for q in range(half):
+        even_place, odd_place = (offset(2 * half, parity_, q) for parity_ in (0, 1))
+        span = slice(q * own, (q + 1) * own)
+        for out, far_out, place in (
+            (grad_out, keep_far, me ^ jnp.where(odd == 1, odd_place, even_place)),
+            (give_out, give_far, me ^ 1 ^ jnp.where(odd == 1, even_place, odd_place)),
+        ):
+            rows = pl.ds(pl.multiple_of(place * own, own), own)
+            out[span, :] = grad_ref[rows, :]
+            far_out[span, :] = far_ref[rows, :]
+
+
+def rating_part(user_idx, item_idx, count, target, users, items, ratings, similarity, near, own_rows, half):
     tile = ratings.shape[1]
     n_item = items.shape[0] // tile
     smem = pl.BlockSpec(memory_space=pltpu.SMEM)
@@ -87,17 +105,18 @@
     vmem = pl.BlockSpec(memory_space=pltpu.VMEM)
     sums = pltpu.VMEM((n_item, users.shape[0], tile), F32)
     limit = 16 if n_item <= 2 else 56
+    count_rows = half * own_rows if half else items.shape[0]
+    rows = jax.ShapeDtypeStruct((count_rows, items.shape[1]), F32)
+    far_rows = jax.ShapeDtypeStruct((count_rows, tile), BF16)
     return pl.pallas_call(
-        rating_kernel,
+        functools.partial(rating_kernel, half),
         name="rating_part",
-        out_shape=(
-            jax.ShapeDtypeStruct(items.shape, F32),
-            jax.ShapeDtypeStruct((own_rows, items.shape[1]), BF16),
-            jax.ShapeDtypeStruct((target.shape[0], n_item, 8, 128), F32),
-        ),
-        in_specs=[hbm] * 3 + [smem] + [vmem] * 3,
-        out_specs=(vmem, vmem, vmem),
+        out_shape=(rows, jax.ShapeDtypeStruct((own_rows, items.shape[1]), BF16), far_rows, far_rows, rows),
+        in_specs=[hbm] * 3 + [smem] + [vmem] * 5,
+        out_specs=(vmem,) * 5,
         scratch_shapes=[
+            pltpu.VMEM(items.shape, F32),
+            pltpu.VMEM((items.shape[0], tile), BF16),
             pltpu.SMEM(user_idx.shape, jnp.int32),
             pltpu.SMEM(item_idx.shape, jnp.int32),
             pltpu.SMEM(target.shape, jnp.int32),
@@ -107,7 +126,7 @@
             pltpu.SemaphoreType.DMA((3,)),
         ],
         compiler_params=pltpu.CompilerParams(vmem_limit_bytes=limit * 1024 * 1024),
-    )(*in_hbm(user_idx, item_idx, target), count, users, items, ratings)
+    )(*in_hbm(user_idx, item_idx, target), count, users, items, ratings, similarity, near)
 
 
 def pick_kernel(send_list_hbm, items_hbm, kept, sent, send_list, items, sem_s, sems):
@@ -162,47 +181,9 @@
     return value | parity(value)
 
 
-def graph_kernel(n_panels, hit, grad, similarity, *refs):
-    panels, outs, total = refs[:n_panels], refs[n_panels:-1], refs[-1]
-    blocks, tile, unused = similarity.shape
-    col = lax.axis_index("cols")
-    parts = []
-    for k in range(blocks):
-        block = k if n_panels == 1 else k ^ col
-        panel = panels[0][k] if n_panels == 1 else panels[k][...]
-        parts.append((block, dot(similarity[block], panel, ((1,), (0,)))))
-    for j in range(total.shape[0] // tile):
-        value = grad[j * tile:(j + 1) * tile, :]
-        for block, part in parts:
-            value += jnp.where(jnp.broadcast_to(hit[block, j][:1, :1], part.shape) > 0, part, 0)
-        total[j * tile:(j + 1) * tile, :] = value
-    me = lax.axis_index("rows")
-    if len(outs) == 1:
-        outs[0][...] = total[...]
-        return
-    keep, give = outs
-    half, own = keep.shape[:2]
-    odd = sum((me >> b) & 1 for b in range(half.bit_length())) % 2
-    for q in range(half):
-        even_place, odd_place = (offset(2 * half, parity_, q) for parity_ in (0, 1))
-        for out, block in (
-            (keep, me ^ jnp.where(odd == 1, odd_place, even_place)),
-            (give, me ^ 1 ^ jnp.where(odd == 1, even_place, odd_place)),
-        ):
-            out[q] = total[pl.ds(pl.multiple_of(block * own, own), own), :]
-
-
-def graph_part(hit, grad, similarity, panels, out_shape):
-    vmem = pl.BlockSpec(memory_space=pltpu.VMEM)
-    return pl.pallas_call(
-        functools.partial(graph_kernel, len(panels)),
-        name="graph_part",
-        out_shape=out_shape,
-        in_specs=[vmem] * (3 + len(panels)),
-        out_specs=jax.tree.map(lambda unused: vmem, out_shape),
-        scratch_shapes=[pltpu.VMEM(grad.shape, F32)],
-        compiler_params=pltpu.CompilerParams(vmem_limit_bytes=SMALL if grad.size <= 2**16 else 32 * 1024 * 1024),
-    )(hit, grad, similarity, *panels)
+def graph_kernel(grad, far_blocks, far, total):
+    whole = grad[...] + dot(far_blocks[...], far[...], ((1,), (0,)))
+    total[...] = whole.reshape(total.shape)
 
 
 def split_places(half, bit):
@@ -284,34 +265,38 @@
     icount, rank = items.shape[1:]
     tile = ratings.shape[-1]
     blocks = similarity.shape[2]
-    panels = items[0].reshape(-1, tile, rank)
     slots = send_list.shape[3]
-    if n_cols == 2 and slots == 1:
-        kept, sent = pick_panels(send_list.reshape(-1), items[0], tile)
-        incoming = (kept, swap(sent, "cols", 1))
-    else:
-        incoming = lax.all_to_all(panels[send_list[0, 0]], "cols", 0, 0, tiled=True)
-        incoming = (incoming.reshape(blocks, tile, rank),)
     own_rows = icount // n_rows
     target = block_target.reshape(-1)
-    grad, mine, hit = rating_part(
-        tile_users.reshape(-1), tile_items.reshape(-1), tile_count, target, users, items[0],
-        ratings[0, 0], own_rows,
+    entries = n_cols * icount * rank
+    by_hops = n_rows >= 4 and not n_rows & (n_rows - 1) and n_cols == 2 and slots == 1 and own_rows % 16 == 0
+    if by_hops:
+        near, sent = pick_panels(send_list.reshape(-1), items[0], tile)
+        far = swap(sent, "cols", 1)
+    else:
+        panels = items[0].reshape(-1, tile, rank)
+        incoming = lax.all_to_all(panels[send_list[0, 0]], "cols", 0, 0, tiled=True)
+        incoming = incoming.reshape(blocks, tile, rank)
+        near = jnp.zeros((tile, rank), BF16)
+    half = n_rows // 2 if by_hops else 0
+    grad, mine, keep_far, give_far, given = rating_part(
+        tile_users.reshape(-1), tile_items.reshape(-1), tile_count, target, users, items[0], ratings[0, 0],
+        similarity[0, 0, :2], near, own_rows, half,
     )
-    entries = n_cols * icount * rank
-    if n_rows & (n_rows - 1) or n_rows < 4 or n_cols != 2 or own_rows % 16:
-        flat = graph_part(hit, grad, similarity[0, 0], incoming, (jax.ShapeDtypeStruct((icount, rank), F32),))[0]
+    if not by_hops:
+        contrib = jnp.einsum("kab,kbr->kar", similarity[0, 0], incoming, preferred_element_type=F32)
+        flat = grad.reshape(-1, tile, rank).at[target].add(contrib).reshape(icount, rank)
         owned = lax.psum_scatter(flat, "rows", scatter_dimension=0, tiled=True)
         squares = lax.psum(jnp.sum(owned * owned), ("rows", "cols"))
         return (mine.astype(F32) - 0.5 * owned / jnp.sqrt(squares / entries + 1e-06))[None]
 
-    half = n_rows // 2
     block = jax.ShapeDtypeStruct((half, own_rows, rank), F32)
 
     def payload(bit):
         return jax.ShapeDtypeStruct((half + len(split_places(half, bit)), own_rows, rank), BF16)
 
-    keep, give = graph_part(hit, grad, similarity[0, 0], incoming, (block, block))
+    give = local_call(graph_kernel, "graph_give", (given, give_far, far), block)
+    keep = local_call(graph_kernel, "graph_keep", (grad, keep_far, far), block)
     total, sent = local_call(first_kernel, "add_core", (keep, swap(give, "rows", 1)), (block, payload(1)))
     n_hops = len(hops(n_rows, 0))
     for b in range(n_hops - 1):

time: 26.9 us -> 26.9 us (level)
  starting transfers between devices: 11.4 us -> 11.1 us
    pallas_call x5 -> x7, Pallas kernels: 0.81 us -> 1.11 us  [local_call(): pl.pallas_call(kernel, name=name, out_shape=out_shape, in_specs=[vmem] *...]
    ppermute x4, starting transfers between devices: 4.7 us -> 4.42 us  [swap(): return lax.ppermute(value, axis, [(i, i ^ bit) for i in range(size)])]
    pallas_call x2 -> x1, Pallas kernels: 2.03 us -> 1.82 us  [rating_part(): pl.pallas_call(functools.partial(rating_kernel, half), name='rating_part'...]
where the time goes in v6:
time: 26.9 us; the launch traced here: 26.7 us
  starting transfers between devices  11.1 us (41%)
  waiting for transfers between devices  10.9 us (41%)
  Pallas kernels  3.94 us (15%)
  between operations  0.75 us (3%)
    ppermute x3, waiting for transfers between devices, hop(): lax.ppermute(value, 'rows', [(i, i ^ 1 ^ hops(size, parity(i))[b]) for i...  6.86 us
    ppermute x3, starting transfers between devices, hop(): lax.ppermute(value, 'rows', [(i, i ^ 1 ^ hops(size, parity(i))[b]) for i...  6.69 us
    ppermute x4, starting transfers between devices, swap(): return lax.ppermute(value, axis, [(i, i ^ bit) for i in range(size)])  4.42 us
    ppermute x4, waiting for transfers between devices, swap(): return lax.ppermute(value, axis, [(i, i ^ bit) for i in range(size)])  3.99 us
    pallas_call x1, Pallas kernels, rating_part(): pl.pallas_call(functools.partial(rating_kernel, half), name='rating_part'...  1.82 us
    pallas_call x7, Pallas kernels, local_call(): pl.pallas_call(kernel, name=name, out_shape=out_shape, in_specs=[vmem] *...  1.11 us
    pallas_call x1, Pallas kernels, pick_panels(): pl.pallas_call(pick_kernel, name='pick_panels', out_shape=(panel, panel),...  1.01 us
  transfers between devices with their start and end apart: 7, of which 6 were waited for; matrix products, arithmetic and copies ran while one was open for 0% of the time, Pallas kernels for 7%

profile of v6, /device:TPU:0, one launch (start us, length us, event | category | flops | bytes accessed | tf_op | source)
XLA Modules:
  0.0 26.7 jit_solution(16693764677808493257)
XLA Ops:
  0.0 0.0 copy-start
  0.0 0.0 copy-start.1
  0.0 0.0 copy-start.2
  0.0 0.0 copy-start.3
  0.0 1.0 %pick_panels.1 = (bf16[128,256]{1,0:T(8,128)(2,1)S(1)}, bf16[128,256]{1,0:T(8,128)(2,1)S(1)}) custom-call(s32[2]{0:T(128)} %bitcast.15, bf16[256,256]{1,0:T(8,128)(2,1)} %bitcast.9), custom_call_target="tpu_custom_call" | custom-call | flops 10000000000 | bytes 30000000 | tf_op jit(solution)/shard_map/pick_panels/pallas_call | solution.py:153
  1.0 3.0 %collective-permute-start = (bf16[128,256]{1,0:T(8,128)(2,1)S(1)}, bf16[128,256]{1,0:T(8,128)(2,1)S(1)}, u32[]{:S(2)}, u32[]{:S(2)}) collective-permute-start(bf16[128,256]{1,0:T(8,128)(2,1)S(1)} %get-tuple-element.24), channel_id=1, source_target_pairs={{0,1},{1,0},{2,3},{3,2},{4,5},{5,4},{6,7},{7,6},{8,9},{9,8},{10,11... | collective-permute-start | bytes 196616 | tf_op jit(solution)/shard_map/ppermute | solution.py:253
  4.7 0.0 copy-done
  4.7 0.0 copy-done.1
  4.7 0.0 copy-done.2
  4.7 0.0 copy-done.3
  4.7 1.8 %rating_part.1 = (f32[128,256]{1,0:T(8,128)S(1)}, bf16[16,256]{1,0:T(8,128)(2,1)S(1)}, bf16[128,128]{1,0:T(8,128)(2,1)S(1)}, bf16[128,128]{1,0:T(8,128)(2,1)S(1)}, f32[128,256]{1,0:T(8,128)S(1)}) custom-call(s32[64]{0:T(128)} %bitcast.12, s32[64]{0:T(128)} %bitcast.13, s32[2]{0:T(128)} %bitcast.14, s32[1,1]{1,0:T(1,128)S(6)} %copy.10.count, ...), custom_call_target="tpu_custom_call" | custom-call | tf_op jit(solution)/shard_map/rating_part/pallas_call | solution.py:111
  6.6 0.0 collective-permute-done.far
  6.6 0.1 graph_give.1
  6.7 0.1 collective-permute-start.1
  6.8 0.2 graph_keep.1.keep
  7.0 1.2 %collective-permute-done.1.received = f32[8,16,256]{2,1,0:T(8,128)S(1)} collective-permute-done((f32[8,16,256]{2,1,0:T(8,128)S(1)}, f32[8,16,256]{2,1,0:T(8,128)S(1)}, u32[]{:S(2)}, u32[]{:S(2)}) %collective-permute-start.1) | collective-permute-done | bytes 131104 | tf_op jit(solution)/shard_map/ppermute | solution.py:253
  8.2 1.6 %collective-permute-start.2 = (bf16[12,16,256]{2,1,0:T(8,128)(2,1)S(1)}, bf16[12,16,256]{2,1,0:T(8,128)(2,1)S(1)}, u32[]{:S(2)}, u32[]{:S(2)}) collective-permute-start(bf16[12,16,256]{2,1,0:T(8,128)(2,1)S(1)} %get-tuple-element.28), channel_id=1, source_target_pairs={{0,6},{2,8},{4,14},{6,0},{8,2},{10,12},{12,10},{14,4},{16,26},{18,... | collective-permute-start | bytes 294920 | tf_op jit(solution)/shard_map/ppermute | solution.py:258
  9.7 2.5 %collective-permute-done.2.received = bf16[12,16,256]{2,1,0:T(8,128)(2,1)S(1)} collective-permute-done((bf16[12,16,256]{2,1,0:T(8,128)(2,1)S(1)}, bf16[12,16,256]{2,1,0:T(8,128)(2,1)S(1)}, u32[]{:S(2)}, u32[]{:S(2)}) %collective-permute-start.2) | collective-permute-done | bytes 98336 | tf_op jit(solution)/shard_map/ppermute | solution.py:258
  12.3 1.7 %collective-permute-start.3 = (bf16[10,16,256]{2,1,0:T(8,128)(2,1)S(1)}, bf16[10,16,256]{2,1,0:T(8,128)(2,1)S(1)}, u32[]{:S(2)}, u32[]{:S(2)}) collective-permute-start(bf16[10,16,256]{2,1,0:T(8,128)(2,1)S(1)} %get-tuple-element.30), channel_id=1, source_target_pairs={{0,10},{2,16},{4,22},{6,12},{8,26},{10,0},{12,6},{14,28},{16,2},{1... | collective-permute-start | bytes 245768 | tf_op jit(solution)/shard_map/ppermute | solution.py:258
  14.0 2.3 %collective-permute-done.3.received = bf16[10,16,256]{2,1,0:T(8,128)(2,1)S(1)} collective-permute-done((bf16[10,16,256]{2,1,0:T(8,128)(2,1)S(1)}, bf16[10,16,256]{2,1,0:T(8,128)(2,1)S(1)}, u32[]{:S(2)}, u32[]{:S(2)}) %collective-permute-start.3) | collective-permute-done | bytes 81952 | tf_op jit(solution)/shard_map/ppermute | solution.py:258
  16.4 3.4 %collective-permute-start.4 = (bf16[9,16,256]{2,1,0:T(8,128)(2,1)S(1)}, bf16[9,16,256]{2,1,0:T(8,128)(2,1)S(1)}, u32[]{:S(2)}, u32[]{:S(2)}) collective-permute-start(bf16[9,16,256]{2,1,0:T(8,128)(2,1)S(1)} %get-tuple-element.32), channel_id=1, source_target_pairs={{0,18},{2,4},{4,2},{6,20},{8,14},{10,24},{12,30},{14,8},{16,22},{1... | collective-permute-start | bytes 221192 | tf_op jit(solution)/shard_map/ppermute | solution.py:258
  19.7 2.0 %collective-permute-done.4.received = bf16[9,16,256]{2,1,0:T(8,128)(2,1)S(1)} collective-permute-done((bf16[9,16,256]{2,1,0:T(8,128)(2,1)S(1)}, bf16[9,16,256]{2,1,0:T(8,128)(2,1)S(1)}, u32[]{:S(2)}, u32[]{:S(2)}) %collective-permute-start.4) | collective-permute-done | bytes 73760 | tf_op jit(solution)/shard_map/ppermute | solution.py:258
  21.8 0.1 collective-permute-start.5
  21.9 1.1 %collective-permute-done.5 = f32[1,128]{1,0:T(1,128)S(1)} collective-permute-done((f32[1,128]{1,0:T(1,128)S(1)}, f32[1,128]{1,0:T(1,128)S(1)}, u32[]{:S(2)}, u32[]{:S(2)}) %collective-permute-start.5) | collective-permute-done | bytes 544 | tf_op jit(solution)/shard_map/ppermute | solution.py:253
  23.0 1.3 %collective-permute-start.6 = (f32[1,128]{1,0:T(1,128)S(1)}, f32[1,128]{1,0:T(1,128)S(1)}, u32[]{:S(2)}, u32[]{:S(2)}) collective-permute-start(f32[1,128]{1,0:T(1,128)S(1)} %add.3.squares), channel_id=1, source_target_pairs={{0,3},{1,2},{2,1},{3,0},{4,7},{5,6},{6,5},{7,4},{8,11},{9,10},{10,... | collective-permute-start | bytes 1544 | tf_op jit(solution)/shard_map/ppermute | solution.py:253
  24.3 1.7 %collective-permute-done.6.more = f32[1,128]{1,0:T(1,128)S(1)} collective-permute-done((f32[1,128]{1,0:T(1,128)S(1)}, f32[1,128]{1,0:T(1,128)S(1)}, u32[]{:S(2)}, u32[]{:S(2)}) %collective-permute-start.6) | collective-permute-done | bytes 544 | tf_op jit(solution)/shard_map/ppermute | solution.py:253
  26.0 0.7 %update.1 = f32[16,256]{1,0:T(8,128)} custom-call(bf16[16,256]{1,0:T(8,128)(2,1)S(1)} %get-tuple-element.21.mine, f32[16,256]{1,0:T(8,128)S(1)} %get-tuple-element.33.own, f32[1,128]{1,0:T(1,128)S(1)} %add.3.squares, f32[1,128]{1,0:T(1,128)S(1)} %collective-permute-done.6.more), custom_call_target="tpu_custom_call" | custom-call | tf_op jit(solution)/shard_map/update/pallas_call | solution.py:239
  (5 shorter events, 0.1 us)
Async XLA Ops:
  0.0 4.7 %copy-start = (bf16[1,1,64,128,128]{4,3,2,1,0:T(8,128)(2,1)S(1)}, bf16[1,1,64,128,128]{4,3,2,1,0:T(8,128)(2,1)}, u32[]{:S(2)}) copy-start(bf16[1,1,64,128,128]{4,3,2,1,0:T(8,128)(2,1)} %param.11) | copy-start | bytes 6291460
  0.0 4.7 %copy-start.1 = (bf16[2048,256]{1,0:T(8,128)(2,1)S(1)}, bf16[2048,256]{1,0:T(8,128)(2,1)}, u32[]{:S(2)}) copy-start(bf16[2048,256]{1,0:T(8,128)(2,1)} %users.1) | copy-start | bytes 3145732
  0.0 4.7 %copy-start.2 = (bf16[1,256,256]{2,1,0:T(8,128)(2,1)S(1)}, bf16[1,256,256]{2,1,0:T(8,128)(2,1)}, u32[]{:S(2)}) copy-start(bf16[1,256,256]{2,1,0:T(8,128)(2,1)} %param.10) | copy-start | bytes 393220
  0.0 4.7 %copy-start.3 = (bf16[1,1,2,128,128]{4,3,2,1,0:T(8,128)(2,1)S(1)}, bf16[1,1,2,128,128]{4,3,2,1,0:T(8,128)(2,1)}, u32[]{:S(2)}) copy-start(bf16[1,1,2,128,128]{4,3,2,1,0:T(8,128)(2,1)} %param.17) | copy-start | bytes 196612
  1.0 5.5 %collective-permute-start = (bf16[128,256]{1,0:T(8,128)(2,1)S(1)}, bf16[128,256]{1,0:T(8,128)(2,1)S(1)}, u32[]{:S(2)}, u32[]{:S(2)}) collective-permute-start(bf16[128,256]{1,0:T(8,128)(2,1)S(1)} %get-tuple-element.24), channel_id=1, source_target_pairs={{0,1},{1,0},{2,3},{3,2},{4,5},{5,4},{6,7},{7,6},{8,9},{9,8},{10,11... | collective-permute-start | bytes 196616 | tf_op jit(solution)/shard_map/ppermute | solution.py:253
  6.7 1.4 %collective-permute-start.1 = (f32[8,16,256]{2,1,0:T(8,128)S(1)}, f32[8,16,256]{2,1,0:T(8,128)S(1)}, u32[]{:S(2)}, u32[]{:S(2)}) collective-permute-start(f32[8,16,256]{2,1,0:T(8,128)S(1)} %graph_give.1), channel_id=1, source_target_pairs={{0,2},{2,0},{4,6},{6,4},{8,10},{10,8},{12,14},{14,12},{16,18},{18,... | collective-permute-start | bytes 393224 | tf_op jit(solution)/shard_map/ppermute | solution.py:253
  8.2 4.1 %collective-permute-start.2 = (bf16[12,16,256]{2,1,0:T(8,128)(2,1)S(1)}, bf16[12,16,256]{2,1,0:T(8,128)(2,1)S(1)}, u32[]{:S(2)}, u32[]{:S(2)}) collective-permute-start(bf16[12,16,256]{2,1,0:T(8,128)(2,1)S(1)} %get-tuple-element.28), channel_id=1, source_target_pairs={{0,6},{2,8},{4,14},{6,0},{8,2},{10,12},{12,10},{14,4},{16,26},{18,... | collective-permute-start | bytes 294920 | tf_op jit(solution)/shard_map/ppermute | solution.py:258
  12.3 4.0 %collective-permute-start.3 = (bf16[10,16,256]{2,1,0:T(8,128)(2,1)S(1)}, bf16[10,16,256]{2,1,0:T(8,128)(2,1)S(1)}, u32[]{:S(2)}, u32[]{:S(2)}) collective-permute-start(bf16[10,16,256]{2,1,0:T(8,128)(2,1)S(1)} %get-tuple-element.30), channel_id=1, source_target_pairs={{0,10},{2,16},{4,22},{6,12},{8,26},{10,0},{12,6},{14,28},{16,2},{1... | collective-permute-start | bytes 245768 | tf_op jit(solution)/shard_map/ppermute | solution.py:258
  16.4 5.4 %collective-permute-start.4 = (bf16[9,16,256]{2,1,0:T(8,128)(2,1)S(1)}, bf16[9,16,256]{2,1,0:T(8,128)(2,1)S(1)}, u32[]{:S(2)}, u32[]{:S(2)}) collective-permute-start(bf16[9,16,256]{2,1,0:T(8,128)(2,1)S(1)} %get-tuple-element.32), channel_id=1, source_target_pairs={{0,18},{2,4},{4,2},{6,20},{8,14},{10,24},{12,30},{14,8},{16,22},{1... | collective-permute-start | bytes 221192 | tf_op jit(solution)/shard_map/ppermute | solution.py:258
  21.8 1.2 %collective-permute-start.5 = (f32[1,128]{1,0:T(1,128)S(1)}, f32[1,128]{1,0:T(1,128)S(1)}, u32[]{:S(2)}, u32[]{:S(2)}) collective-permute-start(f32[1,128]{1,0:T(1,128)S(1)} %get-tuple-element.34), channel_id=1, source_target_pairs={{0,2},{2,0},{4,6},{6,4},{8,10},{10,8},{12,14},{14,12},{16,18},{18,... | collective-permute-start | bytes 1544 | tf_op jit(solution)/shard_map/ppermute | solution.py:253
  23.0 3.0 %collective-permute-start.6 = (f32[1,128]{1,0:T(1,128)S(1)}, f32[1,128]{1,0:T(1,128)S(1)}, u32[]{:S(2)}, u32[]{:S(2)}) collective-permute-start(f32[1,128]{1,0:T(1,128)S(1)} %add.3.squares), channel_id=1, source_target_pairs={{0,3},{1,2},{2,1},{3,0},{4,7},{5,6},{6,5},{7,4},{8,11},{9,10},{10,... | collective-permute-start | bytes 1544 | tf_op jit(solution)/shard_map/ppermute | solution.py:253

commit v7 on v6

--- a/solution.py
+++ b/solution.py
@@ -21,14 +21,16 @@
     return lax.dot_general(a, b, (dims, ((), ())), preferred_element_type=F32)
 
 
-def rating_kernel(half, user_idx_hbm, item_idx_hbm, target_hbm, count, users, items, ratings, similarity, near, *refs):
+def rating_kernel(half, user_idx_hbm, item_idx_hbm, target_hbm, count, list_hbm, users, items, ratings, similarity, *refs):
     grad_out, mine_ref, keep_far, give_far, give_out = refs[:5]
-    grad_ref, far_ref, user_idx, item_idx, target, items_t, pred, err, sem_s = refs[5:]
+    grad_ref, far_ref, user_idx, item_idx, target, send_list, items_t, pred, err, sem_s = refs[5:]
     n_tiles, tile = ratings.shape[0], ratings.shape[1]
     n_item = items.shape[0] // tile
     scalars = [
-        pltpu.make_async_copy(source, target, sem_s.at[n])
-        for n, (source, target) in enumerate(((target_hbm, target), (user_idx_hbm, user_idx), (item_idx_hbm, item_idx)))
+        pltpu.make_async_copy(source, place, sem_s.at[n])
+        for n, (source, place) in enumerate(
+            ((target_hbm, target), (list_hbm, send_list), (user_idx_hbm, user_idx), (item_idx_hbm, item_idx))
+        )
     ]
     for copy in scalars:
         copy.start()
@@ -82,7 +84,8 @@
         grad_out[...] = grad_ref[...]
         return
     rows = pl.ds(pl.multiple_of(target[col] * tile, tile), tile)
-    grad_ref[rows, :] += dot(similarity[col], near[...], ((1,), (0,)))
+    near = items[pl.ds(pl.multiple_of(send_list[col] * tile, tile), tile), :]
+    grad_ref[rows, :] += dot(similarity[col], near, ((1,), (0,)))
     me = lax.axis_index("rows")
     odd = sum((me >> b) & 1 for b in range(half.bit_length())) % 2
     for q in range(half):
@@ -97,7 +100,7 @@
             far_out[span, :] = far_ref[rows, :]
 
 
-def rating_part(user_idx, item_idx, count, target, users, items, ratings, similarity, near, own_rows, half):
+def rating_part(user_idx, item_idx, count, target, send_list, users, items, ratings, similarity, own_rows, half):
     tile = ratings.shape[1]
     n_item = items.shape[0] // tile
     smem = pl.BlockSpec(memory_space=pltpu.SMEM)
@@ -112,7 +115,7 @@
         functools.partial(rating_kernel, half),
         name="rating_part",
         out_shape=(rows, jax.ShapeDtypeStruct((own_rows, items.shape[1]), BF16), far_rows, far_rows, rows),
-        in_specs=[hbm] * 3 + [smem] + [vmem] * 5,
+        in_specs=[hbm] * 3 + [smem, hbm] + [vmem] * 4,
         out_specs=(vmem,) * 5,
         scratch_shapes=[
             pltpu.VMEM(items.shape, F32),
@@ -120,17 +123,18 @@
             pltpu.SMEM(user_idx.shape, jnp.int32),
             pltpu.SMEM(item_idx.shape, jnp.int32),
             pltpu.SMEM(target.shape, jnp.int32),
+            pltpu.SMEM(send_list.shape, jnp.int32),
             pltpu.VMEM((n_item, items.shape[1], tile), BF16),
             sums,
             sums,
-            pltpu.SemaphoreType.DMA((3,)),
+            pltpu.SemaphoreType.DMA((4,)),
         ],
         compiler_params=pltpu.CompilerParams(vmem_limit_bytes=limit * 1024 * 1024),
-    )(*in_hbm(user_idx, item_idx, target), count, users, items, ratings, similarity, near)
-
-
-def pick_kernel(send_list_hbm, items_hbm, kept, sent, send_list, items, sem_s, sems):
-    tile = kept.shape[0]
+    )(*in_hbm(user_idx, item_idx, target), count, *in_hbm(send_list), users, items, ratings, similarity)
+
+
+def pick_kernel(send_list_hbm, items_hbm, sent, send_list, items, sem_s, sems):
+    tile = sent.shape[0]
     copy_list = pltpu.make_async_copy(send_list_hbm, send_list, sem_s)
     copies = []
     for n in range(sems.shape[0]):
@@ -143,8 +147,7 @@
     for copy in copies:
         copy.wait()
     me = lax.axis_index("cols")
-    for out, col in ((kept, me), (sent, 1 - me)):
-        out[...] = items[pl.ds(pl.multiple_of(send_list[col] * tile, tile), tile), :]
+    sent[...] = items[pl.ds(pl.multiple_of(send_list[1 - me] * tile, tile), tile), :]
 
 
 def pick_panels(send_list, items, tile):
@@ -153,9 +156,9 @@
     return pl.pallas_call(
         pick_kernel,
         name="pick_panels",
-        out_shape=(panel, panel),
+        out_shape=panel,
         in_specs=[pl.BlockSpec(memory_space=pltpu.HBM)] * 2,
-        out_specs=(vmem, vmem),
+        out_specs=vmem,
         scratch_shapes=[
             pltpu.SMEM(send_list.shape, jnp.int32),
             pltpu.VMEM(items.shape, BF16),
@@ -271,17 +274,16 @@
     entries = n_cols * icount * rank
     by_hops = n_rows >= 4 and not n_rows & (n_rows - 1) and n_cols == 2 and slots == 1 and own_rows % 16 == 0
     if by_hops:
-        near, sent = pick_panels(send_list.reshape(-1), items[0], tile)
+        sent = pick_panels(send_list.reshape(-1), items[0], tile)
         far = swap(sent, "cols", 1)
     else:
         panels = items[0].reshape(-1, tile, rank)
         incoming = lax.all_to_all(panels[send_list[0, 0]], "cols", 0, 0, tiled=True)
         incoming = incoming.reshape(blocks, tile, rank)
-        near = jnp.zeros((tile, rank), BF16)
     half = n_rows // 2 if by_hops else 0
     grad, mine, keep_far, give_far, given = rating_part(
-        tile_users.reshape(-1), tile_items.reshape(-1), tile_count, target, users, items[0], ratings[0, 0],
-        similarity[0, 0, :2], near, own_rows, half,
+        tile_users.reshape(-1), tile_items.reshape(-1), tile_count, target, send_list[0, 0, :, 0], users, items[0],
+        ratings[0, 0], similarity[0, 0, :2], own_rows, half,
     )
     if not by_hops:
         contrib = jnp.einsum("kab,kbr->kar", similarity[0, 0], incoming, preferred_element_type=F32)

time: 26.9 us -> 26.9 us (level)
  starting transfers between devices: 11.1 us -> 10.5 us
  Pallas kernels: 3.94 us -> 4.24 us
  waiting for transfers between devices: 10.9 us -> 11.2 us
    ppermute x3, starting transfers between devices: 6.69 us -> 5.69 us  [hop(): lax.ppermute(value, 'rows', [(i, i ^ 1 ^ hops(size, parity(i))[b]) for i...]
    ppermute x3, waiting for transfers between devices: 6.86 us -> 7.47 us  [hop(): lax.ppermute(value, 'rows', [(i, i ^ 1 ^ hops(size, parity(i))[b]) for i...]
    ppermute x4, starting transfers between devices: 4.42 us -> 4.81 us  [swap(): return lax.ppermute(value, axis, [(i, i ^ bit) for i in range(size)])]
    pallas_call x1, Pallas kernels: 1.82 us -> 2.13 us  [rating_part(): pl.pallas_call(functools.partial(rating_kernel, half), name='rating_part'...]
    ppermute x4, waiting for transfers between devices: 3.99 us -> 3.69 us  [swap(): return lax.ppermute(value, axis, [(i, i ^ bit) for i in range(size)])]
  transfers between devices with their start and end apart: 7 -> 7, of which waited for: 6 -> 6; matrix products, arithmetic and copies ran while one was open for 0% -> 0% of each run, Pallas kernels for 7% -> 9%
where the time goes in v7:
time: 26.9 us; the launch traced here: 26.7 us
  waiting for transfers between devices  11.2 us (42%)
  starting transfers between devices  10.5 us (39%)
  Pallas kernels  4.24 us (16%)
  between operations  0.74 us (3%)
    ppermute x3, waiting for transfers between devices, hop(): lax.ppermute(value, 'rows', [(i, i ^ 1 ^ hops(size, parity(i))[b]) for i...  7.47 us
    ppermute x3, starting transfers between devices, hop(): lax.ppermute(value, 'rows', [(i, i ^ 1 ^ hops(size, parity(i))[b]) for i...  5.69 us
    ppermute x4, starting transfers between devices, swap(): return lax.ppermute(value, axis, [(i, i ^ bit) for i in range(size)])  4.81 us
    ppermute x4, waiting for transfers between devices, swap(): return lax.ppermute(value, axis, [(i, i ^ bit) for i in range(size)])  3.69 us
    pallas_call x1, Pallas kernels, rating_part(): pl.pallas_call(functools.partial(rating_kernel, half), name='rating_part'...  2.13 us
    pallas_call x7, Pallas kernels, local_call(): pl.pallas_call(kernel, name=name, out_shape=out_shape, in_specs=[vmem] *...  1.11 us
    pallas_call x1, Pallas kernels, pick_panels(): pl.pallas_call(pick_kernel, name='pick_panels', out_shape=panel, in_specs...  1 us
  transfers between devices with their start and end apart: 7, of which 6 were waited for; matrix products, arithmetic and copies ran while one was open for 0% of the time, Pallas kernels for 9%

profile of v7, /device:TPU:0, one launch (start us, length us, event | category | flops | bytes accessed | tf_op | source)
XLA Modules:
  0.0 26.7 jit_solution(9110038978747380372)
XLA Ops:
  0.0 0.0 copy-start
  0.0 0.0 copy-start.1
  0.0 0.0 copy-start.2
  0.0 0.0 copy-start.3
  0.0 1.0 %pick_panels.1 = bf16[128,256]{1,0:T(8,128)(2,1)S(1)} custom-call(s32[2]{0:T(128)} %bitcast.15, bf16[256,256]{1,0:T(8,128)(2,1)} %bitcast.9), custom_call_target="tpu_custom_call" | custom-call | flops 10000000000 | bytes 30000000 | tf_op jit(solution)/shard_map/pick_panels/pallas_call | solution.py:156
  1.0 3.0 %collective-permute-start = (bf16[128,256]{1,0:T(8,128)(2,1)S(1)}, bf16[128,256]{1,0:T(8,128)(2,1)S(1)}, u32[]{:S(2)}, u32[]{:S(2)}) collective-permute-start(bf16[128,256]{1,0:T(8,128)(2,1)S(1)} %pick_panels.1), channel_id=1, source_target_pairs={{0,1},{1,0},{2,3},{3,2},{4,5},{5,4},{6,7},{7,6},{8,9},{9,8},{10,11... | collective-permute-start | bytes 196616 | tf_op jit(solution)/shard_map/ppermute | solution.py:256
  4.7 0.0 copy-done
  4.7 0.0 copy-done.1
  4.7 0.0 copy-done.2
  4.7 0.0 copy-done.3
  4.7 2.1 %rating_part.1 = (f32[128,256]{1,0:T(8,128)S(1)}, bf16[16,256]{1,0:T(8,128)(2,1)S(1)}, bf16[128,128]{1,0:T(8,128)(2,1)S(1)}, bf16[128,128]{1,0:T(8,128)(2,1)S(1)}, f32[128,256]{1,0:T(8,128)S(1)}) custom-call(s32[64]{0:T(128)} %bitcast.12, s32[64]{0:T(128)} %bitcast.13, s32[2]{0:T(128)} %bitcast.14, s32[1,1]{1,0:T(1,128)S(6)} %copy.10.count, s32[2]{0:T(128)} %bitcast.16, ...), custom_call_target="tpu_custom_call" | custom-call | tf_op jit(solution)/shard_map/rating_part/pallas_call | solution.py:114
  6.9 0.0 collective-permute-done.far
  6.9 0.1 graph_give.1
  7.0 0.1 collective-permute-start.1
  7.1 0.2 graph_keep.1.keep
  7.3 1.2 %collective-permute-done.1.received = f32[8,16,256]{2,1,0:T(8,128)S(1)} collective-permute-done((f32[8,16,256]{2,1,0:T(8,128)S(1)}, f32[8,16,256]{2,1,0:T(8,128)S(1)}, u32[]{:S(2)}, u32[]{:S(2)}) %collective-permute-start.1) | collective-permute-done | bytes 131104 | tf_op jit(solution)/shard_map/ppermute | solution.py:256
  8.5 1.3 %collective-permute-start.2 = (bf16[12,16,256]{2,1,0:T(8,128)(2,1)S(1)}, bf16[12,16,256]{2,1,0:T(8,128)(2,1)S(1)}, u32[]{:S(2)}, u32[]{:S(2)}) collective-permute-start(bf16[12,16,256]{2,1,0:T(8,128)(2,1)S(1)} %get-tuple-element.24), channel_id=1, source_target_pairs={{0,6},{2,8},{4,14},{6,0},{8,2},{10,12},{12,10},{14,4},{16,26},{18,... | collective-permute-start | bytes 294920 | tf_op jit(solution)/shard_map/ppermute | solution.py:261
  9.7 2.8 %collective-permute-done.2.received = bf16[12,16,256]{2,1,0:T(8,128)(2,1)S(1)} collective-permute-done((bf16[12,16,256]{2,1,0:T(8,128)(2,1)S(1)}, bf16[12,16,256]{2,1,0:T(8,128)(2,1)S(1)}, u32[]{:S(2)}, u32[]{:S(2)}) %collective-permute-start.2) | collective-permute-done | bytes 98336 | tf_op jit(solution)/shard_map/ppermute | solution.py:261
  12.6 1.3 %collective-permute-start.3 = (bf16[10,16,256]{2,1,0:T(8,128)(2,1)S(1)}, bf16[10,16,256]{2,1,0:T(8,128)(2,1)S(1)}, u32[]{:S(2)}, u32[]{:S(2)}) collective-permute-start(bf16[10,16,256]{2,1,0:T(8,128)(2,1)S(1)} %get-tuple-element.26), channel_id=1, source_target_pairs={{0,10},{2,16},{4,22},{6,12},{8,26},{10,0},{12,6},{14,28},{16,2},{1... | collective-permute-start | bytes 245768 | tf_op jit(solution)/shard_map/ppermute | solution.py:261
  13.9 2.6 %collective-permute-done.3.received = bf16[10,16,256]{2,1,0:T(8,128)(2,1)S(1)} collective-permute-done((bf16[10,16,256]{2,1,0:T(8,128)(2,1)S(1)}, bf16[10,16,256]{2,1,0:T(8,128)(2,1)S(1)}, u32[]{:S(2)}, u32[]{:S(2)}) %collective-permute-start.3) | collective-permute-done | bytes 81952 | tf_op jit(solution)/shard_map/ppermute | solution.py:261
  16.6 3.1 %collective-permute-start.4 = (bf16[9,16,256]{2,1,0:T(8,128)(2,1)S(1)}, bf16[9,16,256]{2,1,0:T(8,128)(2,1)S(1)}, u32[]{:S(2)}, u32[]{:S(2)}) collective-permute-start(bf16[9,16,256]{2,1,0:T(8,128)(2,1)S(1)} %get-tuple-element.28), channel_id=1, source_target_pairs={{0,18},{2,4},{4,2},{6,20},{8,14},{10,24},{12,30},{14,8},{16,22},{1... | collective-permute-start | bytes 221192 | tf_op jit(solution)/shard_map/ppermute | solution.py:261
  19.6 2.0 %collective-permute-done.4.received = bf16[9,16,256]{2,1,0:T(8,128)(2,1)S(1)} collective-permute-done((bf16[9,16,256]{2,1,0:T(8,128)(2,1)S(1)}, bf16[9,16,256]{2,1,0:T(8,128)(2,1)S(1)}, u32[]{:S(2)}, u32[]{:S(2)}) %collective-permute-start.4) | collective-permute-done | bytes 73760 | tf_op jit(solution)/shard_map/ppermute | solution.py:261
  21.7 0.4 %collective-permute-start.5 = (f32[1,128]{1,0:T(1,128)S(1)}, f32[1,128]{1,0:T(1,128)S(1)}, u32[]{:S(2)}, u32[]{:S(2)}) collective-permute-start(f32[1,128]{1,0:T(1,128)S(1)} %get-tuple-element.30), channel_id=1, source_target_pairs={{0,2},{2,0},{4,6},{6,4},{8,10},{10,8},{12,14},{14,12},{16,18},{18,... | collective-permute-start | bytes 1544 | tf_op jit(solution)/shard_map/ppermute | solution.py:256
  22.2 0.8 %collective-permute-done.5 = f32[1,128]{1,0:T(1,128)S(1)} collective-permute-done((f32[1,128]{1,0:T(1,128)S(1)}, f32[1,128]{1,0:T(1,128)S(1)}, u32[]{:S(2)}, u32[]{:S(2)}) %collective-permute-start.5) | collective-permute-done | bytes 544 | tf_op jit(solution)/shard_map/ppermute | solution.py:256
  23.0 1.3 %collective-permute-start.6 = (f32[1,128]{1,0:T(1,128)S(1)}, f32[1,128]{1,0:T(1,128)S(1)}, u32[]{:S(2)}, u32[]{:S(2)}) collective-permute-start(f32[1,128]{1,0:T(1,128)S(1)} %add.3.squares), channel_id=1, source_target_pairs={{0,3},{1,2},{2,1},{3,0},{4,7},{5,6},{6,5},{7,4},{8,11},{9,10},{10,... | collective-permute-start | bytes 1544 | tf_op jit(solution)/shard_map/ppermute | solution.py:256
  24.3 1.7 %collective-permute-done.6.more = f32[1,128]{1,0:T(1,128)S(1)} collective-permute-done((f32[1,128]{1,0:T(1,128)S(1)}, f32[1,128]{1,0:T(1,128)S(1)}, u32[]{:S(2)}, u32[]{:S(2)}) %collective-permute-start.6) | collective-permute-done | bytes 544 | tf_op jit(solution)/shard_map/ppermute | solution.py:256
  26.0 0.7 %update.1 = f32[16,256]{1,0:T(8,128)} custom-call(bf16[16,256]{1,0:T(8,128)(2,1)S(1)} %get-tuple-element.18.mine, f32[16,256]{1,0:T(8,128)S(1)} %get-tuple-element.29.own, f32[1,128]{1,0:T(1,128)S(1)} %add.3.squares, f32[1,128]{1,0:T(1,128)S(1)} %collective-permute-done.6.more), custom_call_target="tpu_custom_call" | custom-call | tf_op jit(solution)/shard_map/update/pallas_call | solution.py:242
  (5 shorter events, 0.1 us)
Async XLA Ops:
  0.0 4.7 %copy-start = (bf16[1,1,64,128,128]{4,3,2,1,0:T(8,128)(2,1)S(1)}, bf16[1,1,64,128,128]{4,3,2,1,0:T(8,128)(2,1)}, u32[]{:S(2)}) copy-start(bf16[1,1,64,128,128]{4,3,2,1,0:T(8,128)(2,1)} %param.11) | copy-start | bytes 6291460
  0.0 4.7 %copy-start.1 = (bf16[2048,256]{1,0:T(8,128)(2,1)S(1)}, bf16[2048,256]{1,0:T(8,128)(2,1)}, u32[]{:S(2)}) copy-start(bf16[2048,256]{1,0:T(8,128)(2,1)} %users.1) | copy-start | bytes 3145732
  0.0 4.7 %copy-start.2 = (bf16[1,256,256]{2,1,0:T(8,128)(2,1)S(1)}, bf16[1,256,256]{2,1,0:T(8,128)(2,1)}, u32[]{:S(2)}) copy-start(bf16[1,256,256]{2,1,0:T(8,128)(2,1)} %param.10) | copy-start | bytes 393220
  0.0 4.7 %copy-start.3 = (bf16[1,1,2,128,128]{4,3,2,1,0:T(8,128)(2,1)S(1)}, bf16[1,1,2,128,128]{4,3,2,1,0:T(8,128)(2,1)}, u32[]{:S(2)}) copy-start(bf16[1,1,2,128,128]{4,3,2,1,0:T(8,128)(2,1)} %param.17) | copy-start | bytes 196612
  1.0 5.8 %collective-permute-start = (bf16[128,256]{1,0:T(8,128)(2,1)S(1)}, bf16[128,256]{1,0:T(8,128)(2,1)S(1)}, u32[]{:S(2)}, u32[]{:S(2)}) collective-permute-start(bf16[128,256]{1,0:T(8,128)(2,1)S(1)} %pick_panels.1), channel_id=1, source_target_pairs={{0,1},{1,0},{2,3},{3,2},{4,5},{5,4},{6,7},{7,6},{8,9},{9,8},{10,11... | collective-permute-start | bytes 196616 | tf_op jit(solution)/shard_map/ppermute | solution.py:256
  7.0 1.4 %collective-permute-start.1 = (f32[8,16,256]{2,1,0:T(8,128)S(1)}, f32[8,16,256]{2,1,0:T(8,128)S(1)}, u32[]{:S(2)}, u32[]{:S(2)}) collective-permute-start(f32[8,16,256]{2,1,0:T(8,128)S(1)} %graph_give.1), channel_id=1, source_target_pairs={{0,2},{2,0},{4,6},{6,4},{8,10},{10,8},{12,14},{14,12},{16,18},{18,... | collective-permute-start | bytes 393224 | tf_op jit(solution)/shard_map/ppermute | solution.py:256
  8.5 4.1 %collective-permute-start.2 = (bf16[12,16,256]{2,1,0:T(8,128)(2,1)S(1)}, bf16[12,16,256]{2,1,0:T(8,128)(2,1)S(1)}, u32[]{:S(2)}, u32[]{:S(2)}) collective-permute-start(bf16[12,16,256]{2,1,0:T(8,128)(2,1)S(1)} %get-tuple-element.24), channel_id=1, source_target_pairs={{0,6},{2,8},{4,14},{6,0},{8,2},{10,12},{12,10},{14,4},{16,26},{18,... | collective-permute-start | bytes 294920 | tf_op jit(solution)/shard_map/ppermute | solution.py:261
  12.6 3.9 %collective-permute-start.3 = (bf16[10,16,256]{2,1,0:T(8,128)(2,1)S(1)}, bf16[10,16,256]{2,1,0:T(8,128)(2,1)S(1)}, u32[]{:S(2)}, u32[]{:S(2)}) collective-permute-start(bf16[10,16,256]{2,1,0:T(8,128)(2,1)S(1)} %get-tuple-element.26), channel_id=1, source_target_pairs={{0,10},{2,16},{4,22},{6,12},{8,26},{10,0},{12,6},{14,28},{16,2},{1... | collective-permute-start | bytes 245768 | tf_op jit(solution)/shard_map/ppermute | solution.py:261
  16.6 5.1 %collective-permute-start.4 = (bf16[9,16,256]{2,1,0:T(8,128)(2,1)S(1)}, bf16[9,16,256]{2,1,0:T(8,128)(2,1)S(1)}, u32[]{:S(2)}, u32[]{:S(2)}) collective-permute-start(bf16[9,16,256]{2,1,0:T(8,128)(2,1)S(1)} %get-tuple-element.28), channel_id=1, source_target_pairs={{0,18},{2,4},{4,2},{6,20},{8,14},{10,24},{12,30},{14,8},{16,22},{1... | collective-permute-start | bytes 221192 | tf_op jit(solution)/shard_map/ppermute | solution.py:261
  21.7 1.3 %collective-permute-start.5 = (f32[1,128]{1,0:T(1,128)S(1)}, f32[1,128]{1,0:T(1,128)S(1)}, u32[]{:S(2)}, u32[]{:S(2)}) collective-permute-start(f32[1,128]{1,0:T(1,128)S(1)} %get-tuple-element.30), channel_id=1, source_target_pairs={{0,2},{2,0},{4,6},{6,4},{8,10},{10,8},{12,14},{14,12},{16,18},{18,... | collective-permute-start | bytes 1544 | tf_op jit(solution)/shard_map/ppermute | solution.py:256
  23.0 3.0 %collective-permute-start.6 = (f32[1,128]{1,0:T(1,128)S(1)}, f32[1,128]{1,0:T(1,128)S(1)}, u32[]{:S(2)}, u32[]{:S(2)}) collective-permute-start(f32[1,128]{1,0:T(1,128)S(1)} %add.3.squares), channel_id=1, source_target_pairs={{0,3},{1,2},{2,1},{3,0},{4,7},{5,6},{6,5},{7,4},{8,11},{9,10},{10,... | collective-permute-start | bytes 1544 | tf_op jit(solution)/shard_map/ppermute | solution.py:256

commit v8 on v7

--- a/solution.py
+++ b/solution.py
@@ -309,9 +309,9 @@
         functools.partial(last_kernel, half // 2), "add_last", (total, hop(sent, n_hops - 1)),
         (jax.ShapeDtypeStruct((own_rows, rank), F32), jax.ShapeDtypeStruct((1, 128), F32)),
     )
-    squares = squares + swap(squares, "rows", 1)
+    squares = squares + swap(squares, ("rows", "cols"), 3)
     updated = local_call(
-        functools.partial(update_kernel, entries), "update", (mine, own, squares, swap(squares, ("rows", "cols"), 3)),
+        functools.partial(update_kernel, entries), "update", (mine, own, squares, swap(squares, "rows", 1)),
         jax.ShapeDtypeStruct((own_rows, rank), F32),
     )
     return updated[None]

time: 26.9 us -> 27.1 us (level)
    ppermute x3, starting transfers between devices: 5.69 us -> 5.39 us  [hop(): lax.ppermute(value, 'rows', [(i, i ^ 1 ^ hops(size, parity(i))[b]) for i...]
    ppermute x4, starting transfers between devices: 4.81 us -> 5.1 us  [swap(): return lax.ppermute(value, axis, [(i, i ^ bit) for i in range(size)])]
where the time goes in v8:
time: 27.1 us; the launch traced here: 26.9 us
  waiting for transfers between devices  11.3 us (42%)
  starting transfers between devices  10.5 us (39%)
  Pallas kernels  4.36 us (16%)
  between operations  0.74 us (3%)
    ppermute x3, waiting for transfers between devices, hop(): lax.ppermute(value, 'rows', [(i, i ^ 1 ^ hops(size, parity(i))[b]) for i...  7.67 us
    ppermute x3, starting transfers between devices, hop(): lax.ppermute(value, 'rows', [(i, i ^ 1 ^ hops(size, parity(i))[b]) for i...  5.39 us
    ppermute x4, starting transfers between devices, swap(): return lax.ppermute(value, axis, [(i, i ^ bit) for i in range(size)])  5.1 us
    ppermute x4, waiting for transfers between devices, swap(): return lax.ppermute(value, axis, [(i, i ^ bit) for i in range(size)])  3.64 us
    pallas_call x1, Pallas kernels, rating_part(): pl.pallas_call(functools.partial(rating_kernel, half), name='rating_part'...  2.24 us
    pallas_call x7, Pallas kernels, local_call(): pl.pallas_call(kernel, name=name, out_shape=out_shape, in_specs=[vmem] *...  1.11 us
    pallas_call x1, Pallas kernels, pick_panels(): pl.pallas_call(pick_kernel, name='pick_panels', out_shape=panel, in_specs...  1 us
  transfers between devices with their start and end apart: 7, of which 6 were waited for; matrix products, arithmetic and copies ran while one was open for 0% of the time, Pallas kernels for 9%

profile of v8, /device:TPU:0, one launch (start us, length us, event | category | flops | bytes accessed | tf_op | source)
XLA Modules:
  0.0 26.9 jit_solution(10751469288209281420)
XLA Ops:
  0.0 0.0 copy-start
  0.0 0.0 copy-start.1
  0.0 0.0 copy-start.2
  0.0 0.0 copy-start.3
  0.0 1.0 %pick_panels.1 = bf16[128,256]{1,0:T(8,128)(2,1)S(1)} custom-call(s32[2]{0:T(128)} %bitcast.15, bf16[256,256]{1,0:T(8,128)(2,1)} %bitcast.9), custom_call_target="tpu_custom_call" | custom-call | flops 10000000000 | bytes 30000000 | tf_op jit(solution)/shard_map/pick_panels/pallas_call | solution.py:156
  1.0 3.0 %collective-permute-start = (bf16[128,256]{1,0:T(8,128)(2,1)S(1)}, bf16[128,256]{1,0:T(8,128)(2,1)S(1)}, u32[]{:S(2)}, u32[]{:S(2)}) collective-permute-start(bf16[128,256]{1,0:T(8,128)(2,1)S(1)} %pick_panels.1), channel_id=1, source_target_pairs={{0,1},{1,0},{2,3},{3,2},{4,5},{5,4},{6,7},{7,6},{8,9},{9,8},{10,11... | collective-permute-start | bytes 196616 | tf_op jit(solution)/shard_map/ppermute | solution.py:256
  4.7 0.0 copy-done
  4.7 0.0 copy-done.1
  4.7 0.0 copy-done.2
  4.7 0.0 copy-done.3
  4.7 2.2 %rating_part.1 = (f32[128,256]{1,0:T(8,128)S(1)}, bf16[16,256]{1,0:T(8,128)(2,1)S(1)}, bf16[128,128]{1,0:T(8,128)(2,1)S(1)}, bf16[128,128]{1,0:T(8,128)(2,1)S(1)}, f32[128,256]{1,0:T(8,128)S(1)}) custom-call(s32[64]{0:T(128)} %bitcast.12, s32[64]{0:T(128)} %bitcast.13, s32[2]{0:T(128)} %bitcast.14, s32[1,1]{1,0:T(1,128)S(6)} %copy.10.count, s32[2]{0:T(128)} %bitcast.16, ...), custom_call_target="tpu_custom_call" | custom-call | tf_op jit(solution)/shard_map/rating_part/pallas_call | solution.py:114
  7.0 0.0 collective-permute-done.far
  7.0 0.1 graph_give.1
  7.1 0.1 collective-permute-start.1
  7.2 0.2 graph_keep.1.keep
  7.4 1.2 %collective-permute-done.1.received = f32[8,16,256]{2,1,0:T(8,128)S(1)} collective-permute-done((f32[8,16,256]{2,1,0:T(8,128)S(1)}, f32[8,16,256]{2,1,0:T(8,128)S(1)}, u32[]{:S(2)}, u32[]{:S(2)}) %collective-permute-start.1) | collective-permute-done | bytes 131104 | tf_op jit(solution)/shard_map/ppermute | solution.py:256
  8.6 1.2 %collective-permute-start.2 = (bf16[12,16,256]{2,1,0:T(8,128)(2,1)S(1)}, bf16[12,16,256]{2,1,0:T(8,128)(2,1)S(1)}, u32[]{:S(2)}, u32[]{:S(2)}) collective-permute-start(bf16[12,16,256]{2,1,0:T(8,128)(2,1)S(1)} %get-tuple-element.24), channel_id=1, source_target_pairs={{0,6},{2,8},{4,14},{6,0},{8,2},{10,12},{12,10},{14,4},{16,26},{18,... | collective-permute-start | bytes 294920 | tf_op jit(solution)/shard_map/ppermute | solution.py:261
  9.7 2.9 %collective-permute-done.2.received = bf16[12,16,256]{2,1,0:T(8,128)(2,1)S(1)} collective-permute-done((bf16[12,16,256]{2,1,0:T(8,128)(2,1)S(1)}, bf16[12,16,256]{2,1,0:T(8,128)(2,1)S(1)}, u32[]{:S(2)}, u32[]{:S(2)}) %collective-permute-start.2) | collective-permute-done | bytes 98336 | tf_op jit(solution)/shard_map/ppermute | solution.py:261
  12.7 1.2 %collective-permute-start.3 = (bf16[10,16,256]{2,1,0:T(8,128)(2,1)S(1)}, bf16[10,16,256]{2,1,0:T(8,128)(2,1)S(1)}, u32[]{:S(2)}, u32[]{:S(2)}) collective-permute-start(bf16[10,16,256]{2,1,0:T(8,128)(2,1)S(1)} %get-tuple-element.26), channel_id=1, source_target_pairs={{0,10},{2,16},{4,22},{6,12},{8,26},{10,0},{12,6},{14,28},{16,2},{1... | collective-permute-start | bytes 245768 | tf_op jit(solution)/shard_map/ppermute | solution.py:261
  14.0 2.7 %collective-permute-done.3.received = bf16[10,16,256]{2,1,0:T(8,128)(2,1)S(1)} collective-permute-done((bf16[10,16,256]{2,1,0:T(8,128)(2,1)S(1)}, bf16[10,16,256]{2,1,0:T(8,128)(2,1)S(1)}, u32[]{:S(2)}, u32[]{:S(2)}) %collective-permute-start.3) | collective-permute-done | bytes 81952 | tf_op jit(solution)/shard_map/ppermute | solution.py:261
  16.7 3.0 %collective-permute-start.4 = (bf16[9,16,256]{2,1,0:T(8,128)(2,1)S(1)}, bf16[9,16,256]{2,1,0:T(8,128)(2,1)S(1)}, u32[]{:S(2)}, u32[]{:S(2)}) collective-permute-start(bf16[9,16,256]{2,1,0:T(8,128)(2,1)S(1)} %get-tuple-element.28), channel_id=1, source_target_pairs={{0,18},{2,4},{4,2},{6,20},{8,14},{10,24},{12,30},{14,8},{16,22},{1... | collective-permute-start | bytes 221192 | tf_op jit(solution)/shard_map/ppermute | solution.py:261
  19.7 2.0 %collective-permute-done.4.received = bf16[9,16,256]{2,1,0:T(8,128)(2,1)S(1)} collective-permute-done((bf16[9,16,256]{2,1,0:T(8,128)(2,1)S(1)}, bf16[9,16,256]{2,1,0:T(8,128)(2,1)S(1)}, u32[]{:S(2)}, u32[]{:S(2)}) %collective-permute-start.4) | collective-permute-done | bytes 73760 | tf_op jit(solution)/shard_map/ppermute | solution.py:261
  21.8 1.4 %collective-permute-start.5 = (f32[1,128]{1,0:T(1,128)S(1)}, f32[1,128]{1,0:T(1,128)S(1)}, u32[]{:S(2)}, u32[]{:S(2)}) collective-permute-start(f32[1,128]{1,0:T(1,128)S(1)} %get-tuple-element.30), channel_id=1, source_target_pairs={{0,3},{1,2},{2,1},{3,0},{4,7},{5,6},{6,5},{7,4},{8,11},{9,10},{10,... | collective-permute-start | bytes 1544 | tf_op jit(solution)/shard_map/ppermute | solution.py:256
  23.1 1.6 %collective-permute-done.5 = f32[1,128]{1,0:T(1,128)S(1)} collective-permute-done((f32[1,128]{1,0:T(1,128)S(1)}, f32[1,128]{1,0:T(1,128)S(1)}, u32[]{:S(2)}, u32[]{:S(2)}) %collective-permute-start.5) | collective-permute-done | bytes 544 | tf_op jit(solution)/shard_map/ppermute | solution.py:256
  24.8 0.6 %collective-permute-start.6 = (f32[1,128]{1,0:T(1,128)S(1)}, f32[1,128]{1,0:T(1,128)S(1)}, u32[]{:S(2)}, u32[]{:S(2)}) collective-permute-start(f32[1,128]{1,0:T(1,128)S(1)} %add.3.squares), channel_id=1, source_target_pairs={{0,2},{2,0},{4,6},{6,4},{8,10},{10,8},{12,14},{14,12},{16,18},{18,... | collective-permute-start | bytes 1544 | tf_op jit(solution)/shard_map/ppermute | solution.py:256
  25.4 0.8 %collective-permute-done.6.more = f32[1,128]{1,0:T(1,128)S(1)} collective-permute-done((f32[1,128]{1,0:T(1,128)S(1)}, f32[1,128]{1,0:T(1,128)S(1)}, u32[]{:S(2)}, u32[]{:S(2)}) %collective-permute-start.6) | collective-permute-done | bytes 544 | tf_op jit(solution)/shard_map/ppermute | solution.py:256
  26.2 0.7 %update.1 = f32[16,256]{1,0:T(8,128)} custom-call(bf16[16,256]{1,0:T(8,128)(2,1)S(1)} %get-tuple-element.18.mine, f32[16,256]{1,0:T(8,128)S(1)} %get-tuple-element.29.own, f32[1,128]{1,0:T(1,128)S(1)} %add.3.squares, f32[1,128]{1,0:T(1,128)S(1)} %collective-permute-done.6.more), custom_call_target="tpu_custom_call" | custom-call | tf_op jit(solution)/shard_map/update/pallas_call | solution.py:242
  (5 shorter events, 0.1 us)
Async XLA Ops:
  0.0 4.7 %copy-start = (bf16[1,1,64,128,128]{4,3,2,1,0:T(8,128)(2,1)S(1)}, bf16[1,1,64,128,128]{4,3,2,1,0:T(8,128)(2,1)}, u32[]{:S(2)}) copy-start(bf16[1,1,64,128,128]{4,3,2,1,0:T(8,128)(2,1)} %param.11) | copy-start | bytes 6291460
  0.0 4.7 %copy-start.1 = (bf16[2048,256]{1,0:T(8,128)(2,1)S(1)}, bf16[2048,256]{1,0:T(8,128)(2,1)}, u32[]{:S(2)}) copy-start(bf16[2048,256]{1,0:T(8,128)(2,1)} %users.1) | copy-start | bytes 3145732
  0.0 4.7 %copy-start.2 = (bf16[1,256,256]{2,1,0:T(8,128)(2,1)S(1)}, bf16[1,256,256]{2,1,0:T(8,128)(2,1)}, u32[]{:S(2)}) copy-start(bf16[1,256,256]{2,1,0:T(8,128)(2,1)} %param.10) | copy-start | bytes 393220
  0.0 4.7 %copy-start.3 = (bf16[1,1,2,128,128]{4,3,2,1,0:T(8,128)(2,1)S(1)}, bf16[1,1,2,128,128]{4,3,2,1,0:T(8,128)(2,1)}, u32[]{:S(2)}) copy-start(bf16[1,1,2,128,128]{4,3,2,1,0:T(8,128)(2,1)} %param.17) | copy-start | bytes 196612
  1.0 6.0 %collective-permute-start = (bf16[128,256]{1,0:T(8,128)(2,1)S(1)}, bf16[128,256]{1,0:T(8,128)(2,1)S(1)}, u32[]{:S(2)}, u32[]{:S(2)}) collective-permute-start(bf16[128,256]{1,0:T(8,128)(2,1)S(1)} %pick_panels.1), channel_id=1, source_target_pairs={{0,1},{1,0},{2,3},{3,2},{4,5},{5,4},{6,7},{7,6},{8,9},{9,8},{10,11... | collective-permute-start | bytes 196616 | tf_op jit(solution)/shard_map/ppermute | solution.py:256
  7.1 1.4 %collective-permute-start.1 = (f32[8,16,256]{2,1,0:T(8,128)S(1)}, f32[8,16,256]{2,1,0:T(8,128)S(1)}, u32[]{:S(2)}, u32[]{:S(2)}) collective-permute-start(f32[8,16,256]{2,1,0:T(8,128)S(1)} %graph_give.1), channel_id=1, source_target_pairs={{0,2},{2,0},{4,6},{6,4},{8,10},{10,8},{12,14},{14,12},{16,18},{18,... | collective-permute-start | bytes 393224 | tf_op jit(solution)/shard_map/ppermute | solution.py:256
  8.6 4.1 %collective-permute-start.2 = (bf16[12,16,256]{2,1,0:T(8,128)(2,1)S(1)}, bf16[12,16,256]{2,1,0:T(8,128)(2,1)S(1)}, u32[]{:S(2)}, u32[]{:S(2)}) collective-permute-start(bf16[12,16,256]{2,1,0:T(8,128)(2,1)S(1)} %get-tuple-element.24), channel_id=1, source_target_pairs={{0,6},{2,8},{4,14},{6,0},{8,2},{10,12},{12,10},{14,4},{16,26},{18,... | collective-permute-start | bytes 294920 | tf_op jit(solution)/shard_map/ppermute | solution.py:261
  12.7 3.9 %collective-permute-start.3 = (bf16[10,16,256]{2,1,0:T(8,128)(2,1)S(1)}, bf16[10,16,256]{2,1,0:T(8,128)(2,1)S(1)}, u32[]{:S(2)}, u32[]{:S(2)}) collective-permute-start(bf16[10,16,256]{2,1,0:T(8,128)(2,1)S(1)} %get-tuple-element.26), channel_id=1, source_target_pairs={{0,10},{2,16},{4,22},{6,12},{8,26},{10,0},{12,6},{14,28},{16,2},{1... | collective-permute-start | bytes 245768 | tf_op jit(solution)/shard_map/ppermute | solution.py:261
  16.7 5.0 %collective-permute-start.4 = (bf16[9,16,256]{2,1,0:T(8,128)(2,1)S(1)}, bf16[9,16,256]{2,1,0:T(8,128)(2,1)S(1)}, u32[]{:S(2)}, u32[]{:S(2)}) collective-permute-start(bf16[9,16,256]{2,1,0:T(8,128)(2,1)S(1)} %get-tuple-element.28), channel_id=1, source_target_pairs={{0,18},{2,4},{4,2},{6,20},{8,14},{10,24},{12,30},{14,8},{16,22},{1... | collective-permute-start | bytes 221192 | tf_op jit(solution)/shard_map/ppermute | solution.py:261
  21.8 3.0 %collective-permute-start.5 = (f32[1,128]{1,0:T(1,128)S(1)}, f32[1,128]{1,0:T(1,128)S(1)}, u32[]{:S(2)}, u32[]{:S(2)}) collective-permute-start(f32[1,128]{1,0:T(1,128)S(1)} %get-tuple-element.30), channel_id=1, source_target_pairs={{0,3},{1,2},{2,1},{3,0},{4,7},{5,6},{6,5},{7,4},{8,11},{9,10},{10,... | collective-permute-start | bytes 1544 | tf_op jit(solution)/shard_map/ppermute | solution.py:256
  24.8 1.4 %collective-permute-start.6 = (f32[1,128]{1,0:T(1,128)S(1)}, f32[1,128]{1,0:T(1,128)S(1)}, u32[]{:S(2)}, u32[]{:S(2)}) collective-permute-start(f32[1,128]{1,0:T(1,128)S(1)} %add.3.squares), channel_id=1, source_target_pairs={{0,2},{2,0},{4,6},{6,4},{8,10},{10,8},{12,14},{14,12},{16,18},{18,... | collective-permute-start | bytes 1544 | tf_op jit(solution)/shard_map/ppermute | solution.py:256

commit v9 on v7

--- a/solution.py
+++ b/solution.py
@@ -176,7 +176,7 @@
 
 def hops(n_rows, odd):
     bits = [1 << b for b in range(1, n_rows.bit_length() - 1)]
-    return bits[1:] + bits[:1] if odd else bits
+    return bits[1::-1] + bits[2:] if odd else bits[:1] + bits[:0:-1]
 
 
 def offset(n_rows, odd, q):

time: 26.9 us -> 27.2 us (1.011)
  starting transfers between devices: 10.5 us -> 11.8 us
  waiting for transfers between devices: 11.2 us -> 10.5 us
  Pallas kernels: 4.24 us -> 3.92 us
    ppermute x4, starting transfers between devices: 4.81 us -> 5.69 us  [swap(): return lax.ppermute(value, axis, [(i, i ^ bit) for i in range(size)])]
    ppermute x3, waiting for transfers between devices: 7.47 us -> 7 us  [hop(): lax.ppermute(value, 'rows', [(i, i ^ 1 ^ hops(size, parity(i))[b]) for i...]
    ppermute x3, starting transfers between devices: 5.69 us -> 6.12 us  [hop(): lax.ppermute(value, 'rows', [(i, i ^ 1 ^ hops(size, parity(i))[b]) for i...]
    pallas_call x1, Pallas kernels: 2.13 us -> 1.81 us  [rating_part(): pl.pallas_call(functools.partial(rating_kernel, half), name='rating_part'...]
  transfers between devices with their start and end apart: 7 -> 7, of which waited for: 6 -> 6; matrix products, arithmetic and copies ran while one was open for 0% -> 0% of each run, Pallas kernels for 9% -> 7%
where the time goes in v9:
time: 27.2 us; the launch traced here: 27 us
  starting transfers between devices  11.8 us (43%)
  waiting for transfers between devices  10.5 us (39%)
  Pallas kernels  3.92 us (14%)
  between operations  0.74 us (3%)
    ppermute x3, waiting for transfers between devices, hop(): lax.ppermute(value, 'rows', [(i, i ^ 1 ^ hops(size, parity(i))[b]) for i...  7 us
    ppermute x3, starting transfers between devices, hop(): lax.ppermute(value, 'rows', [(i, i ^ 1 ^ hops(size, parity(i))[b]) for i...  6.12 us
    ppermute x4, starting transfers between devices, swap(): return lax.ppermute(value, axis, [(i, i ^ bit) for i in range(size)])  5.69 us
    ppermute x4, waiting for transfers between devices, swap(): return lax.ppermute(value, axis, [(i, i ^ bit) for i in range(size)])  3.55 us
    pallas_call x1, Pallas kernels, rating_part(): pl.pallas_call(functools.partial(rating_kernel, half), name='rating_part'...  1.81 us
    pallas_call x7, Pallas kernels, local_call(): pl.pallas_call(kernel, name=name, out_shape=out_shape, in_specs=[vmem] *...  1.11 us
    pallas_call x1, Pallas kernels, pick_panels(): pl.pallas_call(pick_kernel, name='pick_panels', out_shape=panel, in_specs...  1 us
  transfers between devices with their start and end apart: 7, of which 6 were waited for; matrix products, arithmetic and copies ran while one was open for 0% of the time, Pallas kernels for 7%

profile of v9, /device:TPU:0, one launch (start us, length us, event | category | flops | bytes accessed | tf_op | source)
XLA Modules:
  0.0 27.0 jit_solution(471381456537590484)
XLA Ops:
  0.0 0.0 copy-start
  0.0 0.0 copy-start.1
  0.0 0.0 copy-start.2
  0.0 0.0 copy-start.3
  0.0 1.0 %pick_panels.1 = bf16[128,256]{1,0:T(8,128)(2,1)S(1)} custom-call(s32[2]{0:T(128)} %bitcast.15, bf16[256,256]{1,0:T(8,128)(2,1)} %bitcast.9), custom_call_target="tpu_custom_call" | custom-call | flops 10000000000 | bytes 30000000 | tf_op jit(solution)/shard_map/pick_panels/pallas_call | solution.py:156
  1.0 3.0 %collective-permute-start = (bf16[128,256]{1,0:T(8,128)(2,1)S(1)}, bf16[128,256]{1,0:T(8,128)(2,1)S(1)}, u32[]{:S(2)}, u32[]{:S(2)}) collective-permute-start(bf16[128,256]{1,0:T(8,128)(2,1)S(1)} %pick_panels.1), channel_id=1, source_target_pairs={{0,1},{1,0},{2,3},{3,2},{4,5},{5,4},{6,7},{7,6},{8,9},{9,8},{10,11... | collective-permute-start | bytes 196616 | tf_op jit(solution)/shard_map/ppermute | solution.py:256
  4.7 0.0 copy-done
  4.7 0.0 copy-done.1
  4.7 0.0 copy-done.2
  4.7 0.0 copy-done.3
  4.7 1.8 %rating_part.1 = (f32[128,256]{1,0:T(8,128)S(1)}, bf16[16,256]{1,0:T(8,128)(2,1)S(1)}, bf16[128,128]{1,0:T(8,128)(2,1)S(1)}, bf16[128,128]{1,0:T(8,128)(2,1)S(1)}, f32[128,256]{1,0:T(8,128)S(1)}) custom-call(s32[64]{0:T(128)} %bitcast.12, s32[64]{0:T(128)} %bitcast.13, s32[2]{0:T(128)} %bitcast.14, s32[1,1]{1,0:T(1,128)S(6)} %copy.10.count, s32[2]{0:T(128)} %bitcast.16, ...), custom_call_target="tpu_custom_call" | custom-call | tf_op jit(solution)/shard_map/rating_part/pallas_call | solution.py:114
  6.5 0.0 collective-permute-done.far
  6.6 0.1 graph_give.1
  6.7 0.1 collective-permute-start.1
  6.8 0.1 graph_keep.1.keep
  6.9 1.2 %collective-permute-done.1.received = f32[8,16,256]{2,1,0:T(8,128)S(1)} collective-permute-done((f32[8,16,256]{2,1,0:T(8,128)S(1)}, f32[8,16,256]{2,1,0:T(8,128)S(1)}, u32[]{:S(2)}, u32[]{:S(2)}) %collective-permute-start.1) | collective-permute-done | bytes 131104 | tf_op jit(solution)/shard_map/ppermute | solution.py:256
  8.1 1.6 %collective-permute-start.2 = (bf16[12,16,256]{2,1,0:T(8,128)(2,1)S(1)}, bf16[12,16,256]{2,1,0:T(8,128)(2,1)S(1)}, u32[]{:S(2)}, u32[]{:S(2)}) collective-permute-start(bf16[12,16,256]{2,1,0:T(8,128)(2,1)S(1)} %get-tuple-element.24), channel_id=1, source_target_pairs={{0,6},{2,8},{4,14},{6,0},{8,2},{10,12},{12,10},{14,4},{16,26},{18,... | collective-permute-start | bytes 294920 | tf_op jit(solution)/shard_map/ppermute | solution.py:261
  9.7 2.5 %collective-permute-done.2.received = bf16[12,16,256]{2,1,0:T(8,128)(2,1)S(1)} collective-permute-done((bf16[12,16,256]{2,1,0:T(8,128)(2,1)S(1)}, bf16[12,16,256]{2,1,0:T(8,128)(2,1)S(1)}, u32[]{:S(2)}, u32[]{:S(2)}) %collective-permute-start.2) | collective-permute-done | bytes 98336 | tf_op jit(solution)/shard_map/ppermute | solution.py:261
  12.3 2.7 %collective-permute-start.3 = (bf16[10,16,256]{2,1,0:T(8,128)(2,1)S(1)}, bf16[10,16,256]{2,1,0:T(8,128)(2,1)S(1)}, u32[]{:S(2)}, u32[]{:S(2)}) collective-permute-start(bf16[10,16,256]{2,1,0:T(8,128)(2,1)S(1)} %get-tuple-element.26), channel_id=1, source_target_pairs={{0,18},{2,4},{4,2},{6,20},{8,14},{10,24},{12,30},{14,8},{16,22},{1... | collective-permute-start | bytes 245768 | tf_op jit(solution)/shard_map/ppermute | solution.py:261
  15.0 2.1 %collective-permute-done.3.received = bf16[10,16,256]{2,1,0:T(8,128)(2,1)S(1)} collective-permute-done((bf16[10,16,256]{2,1,0:T(8,128)(2,1)S(1)}, bf16[10,16,256]{2,1,0:T(8,128)(2,1)S(1)}, u32[]{:S(2)}, u32[]{:S(2)}) %collective-permute-start.3) | collective-permute-done | bytes 81952 | tf_op jit(solution)/shard_map/ppermute | solution.py:261
  17.2 1.8 %collective-permute-start.4 = (bf16[9,16,256]{2,1,0:T(8,128)(2,1)S(1)}, bf16[9,16,256]{2,1,0:T(8,128)(2,1)S(1)}, u32[]{:S(2)}, u32[]{:S(2)}) collective-permute-start(bf16[9,16,256]{2,1,0:T(8,128)(2,1)S(1)} %get-tuple-element.28), channel_id=1, source_target_pairs={{0,10},{2,16},{4,22},{6,12},{8,26},{10,0},{12,6},{14,28},{16,2},{1... | collective-permute-start | bytes 221192 | tf_op jit(solution)/shard_map/ppermute | solution.py:261
  19.0 2.4 %collective-permute-done.4.received = bf16[9,16,256]{2,1,0:T(8,128)(2,1)S(1)} collective-permute-done((bf16[9,16,256]{2,1,0:T(8,128)(2,1)S(1)}, bf16[9,16,256]{2,1,0:T(8,128)(2,1)S(1)}, u32[]{:S(2)}, u32[]{:S(2)}) %collective-permute-start.4) | collective-permute-done | bytes 73760 | tf_op jit(solution)/shard_map/ppermute | solution.py:261
  21.4 1.2 %collective-permute-start.5 = (f32[1,128]{1,0:T(1,128)S(1)}, f32[1,128]{1,0:T(1,128)S(1)}, u32[]{:S(2)}, u32[]{:S(2)}) collective-permute-start(f32[1,128]{1,0:T(1,128)S(1)} %get-tuple-element.30), channel_id=1, source_target_pairs={{0,2},{2,0},{4,6},{6,4},{8,10},{10,8},{12,14},{14,12},{16,18},{18,... | collective-permute-start | bytes 1544 | tf_op jit(solution)/shard_map/ppermute | solution.py:256
  22.6 0.8 %collective-permute-done.5 = f32[1,128]{1,0:T(1,128)S(1)} collective-permute-done((f32[1,128]{1,0:T(1,128)S(1)}, f32[1,128]{1,0:T(1,128)S(1)}, u32[]{:S(2)}, u32[]{:S(2)}) %collective-permute-start.5) | collective-permute-done | bytes 544 | tf_op jit(solution)/shard_map/ppermute | solution.py:256
  23.4 1.4 %collective-permute-start.6 = (f32[1,128]{1,0:T(1,128)S(1)}, f32[1,128]{1,0:T(1,128)S(1)}, u32[]{:S(2)}, u32[]{:S(2)}) collective-permute-start(f32[1,128]{1,0:T(1,128)S(1)} %add.3.squares), channel_id=1, source_target_pairs={{0,3},{1,2},{2,1},{3,0},{4,7},{5,6},{6,5},{7,4},{8,11},{9,10},{10,... | collective-permute-start | bytes 1544 | tf_op jit(solution)/shard_map/ppermute | solution.py:256
  24.8 1.5 %collective-permute-done.6.more = f32[1,128]{1,0:T(1,128)S(1)} collective-permute-done((f32[1,128]{1,0:T(1,128)S(1)}, f32[1,128]{1,0:T(1,128)S(1)}, u32[]{:S(2)}, u32[]{:S(2)}) %collective-permute-start.6) | collective-permute-done | bytes 544 | tf_op jit(solution)/shard_map/ppermute | solution.py:256
  26.3 0.7 %update.1 = f32[16,256]{1,0:T(8,128)} custom-call(bf16[16,256]{1,0:T(8,128)(2,1)S(1)} %get-tuple-element.18.mine, f32[16,256]{1,0:T(8,128)S(1)} %get-tuple-element.29.own, f32[1,128]{1,0:T(1,128)S(1)} %add.3.squares, f32[1,128]{1,0:T(1,128)S(1)} %collective-permute-done.6.more), custom_call_target="tpu_custom_call" | custom-call | tf_op jit(solution)/shard_map/update/pallas_call | solution.py:242
  (5 shorter events, 0.1 us)
Async XLA Ops:
  0.0 4.7 %copy-start = (bf16[1,1,64,128,128]{4,3,2,1,0:T(8,128)(2,1)S(1)}, bf16[1,1,64,128,128]{4,3,2,1,0:T(8,128)(2,1)}, u32[]{:S(2)}) copy-start(bf16[1,1,64,128,128]{4,3,2,1,0:T(8,128)(2,1)} %param.11) | copy-start | bytes 6291460
  0.0 4.7 %copy-start.1 = (bf16[2048,256]{1,0:T(8,128)(2,1)S(1)}, bf16[2048,256]{1,0:T(8,128)(2,1)}, u32[]{:S(2)}) copy-start(bf16[2048,256]{1,0:T(8,128)(2,1)} %users.1) | copy-start | bytes 3145732
  0.0 4.7 %copy-start.2 = (bf16[1,256,256]{2,1,0:T(8,128)(2,1)S(1)}, bf16[1,256,256]{2,1,0:T(8,128)(2,1)}, u32[]{:S(2)}) copy-start(bf16[1,256,256]{2,1,0:T(8,128)(2,1)} %param.10) | copy-start | bytes 393220
  0.0 4.7 %copy-start.3 = (bf16[1,1,2,128,128]{4,3,2,1,0:T(8,128)(2,1)S(1)}, bf16[1,1,2,128,128]{4,3,2,1,0:T(8,128)(2,1)}, u32[]{:S(2)}) copy-start(bf16[1,1,2,128,128]{4,3,2,1,0:T(8,128)(2,1)} %param.17) | copy-start | bytes 196612
  1.0 5.5 %collective-permute-start = (bf16[128,256]{1,0:T(8,128)(2,1)S(1)}, bf16[128,256]{1,0:T(8,128)(2,1)S(1)}, u32[]{:S(2)}, u32[]{:S(2)}) collective-permute-start(bf16[128,256]{1,0:T(8,128)(2,1)S(1)} %pick_panels.1), channel_id=1, source_target_pairs={{0,1},{1,0},{2,3},{3,2},{4,5},{5,4},{6,7},{7,6},{8,9},{9,8},{10,11... | collective-permute-start | bytes 196616 | tf_op jit(solution)/shard_map/ppermute | solution.py:256
  6.7 1.4 %collective-permute-start.1 = (f32[8,16,256]{2,1,0:T(8,128)S(1)}, f32[8,16,256]{2,1,0:T(8,128)S(1)}, u32[]{:S(2)}, u32[]{:S(2)}) collective-permute-start(f32[8,16,256]{2,1,0:T(8,128)S(1)} %graph_give.1), channel_id=1, source_target_pairs={{0,2},{2,0},{4,6},{6,4},{8,10},{10,8},{12,14},{14,12},{16,18},{18,... | collective-permute-start | bytes 393224 | tf_op jit(solution)/shard_map/ppermute | solution.py:256
  8.1 4.1 %collective-permute-start.2 = (bf16[12,16,256]{2,1,0:T(8,128)(2,1)S(1)}, bf16[12,16,256]{2,1,0:T(8,128)(2,1)S(1)}, u32[]{:S(2)}, u32[]{:S(2)}) collective-permute-start(bf16[12,16,256]{2,1,0:T(8,128)(2,1)S(1)} %get-tuple-element.24), channel_id=1, source_target_pairs={{0,6},{2,8},{4,14},{6,0},{8,2},{10,12},{12,10},{14,4},{16,26},{18,... | collective-permute-start | bytes 294920 | tf_op jit(solution)/shard_map/ppermute | solution.py:261
  12.3 4.9 %collective-permute-start.3 = (bf16[10,16,256]{2,1,0:T(8,128)(2,1)S(1)}, bf16[10,16,256]{2,1,0:T(8,128)(2,1)S(1)}, u32[]{:S(2)}, u32[]{:S(2)}) collective-permute-start(bf16[10,16,256]{2,1,0:T(8,128)(2,1)S(1)} %get-tuple-element.26), channel_id=1, source_target_pairs={{0,18},{2,4},{4,2},{6,20},{8,14},{10,24},{12,30},{14,8},{16,22},{1... | collective-permute-start | bytes 245768 | tf_op jit(solution)/shard_map/ppermute | solution.py:261
  17.2 4.1 %collective-permute-start.4 = (bf16[9,16,256]{2,1,0:T(8,128)(2,1)S(1)}, bf16[9,16,256]{2,1,0:T(8,128)(2,1)S(1)}, u32[]{:S(2)}, u32[]{:S(2)}) collective-permute-start(bf16[9,16,256]{2,1,0:T(8,128)(2,1)S(1)} %get-tuple-element.28), channel_id=1, source_target_pairs={{0,10},{2,16},{4,22},{6,12},{8,26},{10,0},{12,6},{14,28},{16,2},{1... | collective-permute-start | bytes 221192 | tf_op jit(solution)/shard_map/ppermute | solution.py:261
  21.4 2.0 %collective-permute-start.5 = (f32[1,128]{1,0:T(1,128)S(1)}, f32[1,128]{1,0:T(1,128)S(1)}, u32[]{:S(2)}, u32[]{:S(2)}) collective-permute-start(f32[1,128]{1,0:T(1,128)S(1)} %get-tuple-element.30), channel_id=1, source_target_pairs={{0,2},{2,0},{4,6},{6,4},{8,10},{10,8},{12,14},{14,12},{16,18},{18,... | collective-permute-start | bytes 1544 | tf_op jit(solution)/shard_map/ppermute | solution.py:256
  23.4 3.0 %collective-permute-start.6 = (f32[1,128]{1,0:T(1,128)S(1)}, f32[1,128]{1,0:T(1,128)S(1)}, u32[]{:S(2)}, u32[]{:S(2)}) collective-permute-start(f32[1,128]{1,0:T(1,128)S(1)} %add.3.squares), channel_id=1, source_target_pairs={{0,3},{1,2},{2,1},{3,0},{4,7},{5,6},{6,5},{7,4},{8,11},{9,10},{10,... | collective-permute-start | bytes 1544 | tf_op jit(solution)/shard_map/ppermute | solution.py:256
